TPU v7x, 512 devices: a whole 4x4x16 slice. The times are simulated.
512 devices in a mesh: dp: 8 (over x, core), expert: 64 (over z, y).
Axes of the slice: x: 4, y: 4, z: 16, core: 2. Of those that a mesh axis runs over, the one named last changes fastest.
Arguments:
- tokens: bfloat16 [2560, 3584], P('expert', 'dp'), may hold values from -6 to 6
- cotangent: bfloat16 [2560, 3584], P('expert', 'dp'), may hold values from -1.1953125 to 1.1953125
- expert_ids: int32 [2560, 8], P('expert'), may hold values from 0 to 31, all different within a row; in each aligned block of 40 rows (0 to 39, 40 to 79, ...) at most 20 rows name the same one
- route_weight: bfloat16 [2560, 8], P('expert'), may hold values from 0.099609375 to 1
- gate_weight: bfloat16 [64, 3584, 512], P('expert', 'dp'), may hold values from -0.09375 to 0.09375
- up_weight: bfloat16 [64, 3584, 512], P('expert', 'dp'), may hold values from -0.09375 to 0.09375
- down_weight: bfloat16 [64, 512, 3584], P('expert', None, 'dp'), may hold values from -0.1875 to 0.1875
Outputs:
- token_grad: bfloat16 [2560, 3584], P('expert', 'dp')
- route_grad: bfloat16 [2560, 8], P('expert')
- gate_grad: bfloat16 [64, 3584, 512], P('expert', 'dp')
- up_grad: bfloat16 [64, 3584, 512], P('expert', 'dp')
- down_grad: bfloat16 [64, 512, 3584], P('expert', None, 'dp')
Inputs may be any that keep to these rules, and one draw needn't show every extreme that they name: `expert_ids`: each row names distinct experts. In each aligned block of 40 rows no expert is named by more than 20 rows, a bound that some block reaches.
All inputs are finite; a program needn't handle non-finite values.
Results may differ from a plain program's by a relative error of at most 0.034.
Values may be sent and summed in bfloat16 or wider, within the bound.
No kernel may reach another device: no remote copies, remote signals or barrier semaphores. Data moves between devices by JAX's collectives and lax.ppermute only.
A program may use at most 64 MiB of HBM per device.

v0:
```python
import jax
import jax.numpy as jnp
from jax import lax
from jax.sharding import PartitionSpec as P


def activate(gate_pre, up_pre, hidden_grad, scale):
    sigmoid_g = jax.nn.sigmoid(gate_pre)
    hidden = (gate_pre * sigmoid_g * up_pre).astype(jnp.bfloat16)
    hidden_f = hidden.astype(jnp.float32)
    slot_dots = jnp.sum(hidden_f * hidden_grad, axis=1)
    scaled = (scale * hidden_f).astype(jnp.bfloat16)
    act_grad = scale * hidden_grad
    gate_g = (act_grad * up_pre * sigmoid_g * (1.0 + gate_pre * (1.0 - sigmoid_g))).astype(
        jnp.bfloat16
    )
    up_g = (act_grad * gate_pre * sigmoid_g).astype(jnp.bfloat16)
    return (scaled, gate_g, up_g, slot_dots)


def on_device(tokens, cotangent, expert_ids, route_weight, gate_weight, up_weight, down_weight):
    tok_rows, feat_cols = tokens.shape
    top_count = expert_ids.shape[1]
    devices_e = lax.axis_size("expert")
    experts = devices_e // 2
    capacity = min(tok_rows, 2 * tok_rows * top_count // experts)
    slot_total = tok_rows * top_count
    flat_ids = expert_ids.reshape(slot_total)
    matches = (flat_ids[:, None] == jnp.arange(experts, dtype=jnp.int32)[None, :]).astype(jnp.int32)
    before = jnp.cumsum(matches, axis=0) - matches
    slot_rank = jnp.sum(before * matches, axis=1)
    target = flat_ids * capacity + slot_rank
    picker = target[None, :] == jnp.arange(experts * capacity, dtype=jnp.int32)[:, None]
    owners = jnp.any(picker.reshape(experts * capacity, tok_rows, top_count), axis=2).astype(
        jnp.bfloat16
    )
    bucket_x = jnp.dot(owners, tokens, preferred_element_type=jnp.float32).astype(jnp.bfloat16)
    bucket_dy = jnp.dot(owners, cotangent, preferred_element_type=jnp.float32).astype(jnp.bfloat16)
    flat_w = route_weight.reshape(slot_total).astype(jnp.float32)
    bucket_w = jnp.sum(jnp.where(picker, flat_w[None, :], 0.0), axis=1).astype(jnp.bfloat16)
    recv_x, recv_dy, recv_w = (
        lax.all_to_all(
            jnp.repeat(bucket_x.reshape(experts, capacity, feat_cols), 2, axis=0),
            "expert",
            split_axis=0,
            concat_axis=0,
            tiled=True,
        ),
        lax.all_to_all(
            jnp.repeat(bucket_dy.reshape(experts, capacity, feat_cols), 2, axis=0),
            "expert",
            split_axis=0,
            concat_axis=0,
            tiled=True,
        ),
        lax.all_to_all(
            jnp.repeat(bucket_w.reshape(experts, capacity), 2, axis=0),
            "expert",
            split_axis=0,
            concat_axis=0,
            tiled=True,
        ),
    )
    row_total = devices_e * capacity
    exp_tokens = recv_x.reshape(row_total, feat_cols)
    exp_cotan = recv_dy.reshape(row_total, feat_cols)
    scale = recv_w.reshape(row_total, 1).astype(jnp.float32)
    gate_mat = gate_weight[0]
    up_mat = up_weight[0]
    down_mat = down_weight[0]
    gate_part = jnp.dot(exp_tokens, gate_mat, preferred_element_type=jnp.float32)
    up_part = jnp.dot(exp_tokens, up_mat, preferred_element_type=jnp.float32)
    grad_part = lax.dot_general(
        exp_cotan, down_mat, (((1,), (1,)), ((), ())), preferred_element_type=jnp.float32
    )
    gate_pre, up_pre, hidden_grad = (
        lax.psum(gate_part.astype(jnp.bfloat16), "dp").astype(jnp.float32),
        lax.psum(up_part.astype(jnp.bfloat16), "dp").astype(jnp.float32),
        lax.psum(grad_part.astype(jnp.bfloat16), "dp").astype(jnp.float32),
    )
    scaled, gate_g, up_g, slot_dots = activate(gate_pre, up_pre, hidden_grad, scale)
    down_g = lax.dot_general(
        scaled, exp_cotan, (((0,), (0,)), ((), ())), preferred_element_type=jnp.float32
    ).astype(jnp.bfloat16)
    gate_w = lax.dot_general(
        exp_tokens, gate_g, (((0,), (0,)), ((), ())), preferred_element_type=jnp.float32
    ).astype(jnp.bfloat16)
    up_w = lax.dot_general(
        exp_tokens, up_g, (((0,), (0,)), ((), ())), preferred_element_type=jnp.float32
    ).astype(jnp.bfloat16)
    token_back = lax.dot_general(
        gate_g, gate_mat, (((1,), (1,)), ((), ())), preferred_element_type=jnp.float32
    )
    token_back = token_back + lax.dot_general(
        up_g, up_mat, (((1,), (1,)), ((), ())), preferred_element_type=jnp.float32
    )
    ret_back, ret_dots = (
        lax.all_to_all(
            token_back.reshape(devices_e, capacity, feat_cols).astype(jnp.bfloat16),
            "expert",
            split_axis=0,
            concat_axis=0,
            tiled=True,
        ).astype(jnp.float32),
        lax.all_to_all(
            slot_dots.reshape(devices_e, capacity).astype(jnp.bfloat16),
            "expert",
            split_axis=0,
            concat_axis=0,
            tiled=True,
        ).astype(jnp.float32),
    )
    slot_back = (
        jnp.sum(ret_back.reshape(experts, 2, capacity, feat_cols), axis=1)
        .astype(jnp.bfloat16)
        .reshape(experts * capacity, feat_cols)
    )
    slot_route = (
        jnp.sum(ret_dots.reshape(experts, 2, capacity), axis=1)
        .astype(jnp.bfloat16)
        .reshape(experts * capacity)
    )
    token_grad = lax.dot_general(
        owners, slot_back, (((0,), (0,)), ((), ())), preferred_element_type=jnp.float32
    ).astype(jnp.bfloat16)
    route_flat = jnp.sum(jnp.where(picker, slot_route.astype(jnp.float32)[:, None], 0.0), axis=0)
    route_grad = route_flat.reshape(tok_rows, top_count).astype(jnp.bfloat16)
    return (token_grad, route_grad, gate_w[None], up_w[None], down_g[None])


def solution(mesh):
    placed = (
        P("expert", "dp"),
        P("expert", "dp"),
        P("expert", None),
        P("expert", None),
        P("expert", "dp", None),
        P("expert", "dp", None),
        P("expert", None, "dp"),
    )
    return jax.shard_map(
        on_device,
        mesh=mesh,
        in_specs=placed,
        out_specs=(
            P("expert", "dp"),
            P("expert", None),
            P("expert", "dp", None),
            P("expert", "dp", None),
            P("expert", None, "dp"),
        ),
        check_vma=False,
    )
```

profile of v0, /device:TPU:6, one launch (start us, length us, event | category | flops | bytes accessed | tf_op | source)
XLA Modules:
  0.0 429.5 jit_solution(8754383653708937528)
XLA Ops:
  11.4 1.3 broadcast_in_dim.49
  12.7 18.9 %all-to-all-start.2 = ((bf16[64,20,448]{2,1,0:T(8,128)(2,1)}), bf16[64,20,448]{2,1,0:T(8,128)(2,1)S(1)}, u32[]{:S(2)}, u32[]{:S(2)}) async-start(bf16[64,20,448]{2,1,0:T(8,128)(2,1)} %bitcast.4), calls=%async_computation.2 | async-start | bytes 3145728 | tf_op jit(solution)/shard_map/all_to_all | solution.py:42
  32.4 77.0 %all-to-all-done.2 = bf16[64,20,448]{2,1,0:T(8,128)(2,1)S(1)} async-done(((bf16[64,20,448]{2,1,0:T(8,128)(2,1)}), bf16[64,20,448]{2,1,0:T(8,128)(2,1)S(1)}, u32[]{:S(2)}, u32[]{:S(2)}) %all-to-all-start.2) | async-done | bytes 1146912 | tf_op jit(solution)/shard_map/all_to_all | solution.py:42
  109.3 1.3 broadcast_in_dim.48
  110.6 6.1 %all-to-all-start.1 = ((bf16[64,20,448]{2,1,0:T(8,128)(2,1)}), bf16[64,20,448]{2,1,0:T(8,128)(2,1)}, u32[]{:S(2)}, u32[]{:S(2)}) async-start(bf16[64,20,448]{2,1,0:T(8,128)(2,1)} %bitcast.2), calls=%async_computation.1 | async-start | bytes 3145728 | tf_op jit(solution)/shard_map/all_to_all | solution.py:49
  117.4 1.9 convolution_convert_fusion
  119.3 1.9 convolution_convert_fusion.1
  121.3 72.5 %all-to-all-done.1 = bf16[64,20,448]{2,1,0:T(8,128)(2,1)} async-done(((bf16[64,20,448]{2,1,0:T(8,128)(2,1)}), bf16[64,20,448]{2,1,0:T(8,128)(2,1)}, u32[]{:S(2)}, u32[]{:S(2)}) %all-to-all-start.1) | async-done | bytes 1146912 | tf_op jit(solution)/shard_map/all_to_all | solution.py:49
  193.7 2.5 reshape.131
  196.3 1.9 convolution_convert_fusion.2
  198.2 76.3 %all-reduce.4.cloned.1.call-done = (bf16[1280,512]{1,0:T(8,128)(2,1)}, bf16[1280,512]{1,0:T(8,128)(2,1)}, bf16[1280,512]{1,0:T(8,128)(2,1)}) async-done(((bf16[1280,512]{1,0:T(8,128)(2,1)}, bf16[1280,512]{1,0:T(8,128)(2,1)}, bf16[1280,512]{1,0:T(8,128)(2,1)}), (bf16[1280,512]{1,0:T(8,128)(2,1)}, bf16[1280,512]{1,0:T(8,128)(2,1)}, bf16[1280,512]{1,0:T(8,128)(2,1)})) %all-reduce.4.cloned.1.call-update) | async-done | bytes 3932176 | tf_op jit(solution)/shard_map/psum | solution.py:79
  274.5 4.3 fusion.5
  279.5 15.6 %all-to-all-start.4 = ((bf16[64,1,20]{2,1,0:T(2,128)(2,1)}), bf16[64,1,20]{2,1,0:T(2,128)(2,1)S(1)}, u32[]{:S(2)}, u32[]{:S(2)}) async-start(bf16[64,1,20]{2,1,0:T(2,128)(2,1)} %convert_element_type.187), calls=%async_computation.4 | async-start | bytes 65536 | tf_op jit(solution)/shard_map/all_to_all | solution.py:105
  295.3 14.3 %all-to-all-done.4 = bf16[64,1,20]{2,1,0:T(2,128)(2,1)S(1)} async-done(((bf16[64,1,20]{2,1,0:T(2,128)(2,1)}), bf16[64,1,20]{2,1,0:T(2,128)(2,1)S(1)}, u32[]{:S(2)}, u32[]{:S(2)}) %all-to-all-start.4) | async-done | bytes 2592 | tf_op jit(solution)/shard_map/all_to_all | solution.py:105
  310.4 18.8 %all_to_all.30 = bf16[64,1,20]{2,1,0:T(2,128)(2,1)S(1)} all-to-all(bf16[64,1,20]{2,1,0:T(2,128)(2,1)S(1)} %copy.50), channel_id=1, replica_groups=mesh['dp'=8,'expert'=64] {'expert'}, dimensions={0} | all-to-all | bytes 5120 | tf_op jit(solution)/shard_map/all_to_all | solution.py:56
  329.4 3.1 fusion.12
  333.9 1.8 fusion
  335.7 1.6 copy.53
  337.2 1.4 convert_element_type.165
  338.6 4.7 %all-to-all-start.3 = ((bf16[64,20,448]{2,1,0:T(8,128)(2,1)}), bf16[64,20,448]{2,1,0:T(8,128)(2,1)S(1)}, u32[]{:S(2)}, u32[]{:S(2)}) async-start(bf16[64,20,448]{2,1,0:T(8,128)(2,1)} %convert_element_type.165), calls=%async_computation.3 | async-start | bytes 3145728 | tf_op jit(solution)/shard_map/all_to_all | solution.py:98
  344.0 3.4 fusion.20
  347.4 1.6 fusion.19
  349.1 1.7 fusion.21
  350.8 70.4 %all-to-all-done.3 = bf16[64,20,448]{2,1,0:T(8,128)(2,1)S(1)} async-done(((bf16[64,20,448]{2,1,0:T(8,128)(2,1)}), bf16[64,20,448]{2,1,0:T(8,128)(2,1)S(1)}, u32[]{:S(2)}, u32[]{:S(2)}) %all-to-all-start.3) | async-done | bytes 1146912 | tf_op jit(solution)/shard_map/all_to_all | solution.py:98
  (66 shorter events, 11.1 us)
Async XLA Ops:
  7.2 110.2 %copy-start = (bf16[1,448,512]{2,1,0:T(8,128)(2,1)S(1)}, bf16[1,448,512]{2,1,0:T(8,128)(2,1)}, u32[]{:S(2)}) copy-start(bf16[1,448,512]{2,1,0:T(8,128)(2,1)} %param.11) | copy-start | bytes 1376260
  12.7 18.9 %copy-start.10 = (bf16[40,448]{1,0:T(8,128)(2,1)S(1)}, bf16[40,448]{1,0:T(8,128)(2,1)}, u32[]{:S(2)}) copy-start(bf16[40,448]{1,0:T(8,128)(2,1)} %param.8) | copy-start | bytes 107524
  12.7 96.6 %all-to-all-start.2 = ((bf16[64,20,448]{2,1,0:T(8,128)(2,1)}), bf16[64,20,448]{2,1,0:T(8,128)(2,1)S(1)}, u32[]{:S(2)}, u32[]{:S(2)}) async-start(bf16[64,20,448]{2,1,0:T(8,128)(2,1)} %bitcast.4), calls=%async_computation.2 | async-start | bytes 3145728 | tf_op jit(solution)/shard_map/all_to_all | solution.py:42
  110.6 83.2 %all-to-all-start.1 = ((bf16[64,20,448]{2,1,0:T(8,128)(2,1)}), bf16[64,20,448]{2,1,0:T(8,128)(2,1)}, u32[]{:S(2)}, u32[]{:S(2)}) async-start(bf16[64,20,448]{2,1,0:T(8,128)(2,1)} %bitcast.2), calls=%async_computation.1 | async-start | bytes 3145728 | tf_op jit(solution)/shard_map/all_to_all | solution.py:49
  116.7 157.8 %all-reduce.4.cloned.1.call-start = ((), (), s32[]{:S(2)}) async-start(), calls=%async_computation.5 | async-start | bytes 7864320 | tf_op jit(solution)/shard_map/psum | solution.py:79
  117.4 2.0 copy-start.3
  117.4 2.0 copy-start.8
  121.3 75.0 %copy-start.12 = (bf16[1,512,448]{1,2,0:T(8,128)(2,1)S(1)}, bf16[1,512,448]{1,2,0:T(8,128)(2,1)}, u32[]{:S(2)}) copy-start(bf16[1,512,448]{1,2,0:T(8,128)(2,1)} %param.13) | copy-start | bytes 1376260
  196.3 1.9 copy-start.5
  274.5 20.7 %copy-start.11 = (bf16[40,8]{0,1:T(8,128)(2,1)S(1)}, bf16[40,8]{0,1:T(8,128)(2,1)}, u32[]{:S(2)}) copy-start(bf16[40,8]{0,1:T(8,128)(2,1)} %param.10) | copy-start | bytes 1924
  274.5 54.9 %copy-start.2 = (bf16[1280,512]{1,0:T(8,128)(2,1)S(1)}, bf16[1280,512]{1,0:T(8,128)(2,1)}, u32[]{:S(2)}) copy-start(bf16[1280,512]{1,0:T(8,128)(2,1)} %get-tuple-element.27) | copy-start | bytes 3932164
  279.5 30.2 %all-to-all-start.4 = ((bf16[64,1,20]{2,1,0:T(2,128)(2,1)}), bf16[64,1,20]{2,1,0:T(2,128)(2,1)S(1)}, u32[]{:S(2)}, u32[]{:S(2)}) async-start(bf16[64,1,20]{2,1,0:T(2,128)(2,1)} %convert_element_type.187), calls=%async_computation.4 | async-start | bytes 65536 | tf_op jit(solution)/shard_map/all_to_all | solution.py:105
  332.5 1.1 copy-start.1
  332.5 1.4 copy-start.9
  338.6 82.6 %all-to-all-start.3 = ((bf16[64,20,448]{2,1,0:T(8,128)(2,1)}), bf16[64,20,448]{2,1,0:T(8,128)(2,1)S(1)}, u32[]{:S(2)}, u32[]{:S(2)}) async-start(bf16[64,20,448]{2,1,0:T(8,128)(2,1)} %convert_element_type.165), calls=%async_computation.3 | async-start | bytes 3145728 | tf_op jit(solution)/shard_map/all_to_all | solution.py:98
  344.0 3.4 copy-start.4
  347.4 1.6 copy-start.6
  347.4 1.7 copy-start.7
Sparse Core Ops, SparseCore 0:
  198.3 76.1 all-reduce.3
where the time goes:
time: 430 us; the launch traced here: 429 us
  waiting for transfers between devices  310 us (72%)
  starting transfers between devices  45.3 us (11%)
  blocking collectives  18.8 us (4%)
  matrix products  17.3 us (4%)
  between operations  14.3 us (3%)
  local copies, waits for them, and re-layouts  13.8 us (3%)
  other arithmetic  9.52 us (2%)
    all_to_all x1, waiting for transfers between devices, on_device(): lax.all_to_all(jnp.repeat(bucket_x.reshape(experts, capacity, feat_cols),...  77 us
    psum x1, waiting for transfers between devices, on_device(): lax.psum(grad_part.astype(jnp.bfloat16), 'dp').astype(jnp.float32)  76.3 us
    all_to_all x1, waiting for transfers between devices, on_device(): lax.all_to_all(jnp.repeat(bucket_dy.reshape(experts, capacity, feat_cols)...  72.5 us
    all_to_all x1, waiting for transfers between devices, on_device(): lax.all_to_all(token_back.reshape(devices_e, capacity, feat_cols).astype(...  70.4 us
    all_to_all x1, starting transfers between devices, on_device(): lax.all_to_all(jnp.repeat(bucket_x.reshape(experts, capacity, feat_cols),...  18.9 us
    all_to_all x1, blocking collectives, on_device(): lax.all_to_all(jnp.repeat(bucket_w.reshape(experts, capacity), 2, axis=0)...  18.8 us
    all_to_all x1, starting transfers between devices, on_device(): lax.all_to_all(slot_dots.reshape(devices_e, capacity).astype(jnp.bfloat16...  15.6 us
    all_to_all x1, waiting for transfers between devices, on_device(): lax.all_to_all(slot_dots.reshape(devices_e, capacity).astype(jnp.bfloat16...  14.3 us
  transfers between devices with their start and end apart: 5, of which 5 were waited for; matrix products, arithmetic and copies ran while one was open for 3% of the time, Pallas kernels for 0%

commit v1 on v0

v1 whole, which is shorter than its diff:
```python
import jax
import jax.numpy as jnp
from jax import lax
from jax.sharding import Mesh, PartitionSpec as P

BF = jnp.bfloat16
F32 = jnp.float32
FEAT = 448
WIDE = 512
CAP = 20


def dot(a, b, dims):
    return lax.dot_general(a, b, (dims, ((), ())), preferred_element_type=F32)


def take(a, axis, step):
    n = lax.axis_size(axis)
    return lax.ppermute(a, axis, [((i + step) % n, i) for i in range(n)])


def gather_z(a):
    rows = a.shape[0]
    far = jnp.concatenate([take(a, "z", 4), a, take(a, "z", -4), take(a, "z", 8)], 0)
    return jnp.concatenate(
        [
            far,
            take(far, "z", 1),
            take(far, "z", -1),
            take(far[: 2 * rows], "z", 2),
            take(far[rows : 3 * rows], "z", -2),
        ],
        0,
    )


def reduce_z(d, rows):
    f = lambda a: a.astype(F32)
    one = take(d[4 * rows : 8 * rows], "z", -1)
    back_one = take(d[8 * rows : 12 * rows], "z", 1)
    two = take(d[12 * rows : 14 * rows], "z", -2)
    back_two = take(d[14 * rows : 16 * rows], "z", 2)
    zero = jnp.zeros((rows, d.shape[1]), F32)
    s = f(d[: 4 * rows]) + f(one) + f(back_one)
    s = s + jnp.concatenate([f(two), zero, zero], 0)
    s = s + jnp.concatenate([zero, f(back_two), zero], 0)
    s = s.astype(BF)
    return (
        f(s[rows : 2 * rows])
        + f(take(s[:rows], "z", -4))
        + f(take(s[2 * rows : 3 * rows], "z", 4))
        + f(take(s[3 * rows :], "z", 8))
    )


def swap_core(a):
    return lax.ppermute(a, "core", [(0, 1), (1, 0)])


def trade(a, axis):
    return lax.all_to_all(a, axis, split_axis=0, concat_axis=0, tiled=True)


def on_device(tokens, cotangent, expert_ids, route_weight, gate_weight, up_weight, down_weight):
    rows = tokens.shape[0]
    core = lax.axis_index("core")
    xpos = lax.axis_index("x")
    z = lax.axis_index("z")
    experts = 32
    match = (expert_ids[:, :, None] == jnp.arange(experts, dtype=jnp.int32)).astype(F32)
    named = jnp.sum(match, axis=1)
    below = (jnp.arange(rows)[:, None] > jnp.arange(rows)[None, :]).astype(F32)
    rank = jnp.sum(match * dot(below, named, ((1,), (0,)))[:, None, :], axis=2)
    payload_x = jnp.concatenate(
        [tokens, expert_ids.astype(BF), rank.astype(BF), route_weight, jnp.zeros((rows, 40), BF)], 1
    )
    all_x = gather_z(payload_x)
    all_dy = gather_z(cotangent)
    total = all_x.shape[0]
    ids = all_x[:, FEAT : FEAT + 8]
    ranks = all_x[:, FEAT + 8 : FEAT + 16].astype(F32)
    weights = all_x[:, FEAT + 16 : FEAT + 24].astype(F32)
    half_rows = total // 2 // 2
    blocks = jnp.arange(total, dtype=jnp.int32) // rows

    def choose(which):
        hit = ids == (2 * z + which).astype(BF)
        live = jnp.any(hit, axis=1)
        place = jnp.sum(jnp.where(hit, ranks, 0.0), axis=1).astype(jnp.int32)
        place = (blocks * CAP + place + core * half_rows) % (2 * half_rows)
        place = jnp.where(live, place, -1)
        scale = jnp.sum(jnp.where(hit, weights, 0.0), axis=1)
        one_hot = (place[:, None] == jnp.arange(2 * half_rows, dtype=jnp.int32)).astype(BF)
        return hit, one_hot, scale.astype(BF)

    hit_a, pick_a, scale_a = choose(0)
    hit_b, pick_b, scale_b = choose(1)
    with_a = jnp.concatenate([all_x[:, :FEAT], scale_a[:, None], jnp.zeros((total, 63), BF)], 1)
    with_b = jnp.concatenate([all_x[:, :FEAT], scale_b[:, None], jnp.zeros((total, 63), BF)], 1)
    rows_dim = ((0,), (0,))
    x_a = dot(pick_a, with_a, rows_dim).astype(BF)
    x_b = dot(pick_b, with_b, rows_dim).astype(BF)
    got_x = trade(jnp.stack([x_a, x_a, x_b, x_b]), "y")
    dy_a = dot(pick_a, all_dy, rows_dim).astype(BF)
    dy_b = dot(pick_b, all_dy, rows_dim).astype(BF)
    got_dy = trade(jnp.stack([dy_a, dy_a, dy_b, dy_b]), "y")
    half = 4 * half_rows
    own_x = got_x[:, :half_rows].reshape(half, WIDE)
    oth_x = got_x[:, half_rows:].reshape(half, WIDE)
    own_dy = got_dy[:, :half_rows].reshape(half, FEAT)
    oth_dy = got_dy[:, half_rows:].reshape(half, FEAT)
    gate_mat, up_mat, down_mat = gate_weight[0], up_weight[0], down_weight[0]
    last_first = ((1,), (0,))
    last_last = ((1,), (1,))

    def reduce_dp(mine, others):
        pair = (mine + swap_core(others.astype(BF)).astype(F32)).astype(BF)
        pieces = trade(pair.reshape(4, half // 4, pair.shape[1]), "x")
        return jnp.sum(pieces.astype(F32), axis=0)

    gate_up = jnp.concatenate([gate_mat, up_mat], 1)
    gu = reduce_dp(
        dot(own_x[:, :FEAT], gate_up, last_first), dot(oth_x[:, :FEAT], gate_up, last_first)
    )
    hidden_grad = reduce_dp(
        dot(own_dy, down_mat, last_last), dot(oth_dy, down_mat, last_last)
    )
    hid = gate_mat.shape[1]
    gate_pre, up_pre = gu[:, :hid], gu[:, hid:]
    quarter = half // 4
    scale = lax.dynamic_slice_in_dim(own_x[:, FEAT : FEAT + 1], xpos * quarter, quarter, 0).astype(
        F32
    )
    sig = jax.nn.sigmoid(gate_pre)
    hidden = (gate_pre * sig * up_pre).astype(BF)
    hidden_f = hidden.astype(F32)
    dots = jnp.sum(hidden_f * hidden_grad, axis=1, keepdims=True).astype(BF)
    scaled = (scale * hidden_f).astype(BF)
    act_grad = scale * hidden_grad
    gate_g = (act_grad * up_pre * sig * (1.0 + gate_pre * (1.0 - sig))).astype(BF)
    up_g = (act_grad * gate_pre * sig).astype(BF)

    def spread_dp(a):
        mine = trade(jnp.broadcast_to(a[None], (4,) + a.shape), "x").reshape(half, a.shape[1])
        return mine, swap_core(mine)

    own_g, oth_g = spread_dp(
        jnp.concatenate([gate_g, up_g, jnp.pad(dots, ((0, 0), (0, 127)))], 1)
    )
    own_s, oth_s = spread_dp(scaled)

    def back(g):
        t = dot(g[:, :hid], gate_mat, last_last) + dot(g[:, hid : 2 * hid], up_mat, last_last)
        t = jnp.concatenate([t.astype(BF), g[:, 2 * hid : 2 * hid + 64]], 1)
        return t.reshape(4, half_rows, WIDE)

    ret = trade(jnp.concatenate([back(own_g), back(oth_g)], 1), "y").astype(F32)
    slot_a = (ret[0] + ret[1]).astype(BF)
    slot_b = (ret[2] + ret[3]).astype(BF)
    sum_a = dot(pick_a, slot_a, last_first)
    sum_b = dot(pick_b, slot_b, last_first)
    route = jnp.where(hit_a, sum_a[:, FEAT : FEAT + 1], 0.0) + jnp.where(
        hit_b, sum_b[:, FEAT : FEAT + 1], 0.0
    )
    dense = jnp.concatenate(
        [(sum_a + sum_b)[:, :FEAT].astype(BF), route.astype(BF), jnp.zeros((total, 56), BF)], 1
    )
    final = reduce_z(dense, rows).astype(BF)

    def wgrad(own_l, oth_l, own_r, oth_r):
        return (dot(own_l, own_r, rows_dim) + dot(oth_l, oth_r, rows_dim)).astype(BF)

    down_g = wgrad(own_s, oth_s, own_dy, oth_dy)
    gate_w = wgrad(own_x[:, :FEAT], oth_x[:, :FEAT], own_g[:, :hid], oth_g[:, :hid])
    up_w = wgrad(
        own_x[:, :FEAT], oth_x[:, :FEAT], own_g[:, hid : 2 * hid], oth_g[:, hid : 2 * hid]
    )
    return (final[:, :FEAT], final[:, FEAT : FEAT + 8], gate_w[None], up_w[None], down_g[None])


def solution(mesh):
    fine = Mesh(mesh.devices.reshape(4, 2, 16, 4), ("x", "core", "z", "y"))
    dp, expert = ("x", "core"), ("z", "y")
    return jax.shard_map(
        on_device,
        mesh=fine,
        in_specs=(
            P(expert, dp),
            P(expert, dp),
            P(expert, None),
            P(expert, None),
            P(expert, dp, None),
            P(expert, dp, None),
            P(expert, None, dp),
        ),
        out_specs=(
            P(expert, dp),
            P(expert, None),
            P(expert, dp, None),
            P(expert, dp, None),
            P(expert, None, dp),
        ),
        check_vma=False,
    )
```

time: 430 us -> 313 us (0.73); the launches traced: 429 us -> 307 us
  waiting for transfers between devices: 310 us -> 81.8 us
  starting transfers between devices: 45.3 us -> 141 us
  between operations: 14.3 us -> 1.46 us
  matrix products: 17.3 us -> 26.8 us
  local copies, waits for them, and re-layouts: 13.8 us -> 19.7 us
  other arithmetic: 9.52 us -> 15.4 us
    all_to_all x4 -> x6, waiting for transfers between devices: 234 us -> 53.8 us  [trade(): return lax.all_to_all(a, axis, split_axis=0, concat_axis=0, tiled=True)]
    ppermute x0 -> x25, starting transfers between devices: none -> 112 us  [the longest x21 103 us: take(): return lax.ppermute(a, axis, [((i + step) % n, i) for i in range(n)])]
    psum x1 -> x0, waiting for transfers between devices: 76.3 us -> none  [on_device(): lax.psum(grad_part.astype(jnp.bfloat16), 'dp').astype(jnp.float32)]
    ppermute x0 -> x25, waiting for transfers between devices: none -> 28 us  [the longest x21 26.3 us: take(): return lax.ppermute(a, axis, [((i + step) % n, i) for i in range(n)])]
    all_to_all x4 -> x6, starting transfers between devices: 45.2 us -> 28.9 us  [trade(): return lax.all_to_all(a, axis, split_axis=0, concat_axis=0, tiled=True)]
    dot_general x11 -> x21, matrix products: 17.3 us -> 26.8 us  [dot(): return lax.dot_general(a, b, (dims, ((), ())), preferred_element_type=F32)]
    slice x1 -> x13, local copies, waits for them, and re-layouts: 0.22 us -> 6.29 us  [the longest x2 1.9 us: back(): t = jnp.concatenate([t.astype(BF), g[:, 2 * hid:2 * hid + 64]], 1)]
    concatenate x0 -> x8, other arithmetic: none -> 5.86 us  [the longest x1 2.45 us: on_device(): ret = trade(jnp.concatenate([back(own_g), back(oth_g)], 1), 'y').astype(F32)]
  transfers between devices with their start and end apart: 5 -> 31, of which waited for: 5 -> 14; matrix products, arithmetic and copies ran while one was open for 3% -> 15% of each run, Pallas kernels for 0% -> 0%
where the time goes in v1:
time: 313 us; the launch traced here: 307 us
  starting transfers between devices  141 us (45%)
  waiting for transfers between devices  81.8 us (26%)
  matrix products  26.8 us (9%)
  blocking collectives  20.8 us (7%)
  local copies, waits for them, and re-layouts  19.7 us (6%)
  other arithmetic  15.4 us (5%)
    ppermute x21, starting transfers between devices, take(): return lax.ppermute(a, axis, [((i + step) % n, i) for i in range(n)])  103 us
    all_to_all x6, waiting for transfers between devices, trade(): return lax.all_to_all(a, axis, split_axis=0, concat_axis=0, tiled=True)  53.8 us
    all_to_all x6, starting transfers between devices, trade(): return lax.all_to_all(a, axis, split_axis=0, concat_axis=0, tiled=True)  28.9 us
    dot_general x21, matrix products, dot(): return lax.dot_general(a, b, (dims, ((), ())), preferred_element_type=F32)  26.8 us
    ppermute x21, waiting for transfers between devices, take(): return lax.ppermute(a, axis, [((i + step) % n, i) for i in range(n)])  26.3 us
    all_to_all x1, blocking collectives, trade(): return lax.all_to_all(a, axis, split_axis=0, concat_axis=0, tiled=True)  20.8 us
    ppermute x4, starting transfers between devices, swap_core(): return lax.ppermute(a, 'core', [(0, 1), (1, 0)])  8.78 us
  transfers between devices with their start and end apart: 31, of which 14 were waited for; matrix products, arithmetic and copies ran while one was open for 15% of the time, Pallas kernels for 0%

profile of v1, /device:TPU:6, one launch (start us, length us, event | category | flops | bytes accessed | tf_op | source)
XLA Modules:
  0.0 306.8 jit_solution(11327469450922051738)
XLA Ops:
  0.6 15.9 %collective-permute-start.9 = (bf16[40,448]{1,0:T(8,128)(2,1)}, bf16[40,448]{1,0:T(8,128)(2,1)S(1)}, u32[]{:S(2)}, u32[]{:S(2)}) collective-permute-start(bf16[40,448]{1,0:T(8,128)(2,1)} %param.8), channel_id=1, source_target_pairs={{32,0},{36,4},{40,8},{44,12},{48,16},{52,20},{56,24},{60,28},{0,32... | collective-permute-start | bytes 107528 | tf_op jit(solution)/shard_map/ppermute | solution.py:19
  20.8 5.5 %collective-permute-start.7 = (bf16[40,448]{1,0:T(8,128)(2,1)}, bf16[40,448]{1,0:T(8,128)(2,1)S(1)}, u32[]{:S(2)}, u32[]{:S(2)}) collective-permute-start(bf16[40,448]{1,0:T(8,128)(2,1)} %param.8), channel_id=1, source_target_pairs={{16,0},{20,4},{24,8},{28,12},{32,16},{36,20},{40,24},{44,28},{48,3... | collective-permute-start | bytes 107528 | tf_op jit(solution)/shard_map/ppermute | solution.py:19
  33.9 5.5 %collective-permute-start.1 = (bf16[40,512]{0,1:T(8,128)(2,1)S(1)}, bf16[40,512]{0,1:T(8,128)(2,1)S(1)}, u32[]{:S(2)}, u32[]{:S(2)}) collective-permute-start(bf16[40,512]{0,1:T(8,128)(2,1)S(1)} %constant_dynamic-update-slice_fusion), channel_id=1, source_target_pairs={{48,0},{52,4},{56,8},{60,12},{0,16},{4,20},{8,24},{12,28},{16,32},... | collective-permute-start | bytes 122888 | tf_op jit(solution)/shard_map/ppermute | solution.py:19
  47.5 5.5 %collective-permute-start.10 = (bf16[160,448]{1,0:T(8,128)(2,1)S(1)}, bf16[160,448]{1,0:T(8,128)(2,1)S(1)}, u32[]{:S(2)}, u32[]{:S(2)}) collective-permute-start(bf16[160,448]{1,0:T(8,128)(2,1)S(1)} %get-tuple-element.55), channel_id=1, source_target_pairs={{4,0},{8,4},{12,8},{16,12},{20,16},{24,20},{28,24},{32,28},{36,32}... | collective-permute-start | bytes 430088 | tf_op jit(solution)/shard_map/ppermute | solution.py:19
  53.9 4.4 %collective-permute-start.13 = (bf16[80,448]{1,0:T(8,128)(2,1)S(1)}, bf16[80,448]{1,0:T(8,128)(2,1)S(1)}, u32[]{:S(2)}, u32[]{:S(2)}) collective-permute-start(bf16[80,448]{1,0:T(8,128)(2,1)S(1)} %get-tuple-element.53), channel_id=1, source_target_pairs={{56,0},{60,4},{0,8},{4,12},{8,16},{12,20},{16,24},{20,28},{24,32},... | collective-permute-start | bytes 215048 | tf_op jit(solution)/shard_map/ppermute | solution.py:19
  58.3 5.4 %collective-permute-done.1 = bf16[40,512]{0,1:T(8,128)(2,1)S(1)} collective-permute-done((bf16[40,512]{0,1:T(8,128)(2,1)S(1)}, bf16[40,512]{0,1:T(8,128)(2,1)S(1)}, u32[]{:S(2)}, u32[]{:S(2)}) %collective-permute-start.1) | collective-permute-done | bytes 40992 | tf_op jit(solution)/shard_map/ppermute | solution.py:19
  76.9 5.3 %collective-permute-start.5 = (bf16[80,512]{0,1:T(8,128)(2,1)S(1)}, bf16[80,512]{0,1:T(8,128)(2,1)S(1)}, u32[]{:S(2)}, u32[]{:S(2)}) collective-permute-start(bf16[80,512]{0,1:T(8,128)(2,1)S(1)} %get-tuple-element.52), channel_id=1, source_target_pairs={{8,0},{12,4},{16,8},{20,12},{24,16},{28,20},{32,24},{36,28},{40,32... | collective-permute-start | bytes 245768 | tf_op jit(solution)/shard_map/ppermute | solution.py:19
  89.6 4.5 %all-to-all-start.1 = ((bf16[4,320,448]{2,1,0:T(8,128)(2,1)}), bf16[4,320,448]{2,1,0:T(8,128)(2,1)S(1)}, u32[]{:S(2)}, u32[]{:S(2)}) async-start(bf16[4,320,448]{2,1,0:T(8,128)(2,1)} %pad_maximum_fusion.1), calls=%async_computation.1 | async-start | bytes 2621440 | tf_op jit(solution)/shard_map/all_to_all | solution.py:61
  96.9 11.9 %all-to-all-done.1 = bf16[4,320,448]{2,1,0:T(8,128)(2,1)S(1)} async-done(((bf16[4,320,448]{2,1,0:T(8,128)(2,1)}), bf16[4,320,448]{2,1,0:T(8,128)(2,1)S(1)}, u32[]{:S(2)}, u32[]{:S(2)}) %all-to-all-start.1) | async-done | bytes 1146912 | tf_op jit(solution)/shard_map/all_to_all | solution.py:61
  113.7 12.3 %all-to-all-done = bf16[4,320,512]{2,1,0:T(8,128)(2,1)S(1)} async-done(((bf16[4,320,512]{2,1,0:T(8,128)(2,1)}), bf16[4,320,512]{2,1,0:T(8,128)(2,1)S(1)}, u32[]{:S(2)}, u32[]{:S(2)}) %all-to-all-start) | async-done | bytes 1310752 | tf_op jit(solution)/shard_map/all_to_all | solution.py:61
  137.1 4.8 %all-to-all-start.2 = ((bf16[4,160,512]{2,1,0:T(8,128)(2,1)}), bf16[4,160,512]{2,1,0:T(8,128)(2,1)S(1)}, u32[]{:S(2)}, u32[]{:S(2)}) async-start(bf16[4,160,512]{2,1,0:T(8,128)(2,1)} %bitcast.80), calls=%async_computation.2 | async-start | bytes 1310720 | tf_op jit(solution)/shard_map/all_to_all | solution.py:61
  145.3 5.9 %all-to-all-done.2 = bf16[4,160,512]{2,1,0:T(8,128)(2,1)S(1)} async-done(((bf16[4,160,512]{2,1,0:T(8,128)(2,1)}), bf16[4,160,512]{2,1,0:T(8,128)(2,1)S(1)}, u32[]{:S(2)}, u32[]{:S(2)}) %all-to-all-start.2) | async-done | bytes 655392 | tf_op jit(solution)/shard_map/all_to_all | solution.py:61
  152.0 5.6 %all-to-all-start.3 = ((bf16[4,160,1024]{2,1,0:T(8,128)(2,1)}), bf16[4,160,1024]{2,1,0:T(8,128)(2,1)S(1)}, u32[]{:S(2)}, u32[]{:S(2)}) async-start(bf16[4,160,1024]{2,1,0:T(8,128)(2,1)} %bitcast.74), calls=%async_computation.3 | async-start | bytes 2621440 | tf_op jit(solution)/shard_map/all_to_all | solution.py:61
  160.0 13.2 %all-to-all-done.3 = bf16[4,160,1024]{2,1,0:T(8,128)(2,1)S(1)} async-done(((bf16[4,160,1024]{2,1,0:T(8,128)(2,1)}), bf16[4,160,1024]{2,1,0:T(8,128)(2,1)S(1)}, u32[]{:S(2)}, u32[]{:S(2)}) %all-to-all-start.3) | async-done | bytes 1310752 | tf_op jit(solution)/shard_map/all_to_all | solution.py:61
  174.6 20.8 %all_to_all.35 = bf16[4,160,1152]{2,1,0:T(8,128)(2,1)S(1)} all-to-all(bf16[4,160,1152]{2,1,0:T(8,128)(2,1)S(1)} %broadcast_in_dim.74), channel_id=1, replica_groups=mesh['x'=4,'core'=2,'z'=16,'y'=4] {'x'}, dimensions={0} | all-to-all | bytes 2949120 | tf_op jit(solution)/shard_map/all_to_all | solution.py:61
  200.4 6.2 %all-to-all-start.6 = ((bf16[4,160,512]{2,1,0:T(8,128)(2,1)}), bf16[4,160,512]{2,1,0:T(8,128)(2,1)}, u32[]{:S(2)}, u32[]{:S(2)}) async-start(bf16[4,160,512]{2,1,0:T(8,128)(2,1)} %broadcast_in_dim.83), calls=%async_computation.6 | async-start | bytes 1310720 | tf_op jit(solution)/shard_map/all_to_all | solution.py:61
  235.2 10.5 %all-to-all-done.5 = bf16[4,320,512]{2,1,0:T(8,128)(2,1)} async-done(((bf16[4,320,512]{2,1,0:T(8,128)(2,1)}), bf16[4,320,512]{2,1,0:T(8,128)(2,1)}, u32[]{:S(2)}, u32[]{:S(2)}) %all-to-all-start.5) | async-done | bytes 1310752 | tf_op jit(solution)/shard_map/all_to_all | solution.py:61
  249.6 6.6 %collective-permute-start.19 = (bf16[80,512]{0,1:T(8,128)(2,1)S(1)}, bf16[80,512]{0,1:T(8,128)(2,1)S(1)}, u32[]{:S(2)}, u32[]{:S(2)}) collective-permute-start(bf16[80,512]{0,1:T(8,128)(2,1)S(1)} %get-tuple-element.44), channel_id=1, source_target_pairs={{56,0},{60,4},{0,8},{4,12},{8,16},{12,20},{16,24},{20,28},{24,32},... | collective-permute-start | bytes 245768 | tf_op jit(solution)/shard_map/ppermute | solution.py:19
  258.1 5.3 %collective-permute-start.17 = (bf16[160,512]{0,1:T(8,128)(2,1)S(1)}, bf16[160,512]{0,1:T(8,128)(2,1)S(1)}, u32[]{:S(2)}, u32[]{:S(2)}) collective-permute-start(bf16[160,512]{0,1:T(8,128)(2,1)S(1)} %get-tuple-element.46), channel_id=1, source_target_pairs={{60,0},{0,4},{4,8},{8,12},{12,16},{16,20},{20,24},{24,28},{28,32},... | collective-permute-start | bytes 491528 | tf_op jit(solution)/shard_map/ppermute | solution.py:19
  273.2 6.0 %collective-permute-start.21 = (bf16[40,512]{0,1:T(8,128)(2,1)S(1)}, bf16[40,512]{0,1:T(8,128)(2,1)S(1)}, u32[]{:S(2)}, u32[]{:S(2)}) collective-permute-start(bf16[40,512]{0,1:T(8,128)(2,1)S(1)} %get-tuple-element.48), channel_id=1, source_target_pairs={{48,0},{52,4},{56,8},{60,12},{0,16},{4,20},{8,24},{12,28},{16,32},... | collective-permute-start | bytes 122888 | tf_op jit(solution)/shard_map/ppermute | solution.py:19
  279.2 5.3 %collective-permute-start.23 = (bf16[40,512]{0,1:T(8,128)(2,1)S(1)}, bf16[40,512]{0,1:T(8,128)(2,1)S(1)}, u32[]{:S(2)}, u32[]{:S(2)}) collective-permute-start(bf16[40,512]{0,1:T(8,128)(2,1)S(1)} %get-tuple-element.49), channel_id=1, source_target_pairs={{32,0},{36,4},{40,8},{44,12},{48,16},{52,20},{56,24},{60,28},{0,32... | collective-permute-start | bytes 122888 | tf_op jit(solution)/shard_map/ppermute | solution.py:19
  284.4 4.9 %collective-permute-start.22 = (bf16[40,512]{0,1:T(8,128)(2,1)S(1)}, bf16[40,512]{0,1:T(8,128)(2,1)S(1)}, u32[]{:S(2)}, u32[]{:S(2)}) collective-permute-start(bf16[40,512]{0,1:T(8,128)(2,1)S(1)} %get-tuple-element.50), channel_id=1, source_target_pairs={{16,0},{20,4},{24,8},{28,12},{32,16},{36,20},{40,24},{44,28},{48,3... | collective-permute-start | bytes 122888 | tf_op jit(solution)/shard_map/ppermute | solution.py:19
  295.1 4.9 %collective-permute-done.23 = bf16[40,512]{0,1:T(8,128)(2,1)S(1)} collective-permute-done((bf16[40,512]{0,1:T(8,128)(2,1)S(1)}, bf16[40,512]{0,1:T(8,128)(2,1)S(1)}, u32[]{:S(2)}, u32[]{:S(2)}) %collective-permute-start.23) | collective-permute-done | bytes 40992 | tf_op jit(solution)/shard_map/ppermute | solution.py:19
  300.0 5.3 %collective-permute-done.22 = bf16[40,512]{0,1:T(8,128)(2,1)S(1)} collective-permute-done((bf16[40,512]{0,1:T(8,128)(2,1)S(1)}, bf16[40,512]{0,1:T(8,128)(2,1)S(1)}, u32[]{:S(2)}, u32[]{:S(2)}) %collective-permute-start.22) | collective-permute-done | bytes 40992 | tf_op jit(solution)/shard_map/ppermute | solution.py:19
  (168 shorter events, 124.0 us)
Async XLA Ops:
  0.6 43.9 %collective-permute-start.9 = (bf16[40,448]{1,0:T(8,128)(2,1)}, bf16[40,448]{1,0:T(8,128)(2,1)S(1)}, u32[]{:S(2)}, u32[]{:S(2)}) collective-permute-start(bf16[40,448]{1,0:T(8,128)(2,1)} %param.8), channel_id=1, source_target_pairs={{32,0},{36,4},{40,8},{44,12},{48,16},{52,20},{56,24},{60,28},{0,32... | collective-permute-start | bytes 107528 | tf_op jit(solution)/shard_map/ppermute | solution.py:19
  16.5 28.0 %collective-permute-start.8 = (bf16[40,448]{1,0:T(8,128)(2,1)}, bf16[40,448]{1,0:T(8,128)(2,1)S(1)}, u32[]{:S(2)}, u32[]{:S(2)}) collective-permute-start(bf16[40,448]{1,0:T(8,128)(2,1)} %param.8), channel_id=1, source_target_pairs={{48,0},{52,4},{56,8},{60,12},{0,16},{4,20},{8,24},{12,28},{16,32},... | collective-permute-start | bytes 107528 | tf_op jit(solution)/shard_map/ppermute | solution.py:19
  20.8 18.6 %collective-permute-start.7 = (bf16[40,448]{1,0:T(8,128)(2,1)}, bf16[40,448]{1,0:T(8,128)(2,1)S(1)}, u32[]{:S(2)}, u32[]{:S(2)}) collective-permute-start(bf16[40,448]{1,0:T(8,128)(2,1)} %param.8), channel_id=1, source_target_pairs={{16,0},{20,4},{24,8},{28,12},{32,16},{36,20},{40,24},{44,28},{48,3... | collective-permute-start | bytes 107528 | tf_op jit(solution)/shard_map/ppermute | solution.py:19
  30.2 23.7 %collective-permute-start.2 = (bf16[40,512]{0,1:T(8,128)(2,1)S(1)}, bf16[40,512]{0,1:T(8,128)(2,1)S(1)}, u32[]{:S(2)}, u32[]{:S(2)}) collective-permute-start(bf16[40,512]{0,1:T(8,128)(2,1)S(1)} %constant_dynamic-update-slice_fusion), channel_id=1, source_target_pairs={{32,0},{36,4},{40,8},{44,12},{48,16},{52,20},{56,24},{60,28},{0,32... | collective-permute-start | bytes 122888 | tf_op jit(solution)/shard_map/ppermute | solution.py:19
  33.9 29.8 %collective-permute-start.1 = (bf16[40,512]{0,1:T(8,128)(2,1)S(1)}, bf16[40,512]{0,1:T(8,128)(2,1)S(1)}, u32[]{:S(2)}, u32[]{:S(2)}) collective-permute-start(bf16[40,512]{0,1:T(8,128)(2,1)S(1)} %constant_dynamic-update-slice_fusion), channel_id=1, source_target_pairs={{48,0},{52,4},{56,8},{60,12},{0,16},{4,20},{8,24},{12,28},{16,32},... | collective-permute-start | bytes 122888 | tf_op jit(solution)/shard_map/ppermute | solution.py:19
  39.4 27.2 %collective-permute-start = (bf16[40,512]{0,1:T(8,128)(2,1)S(1)}, bf16[40,512]{0,1:T(8,128)(2,1)S(1)}, u32[]{:S(2)}, u32[]{:S(2)}) collective-permute-start(bf16[40,512]{0,1:T(8,128)(2,1)S(1)} %constant_dynamic-update-slice_fusion), channel_id=1, source_target_pairs={{16,0},{20,4},{24,8},{28,12},{32,16},{36,20},{40,24},{44,28},{48,3... | collective-permute-start | bytes 122888 | tf_op jit(solution)/shard_map/ppermute | solution.py:19
  44.6 29.6 %collective-permute-start.11 = (bf16[160,448]{1,0:T(8,128)(2,1)S(1)}, bf16[160,448]{1,0:T(8,128)(2,1)S(1)}, u32[]{:S(2)}, u32[]{:S(2)}) collective-permute-start(bf16[160,448]{1,0:T(8,128)(2,1)S(1)} %get-tuple-element.55), channel_id=1, source_target_pairs={{60,0},{0,4},{4,8},{8,12},{12,16},{16,20},{20,24},{24,28},{28,32},... | collective-permute-start | bytes 430088 | tf_op jit(solution)/shard_map/ppermute | solution.py:19
  47.5 22.7 %collective-permute-start.10 = (bf16[160,448]{1,0:T(8,128)(2,1)S(1)}, bf16[160,448]{1,0:T(8,128)(2,1)S(1)}, u32[]{:S(2)}, u32[]{:S(2)}) collective-permute-start(bf16[160,448]{1,0:T(8,128)(2,1)S(1)} %get-tuple-element.55), channel_id=1, source_target_pairs={{4,0},{8,4},{12,8},{16,12},{20,16},{24,20},{28,24},{32,28},{36,32}... | collective-permute-start | bytes 430088 | tf_op jit(solution)/shard_map/ppermute | solution.py:19
  53.9 28.3 %collective-permute-start.13 = (bf16[80,448]{1,0:T(8,128)(2,1)S(1)}, bf16[80,448]{1,0:T(8,128)(2,1)S(1)}, u32[]{:S(2)}, u32[]{:S(2)}) collective-permute-start(bf16[80,448]{1,0:T(8,128)(2,1)S(1)} %get-tuple-element.53), channel_id=1, source_target_pairs={{56,0},{60,4},{0,8},{4,12},{8,16},{12,20},{16,24},{20,28},{24,32},... | collective-permute-start | bytes 215048 | tf_op jit(solution)/shard_map/ppermute | solution.py:19
  63.7 13.2 %collective-permute-start.12 = (bf16[80,448]{1,0:T(8,128)(2,1)S(1)}, bf16[80,448]{1,0:T(8,128)(2,1)S(1)}, u32[]{:S(2)}, u32[]{:S(2)}) collective-permute-start(bf16[80,448]{1,0:T(8,128)(2,1)S(1)} %get-tuple-element.54), channel_id=1, source_target_pairs={{8,0},{12,4},{16,8},{20,12},{24,16},{28,20},{32,24},{36,28},{40,32... | collective-permute-start | bytes 215048 | tf_op jit(solution)/shard_map/ppermute | solution.py:19
  66.9 19.3 %collective-permute-start.4 = (bf16[160,512]{0,1:T(8,128)(2,1)S(1)}, bf16[160,512]{0,1:T(8,128)(2,1)S(1)}, u32[]{:S(2)}, u32[]{:S(2)}) collective-permute-start(bf16[160,512]{0,1:T(8,128)(2,1)S(1)} %pad_maximum_fusion.10), channel_id=1, source_target_pairs={{60,0},{0,4},{4,8},{8,12},{12,16},{16,20},{20,24},{24,28},{28,32},... | collective-permute-start | bytes 491528 | tf_op jit(solution)/shard_map/ppermute | solution.py:19
  70.2 16.0 %collective-permute-start.3 = (bf16[160,512]{0,1:T(8,128)(2,1)S(1)}, bf16[160,512]{0,1:T(8,128)(2,1)S(1)}, u32[]{:S(2)}, u32[]{:S(2)}) collective-permute-start(bf16[160,512]{0,1:T(8,128)(2,1)S(1)} %pad_maximum_fusion.10), channel_id=1, source_target_pairs={{4,0},{8,4},{12,8},{16,12},{20,16},{24,20},{28,24},{32,28},{36,32}... | collective-permute-start | bytes 491528 | tf_op jit(solution)/shard_map/ppermute | solution.py:19
  89.6 19.3 %all-to-all-start.1 = ((bf16[4,320,448]{2,1,0:T(8,128)(2,1)}), bf16[4,320,448]{2,1,0:T(8,128)(2,1)S(1)}, u32[]{:S(2)}, u32[]{:S(2)}) async-start(bf16[4,320,448]{2,1,0:T(8,128)(2,1)} %pad_maximum_fusion.1), calls=%async_computation.1 | async-start | bytes 2621440 | tf_op jit(solution)/shard_map/all_to_all | solution.py:61
  108.9 17.1 %all-to-all-start = ((bf16[4,320,512]{2,1,0:T(8,128)(2,1)}), bf16[4,320,512]{2,1,0:T(8,128)(2,1)S(1)}, u32[]{:S(2)}, u32[]{:S(2)}) async-start(bf16[4,320,512]{2,1,0:T(8,128)(2,1)} %pad_maximum_fusion), calls=%async_computation | async-start | bytes 2621440 | tf_op jit(solution)/shard_map/all_to_all | solution.py:61
  137.1 14.1 %all-to-all-start.2 = ((bf16[4,160,512]{2,1,0:T(8,128)(2,1)}), bf16[4,160,512]{2,1,0:T(8,128)(2,1)S(1)}, u32[]{:S(2)}, u32[]{:S(2)}) async-start(bf16[4,160,512]{2,1,0:T(8,128)(2,1)} %bitcast.80), calls=%async_computation.2 | async-start | bytes 1310720 | tf_op jit(solution)/shard_map/all_to_all | solution.py:61
  152.0 21.1 %all-to-all-start.3 = ((bf16[4,160,1024]{2,1,0:T(8,128)(2,1)}), bf16[4,160,1024]{2,1,0:T(8,128)(2,1)S(1)}, u32[]{:S(2)}, u32[]{:S(2)}) async-start(bf16[4,160,1024]{2,1,0:T(8,128)(2,1)} %bitcast.74), calls=%async_computation.3 | async-start | bytes 2621440 | tf_op jit(solution)/shard_map/all_to_all | solution.py:61
  197.6 15.3 %collective-permute-start.16 = (bf16[640,1152]{0,1:T(8,128)(2,1)}, bf16[640,1152]{0,1:T(8,128)(2,1)}, u32[]{:S(2)}, u32[]{:S(2)}) collective-permute-start(bf16[640,1152]{0,1:T(8,128)(2,1)} %copy.48), channel_id=1, source_target_pairs={{0,64},{64,0},{1,65},{65,1},{2,66},{66,2},{3,67},{67,3},{4,68},{68... | collective-permute-start | bytes 4423688 | tf_op jit(solution)/shard_map/ppermute | solution.py:57
  200.4 22.4 %all-to-all-start.6 = ((bf16[4,160,512]{2,1,0:T(8,128)(2,1)}), bf16[4,160,512]{2,1,0:T(8,128)(2,1)}, u32[]{:S(2)}, u32[]{:S(2)}) async-start(bf16[4,160,512]{2,1,0:T(8,128)(2,1)} %broadcast_in_dim.83), calls=%async_computation.6 | async-start | bytes 1310720 | tf_op jit(solution)/shard_map/all_to_all | solution.py:61
  222.8 22.9 %all-to-all-start.5 = ((bf16[4,320,512]{2,1,0:T(8,128)(2,1)}), bf16[4,320,512]{2,1,0:T(8,128)(2,1)}, u32[]{:S(2)}, u32[]{:S(2)}) async-start(bf16[4,320,512]{2,1,0:T(8,128)(2,1)} %pad_maximum_fusion.2), calls=%async_computation.5 | async-start | bytes 2621440 | tf_op jit(solution)/shard_map/all_to_all | solution.py:61
  249.6 19.8 %collective-permute-start.19 = (bf16[80,512]{0,1:T(8,128)(2,1)S(1)}, bf16[80,512]{0,1:T(8,128)(2,1)S(1)}, u32[]{:S(2)}, u32[]{:S(2)}) collective-permute-start(bf16[80,512]{0,1:T(8,128)(2,1)S(1)} %get-tuple-element.44), channel_id=1, source_target_pairs={{56,0},{60,4},{0,8},{4,12},{8,16},{12,20},{16,24},{20,28},{24,32},... | collective-permute-start | bytes 245768 | tf_op jit(solution)/shard_map/ppermute | solution.py:19
  256.2 13.1 %collective-permute-start.20 = (bf16[80,512]{0,1:T(8,128)(2,1)S(1)}, bf16[80,512]{0,1:T(8,128)(2,1)S(1)}, u32[]{:S(2)}, u32[]{:S(2)}) collective-permute-start(bf16[80,512]{0,1:T(8,128)(2,1)S(1)} %get-tuple-element.45), channel_id=1, source_target_pairs={{8,0},{12,4},{16,8},{20,12},{24,16},{28,20},{32,24},{36,28},{40,32... | collective-permute-start | bytes 245768 | tf_op jit(solution)/shard_map/ppermute | solution.py:19
  273.2 21.9 %collective-permute-start.21 = (bf16[40,512]{0,1:T(8,128)(2,1)S(1)}, bf16[40,512]{0,1:T(8,128)(2,1)S(1)}, u32[]{:S(2)}, u32[]{:S(2)}) collective-permute-start(bf16[40,512]{0,1:T(8,128)(2,1)S(1)} %get-tuple-element.48), channel_id=1, source_target_pairs={{48,0},{52,4},{56,8},{60,12},{0,16},{4,20},{8,24},{12,28},{16,32},... | collective-permute-start | bytes 122888 | tf_op jit(solution)/shard_map/ppermute | solution.py:19
  279.2 20.9 %collective-permute-start.23 = (bf16[40,512]{0,1:T(8,128)(2,1)S(1)}, bf16[40,512]{0,1:T(8,128)(2,1)S(1)}, u32[]{:S(2)}, u32[]{:S(2)}) collective-permute-start(bf16[40,512]{0,1:T(8,128)(2,1)S(1)} %get-tuple-element.49), channel_id=1, source_target_pairs={{32,0},{36,4},{40,8},{44,12},{48,16},{52,20},{56,24},{60,28},{0,32... | collective-permute-start | bytes 122888 | tf_op jit(solution)/shard_map/ppermute | solution.py:19
  284.4 20.9 %collective-permute-start.22 = (bf16[40,512]{0,1:T(8,128)(2,1)S(1)}, bf16[40,512]{0,1:T(8,128)(2,1)S(1)}, u32[]{:S(2)}, u32[]{:S(2)}) collective-permute-start(bf16[40,512]{0,1:T(8,128)(2,1)S(1)} %get-tuple-element.50), channel_id=1, source_target_pairs={{16,0},{20,4},{24,8},{28,12},{32,16},{36,20},{40,24},{44,28},{48,3... | collective-permute-start | bytes 122888 | tf_op jit(solution)/shard_map/ppermute | solution.py:19
  (26 other events, 305.8 us)

commit v2 on v1

v2 whole, which is shorter than its diff:
```python
import jax
import jax.numpy as jnp
from jax import lax
from jax.experimental import pallas as pl
from jax.experimental.pallas import tpu as pltpu
from jax.sharding import Mesh, PartitionSpec as P

BF = jnp.bfloat16
F32 = jnp.float32
I32 = jnp.int32
TOK = 40
FEAT = 448
WIDE = 512
HALF = 512
CAP = 20
ALL = 640
PART = 160
ROWS = 320
EXP = 32


def dot(a, b, dims=((1,), (0,))):
    return lax.dot_general(a, b, (dims, ((), ())), preferred_element_type=F32)


LAST = ((1,), (1,))
FIRST = ((0,), (0,))


def call(body, outs, *args, scratch=(), flops=0):
    moved = sum(a.size * a.dtype.itemsize for a in args[1:])
    specs = [pl.BlockSpec(memory_space=pltpu.SMEM)]
    specs += [pl.BlockSpec(memory_space=pltpu.VMEM)] * (len(args) - 1)
    return pl.pallas_call(
        body,
        out_shape=[jax.ShapeDtypeStruct(s, d) for s, d in outs],
        in_specs=specs,
        out_specs=[pl.BlockSpec(memory_space=pltpu.VMEM)] * len(outs),
        scratch_shapes=list(scratch),
        compiler_params=pltpu.CompilerParams(vmem_limit_bytes=24 << 20),
        cost_estimate=pl.CostEstimate(flops=flops, bytes_accessed=moved, transcendentals=0),
    )(*args)


def iota(shape, axis):
    return lax.broadcasted_iota(I32, shape, axis)


def pack(sc, tok, cot, ids, wts, gate, up, down, out, w):
    wts_f = wts[...].astype(F32)
    named = jnp.zeros((EXP, TOK), F32)
    weight = jnp.zeros((EXP, TOK), F32)
    for k in range(8):
        match = iota((EXP, TOK), 0) == ids[k : k + 1, :]
        named += jnp.where(match, 1.0, 0.0)
        weight += jnp.where(match, wts_f[k : k + 1, :], 0.0)
    before = (iota((TOK, TOK), 0) < iota((TOK, TOK), 1)).astype(BF)
    rank = dot(named.astype(BF), before)
    code = jnp.concatenate([named * (rank + 1.0), weight], 0).astype(BF)
    spread = (iota((64, 128), 0) + 64 == iota((64, 128), 1)).astype(BF)
    meta = dot(code, spread, FIRST).astype(BF)
    low = iota((TOK, 128), 1) < 64
    out[:, 0:FEAT] = tok[...]
    out[:, 384:512] = jnp.where(low, out[:, 384:512], meta)
    out[:, 512 : 512 + FEAT] = cot[...]
    out[:, 896:1024] = jnp.where(low, out[:, 896:1024], jnp.zeros((TOK, 128), BF))
    w[0:FEAT, 0:512] = gate[...]
    w[0:FEAT, 512:1024] = up[...]
    w[0:FEAT, 1024:1536] = down[...]
    w[FEAT:WIDE, :] = jnp.zeros((WIDE - FEAT, 1536), BF)


def placed(code, block, core):
    place = code.astype(I32) - 1 + block * CAP + core * PART
    place = jnp.where(place >= ROWS, place - ROWS, place)
    return jnp.where(code > 0.5, place, -1)


def choose(sc, every, near, send):
    lanes = iota((8, 128), 1) - 64
    row = iota((8, 128), 0)
    sel = ((row == 0) & (lanes == sc[0])) | ((row == 1) & (lanes == sc[1]))
    codes = dot(sel.astype(BF), every[:, 384:512], LAST)
    block = (iota((1, ALL), 1) * 1639) >> 16
    for k, out in ((0, near), (1, send)):
        place = placed(codes[k : k + 1, :], block, sc[2])
        one_hot = (iota((ROWS, ALL), 0) == place).astype(BF)
        out[...] = dot(one_hot, every[...]).astype(BF)


def products(a, b, w, wf, lo):
    x = jnp.concatenate([a[lo : lo + PART, 0:512], b[lo : lo + PART, 0:512]], 0)
    dy = jnp.concatenate([a[lo : lo + PART, 512:1024], b[lo : lo + PART, 512:1024]], 0)
    for h, ref in ((0, w), (1, wf)):
        for c, left in ((0, x), (1, x), (2, dy)):
            yield 1536 * h + 512 * c, dot(left, ref[:, 512 * c : 512 * c + 512])


def forward_others(sc, near, far, w, wf, out):
    for at, value in products(near, far, w, wf, PART):
        out[:, at : at + 512] = value.astype(BF)


def forward_mine(sc, near, far, w, wf, got, out):
    for at, value in products(near, far, w, wf, 0):
        out[:, at : at + 512] = (value + got[:, at : at + 512].astype(F32)).astype(BF)


def activate(sc, pieces, near_tile, far_tile, g_out, s_out):
    q = ROWS // 4
    start = pl.multiple_of((sc[3] % 2) * q, 16)
    a = near_tile[pl.ds(start, q), :].astype(F32)
    b = far_tile[pl.ds(start, q), :].astype(F32)
    tile = jnp.where(sc[3] < 2, a, b)
    lane = iota((q, 128), 1)
    scale = jnp.sum(jnp.where(lane == 96 + sc[0], tile, 0.0), axis=1, keepdims=True)
    dots = jnp.zeros((q, 1), F32)
    for h in range(2):
        at = 1536 * h

        def total(c):
            cols = slice(at + 512 * c, at + 512 * c + 512)
            t = pieces[0, :, cols].astype(F32) + pieces[1, :, cols].astype(F32)
            return t + pieces[2, :, cols].astype(F32) + pieces[3, :, cols].astype(F32)

        gate_pre, up_pre, hidden_grad = total(0), total(1), total(2)
        sig = jax.nn.sigmoid(gate_pre)
        hidden = (gate_pre * sig * up_pre).astype(BF).astype(F32)
        dots += jnp.sum(hidden * hidden_grad, axis=1, keepdims=True)
        act_grad = scale * hidden_grad
        gate_g = (act_grad * up_pre * sig * (1.0 + gate_pre * (1.0 - sig))).astype(BF)
        up_g = (act_grad * gate_pre * sig).astype(BF)
        scaled = (scale * hidden).astype(BF)
        for k in range(4):
            g_out[k, :, 1024 * h : 1024 * h + 512] = gate_g
            g_out[k, :, 1024 * h + 512 : 1024 * h + 1024] = up_g
            s_out[k, :, 512 * h : 512 * h + 512] = scaled
    dot_tile = jnp.where(lane == 0, dots, 0.0).astype(BF)
    for k in range(4):
        g_out[k, :, 2048:2176] = dot_tile


def backward(sc, g, go, w, wf, keep, send):
    put = (iota((128, WIDE), 0) == 0) & (iota((128, WIDE), 1) == FEAT + sc[0])
    put = put.astype(BF)
    for lo, out in ((PART, send), (0, keep)):
        for at, ref in ((0, g), (PART, go)):
            t = dot(ref[lo : lo + PART, 0:1024], w[:, 0:1024], LAST)
            t += dot(ref[lo : lo + PART, 1024:2048], wf[:, 0:1024], LAST)
            t += dot(ref[lo : lo + PART, 2048:2176], put)
            out[at : at + PART, :] = t.astype(BF)


def weight_grads(sc, near, far, g, go, s, so, mine, partner):
    for c in range(3):
        at = 0 if c < 2 else 512
        total = [None, None]
        for rows, lo, right, right_s in (
            (near, 0, g, s),
            (far, 0, g, s),
            (near, PART, go, so),
            (far, PART, go, so),
        ):
            at_r = 0 if rows is near else PART
            left = rows[lo : lo + PART, at : at + 512]
            for h in range(2):
                r = right if c < 2 else right_s
                col = 1024 * h + 512 * c if c < 2 else 512 * h
                t = dot(left, r[at_r : at_r + PART, col : col + 512], FIRST)
                total[h] = t if total[h] is None else total[h] + t
        mine[:, 512 * c : 512 * c + 512] = total[0][:FEAT]
        partner[:, 512 * c : 512 * c + 512] = total[1][:FEAT].astype(BF)


def scatter(sc, tile, own, oth, *outs):
    lane = iota((ALL, 128), 1)
    block = (iota((ALL, 1), 0) * 1639) >> 16
    value = tile[...].astype(F32)
    total = None
    for k, slot in ((0, own), (1, oth)):
        code = jnp.sum(jnp.where(lane == 64 + sc[k], value, 0.0), axis=1, keepdims=True)
        place = placed(code, block, sc[2])
        if k == 0:
            hit = iota((ALL, ALL), 1) == place
        else:
            hit = hit | (iota((ALL, ALL), 1) == jnp.where(place >= 0, place + ROWS, -1))
    both = jnp.concatenate([own[...], oth[...]], 0)
    total = dot(hit.astype(BF), both)
    at = 0
    for out in outs:
        rows = out.shape[0]
        out[...] = total[at : at + rows].astype(BF)
        at += rows


def add_near(sc, far, a, b, c, d, e, first, mid, last):
    s = far[...].astype(F32) + a[...].astype(F32) + b[...].astype(F32)
    s = s + c[...].astype(F32) + d[...].astype(F32)
    first[...] = (s[:TOK] + e[...].astype(F32)).astype(BF)
    mid[...] = s[TOK : 2 * TOK]
    last[...] = s[2 * TOK :].astype(BF)


def finish_tokens(sc, mid, a, b, ids, tok, route):
    total = mid[...] + a[...].astype(F32) + b[...].astype(F32)
    tok[...] = total[:, :FEAT].astype(BF)
    sel = (iota((EXP, 128), 0) + 64 == iota((EXP, 128), 1)).astype(BF)
    dots = dot(sel, total[:, 384:512].astype(BF), LAST)
    for k in range(8):
        match = iota((EXP, TOK), 0) == ids[k : k + 1, :]
        route[k : k + 1, :] = jnp.sum(jnp.where(match, dots, 0.0), axis=0, keepdims=True)


def finish_weights(sc, mine, got, gate, up, down):
    for c, out in enumerate((gate, up, down)):
        cols = slice(512 * c, 512 * c + 512)
        out[...] = (mine[:, cols] + got[:, cols].astype(F32)).astype(BF)


def take(a, axis, step):
    n = lax.axis_size(axis)
    return lax.ppermute(a, axis, [((i + step) % n, i) for i in range(n)])


def swap_core(a):
    return lax.ppermute(a, "core", [(0, 1), (1, 0)])


def swap_half(a):
    return lax.ppermute(a, "y", [(0, 1), (1, 0), (2, 3), (3, 2)])


def swap_expert(a):
    return lax.ppermute(a, "y", [(1, 2), (2, 1), (3, 0), (0, 3)])


def trade(a, axis):
    return lax.all_to_all(a, axis, split_axis=0, concat_axis=0, tiled=True)


def on_device(tokens, cotangent, expert_ids, route_weight, gate_weight, up_weight, down_weight):
    core = lax.axis_index("core")
    high = (lax.axis_index("y") >= 2).astype(I32)
    z = lax.axis_index("z")
    sc = jnp.stack([2 * z + high, 2 * z + 1 - high, core, lax.axis_index("x")]).astype(I32)
    ids_t = expert_ids.T
    payload, w = call(
        pack,
        [((TOK, 1024), BF), ((WIDE, 1536), BF)],
        sc, tokens, cotangent, ids_t, route_weight.T,
        gate_weight[0], up_weight[0], down_weight[0].T,
    )
    five = take(payload, "z", 5)
    minus = take(payload, "z", -5)
    group = jnp.concatenate([five, payload, minus], 0)
    near_z = [take(group, "z", step) for step in (1, -1, 2, -2)]
    eight = take(five, "z", 3)
    w_far = swap_half(w)
    every = jnp.concatenate([group] + near_z + [eight], 0)
    every, w_far = lax.optimization_barrier((every, w_far))
    near, send = call(
        choose, [((ROWS, 1024), BF)] * 2, sc, every, flops=4 * ROWS * ALL * 1024
    )
    far = swap_expert(send)
    flops = 2 * ROWS * WIDE * 3072
    others = call(
        forward_others, [((ROWS, 3072), BF)], sc, near, far, w, w_far, flops=flops
    )[0]
    pair = call(
        forward_mine, [((ROWS, 3072), BF)], sc, near, far, w, w_far, swap_core(others), flops=flops
    )[0]
    q = ROWS // 4
    pieces = trade(pair.reshape(4, q, 3072), "x")
    g_out, s_out = call(
        activate, [((4, q, 2176), BF), ((4, q, 1024), BF)],
        sc, pieces, near[:PART, 384:512], far[:PART, 384:512],
    )
    g = trade(g_out, "x")
    s_out, g = lax.optimization_barrier((s_out, g))
    s = trade(s_out, "x").reshape(ROWS, 1024)
    g = g.reshape(ROWS, 2176)
    g_far = swap_core(g)
    keep, away = call(backward, [((ROWS, WIDE), BF)] * 2, sc, g, g_far, w, w_far)
    back = swap_expert(away)
    s_far = swap_core(s)
    mine_w, partner_w = call(
        weight_grads, [((FEAT, 1536), F32), ((FEAT, 1536), BF)],
        sc, near, far, g, g_far, s, s_far, flops=8 * ROWS * WIDE * 1536,
    )
    got_w = swap_half(partner_w)
    sums = call(
        scatter, [((3 * TOK, WIDE), BF)] * 5 + [((TOK, WIDE), BF)],
        sc, every[:, 384:512], keep, back, flops=2 * ALL * ALL * WIDE,
    )
    moved = [take(a, "z", -step) for a, step in zip(sums[1:5], (1, -1, 2, -2))]
    moved.append(take(sums[5], "z", -3))
    first, mid, last = call(
        add_near, [((TOK, WIDE), BF), ((TOK, WIDE), F32), ((TOK, WIDE), BF)], sc, sums[0], *moved
    )
    from_first, from_last = take(first, "z", -5), take(last, "z", 5)
    from_first, from_last, got_w = lax.optimization_barrier((from_first, from_last, got_w))
    tok, route = call(
        finish_tokens, [((TOK, FEAT), BF), ((8, TOK), F32)], sc, mid, from_first, from_last, ids_t
    )
    gate, up, down = call(finish_weights, [((FEAT, 512), BF)] * 3, sc, mine_w, got_w)
    return (tok, route.astype(BF).T, gate[None], up[None], down.T[None])


def solution(mesh):
    fine = Mesh(mesh.devices.reshape(4, 2, 16, 4), ("x", "core", "z", "y"))
    dp, expert = ("x", "core"), ("z", "y")
    return jax.shard_map(
        on_device,
        mesh=fine,
        in_specs=(
            P(expert, dp),
            P(expert, dp),
            P(expert, None),
            P(expert, None),
            P(expert, dp, None),
            P(expert, dp, None),
            P(expert, None, dp),
        ),
        out_specs=(
            P(expert, dp),
            P(expert, None),
            P(expert, dp, None),
            P(expert, dp, None),
            P(expert, None, dp),
        ),
        check_vma=False,
    )
```

time: 313 us -> 240 us (0.77)
  starting transfers between devices: 141 us -> 92.6 us
  matrix products: 26.8 us -> 0 us
  Pallas kernels: 0 us -> 21 us
  other arithmetic: 15.4 us -> 0.66 us
  blocking collectives: 20.8 us -> 35.2 us
  local copies, waits for them, and re-layouts: 19.7 us -> 9.89 us
  waiting for transfers between devices: 81.8 us -> 76.4 us
    ppermute x21 -> x14, starting transfers between devices: 103 us -> 68.3 us  [take(): return lax.ppermute(a, axis, [((i + step) % n, i) for i in range(n)])]
    all_to_all x6 -> x1, waiting for transfers between devices: 53.8 us -> 22 us  [trade(): return lax.all_to_all(a, axis, split_axis=0, concat_axis=0, tiled=True)]
    dot_general x21 -> x0, matrix products: 26.8 us -> none  [dot(): return lax.dot_general(a, b, (dims, ((), ())), preferred_element_type=F32)]
    all_to_all x6 -> x1, starting transfers between devices: 28.9 us -> 4.82 us  [trade(): return lax.all_to_all(a, axis, split_axis=0, concat_axis=0, tiled=True)]
    pallas_call x0 -> x11, Pallas kernels: none -> 21 us  [call(): pl.pallas_call(body, out_shape=[jax.ShapeDtypeStruct(s, d) for s, d in ou...]
    ppermute x0 -> x4, waiting for transfers between devices: none -> 18.1 us  [the longest x2 18.1 us: swap_expert(): return lax.ppermute(a, 'y', [(1, 2), (2, 1), (3, 0), (0, 3)])]
    all_to_all x1 -> x2, blocking collectives: 20.8 us -> 35.2 us  [trade(): return lax.all_to_all(a, axis, split_axis=0, concat_axis=0, tiled=True)]
    ppermute x0 -> x4, starting transfers between devices: none -> 13.7 us  [the longest x2 8.27 us: swap_expert(): return lax.ppermute(a, 'y', [(1, 2), (2, 1), (3, 0), (0, 3)])]
  transfers between devices with their start and end apart: 31 -> 22, of which waited for: 14 -> 13; matrix products, arithmetic and copies ran while one was open for 15% -> 1% of each run, Pallas kernels for 0% -> 2%
where the time goes in v2:
time: 240 us; the launch traced here: 237 us
  starting transfers between devices  92.6 us (39%)
  waiting for transfers between devices  76.4 us (32%)
  blocking collectives  35.2 us (15%)
  Pallas kernels  21 us (9%)
  local copies, waits for them, and re-layouts  9.89 us (4%)
    ppermute x14, starting transfers between devices, take(): return lax.ppermute(a, axis, [((i + step) % n, i) for i in range(n)])  68.3 us
    all_to_all x2, blocking collectives, trade(): return lax.all_to_all(a, axis, split_axis=0, concat_axis=0, tiled=True)  35.2 us
    ppermute x14, waiting for transfers between devices, take(): return lax.ppermute(a, axis, [((i + step) % n, i) for i in range(n)])  30.3 us
    all_to_all x1, waiting for transfers between devices, trade(): return lax.all_to_all(a, axis, split_axis=0, concat_axis=0, tiled=True)  22 us
    pallas_call x11, Pallas kernels, call(): pl.pallas_call(body, out_shape=[jax.ShapeDtypeStruct(s, d) for s, d in ou...  21 us
    ppermute x2, waiting for transfers between devices, swap_expert(): return lax.ppermute(a, 'y', [(1, 2), (2, 1), (3, 0), (0, 3)])  18.1 us
    ppermute x2, starting transfers between devices, swap_expert(): return lax.ppermute(a, 'y', [(1, 2), (2, 1), (3, 0), (0, 3)])  8.27 us
    unnamed x34, local copies, waits for them, and re-layouts  7.38 us
  transfers between devices with their start and end apart: 22, of which 13 were waited for; matrix products, arithmetic and copies ran while one was open for 1% of the time, Pallas kernels for 2%

profile of v2, /device:TPU:6, one launch (start us, length us, event | category | flops | bytes accessed | tf_op | source)
XLA Modules:
  0.0 236.8 jit_solution(1959468996192218341)
XLA Ops:
  7.6 3.5 %collective-permute-start.7 = (bf16[512,1536]{1,0:T(8,128)(2,1)S(1)}, bf16[512,1536]{1,0:T(8,128)(2,1)S(1)}, u32[]{:S(2)}, u32[]{:S(2)}) collective-permute-start(bf16[512,1536]{1,0:T(8,128)(2,1)S(1)} %get-tuple-element.37.w), channel_id=1, source_target_pairs={{0,1},{1,0},{2,3},{3,2},{4,5},{5,4},{6,7},{7,6},{8,9},{9,8},{10,11... | collective-permute-start | bytes 4718600 | tf_op jit(solution)/shard_map/ppermute | solution.py:230
  11.1 14.4 %collective-permute-start = (bf16[40,1024]{1,0:T(8,128)(2,1)S(1)}, bf16[40,1024]{1,0:T(8,128)(2,1)S(1)}, u32[]{:S(2)}, u32[]{:S(2)}) collective-permute-start(bf16[40,1024]{1,0:T(8,128)(2,1)S(1)} %get-tuple-element.36), channel_id=1, source_target_pairs={{20,0},{24,4},{28,8},{32,12},{36,16},{40,20},{44,24},{48,28},{52,3... | collective-permute-start | bytes 245768 | tf_op jit(solution)/shard_map/ppermute | solution.py:222
  27.4 5.7 %collective-permute-done = bf16[40,1024]{1,0:T(8,128)(2,1)S(1)} collective-permute-done((bf16[40,1024]{1,0:T(8,128)(2,1)S(1)}, bf16[40,1024]{1,0:T(8,128)(2,1)S(1)}, u32[]{:S(2)}, u32[]{:S(2)}) %collective-permute-start) | collective-permute-done | bytes 81952 | tf_op jit(solution)/shard_map/ppermute | solution.py:222
  33.2 10.2 %collective-permute-done.1 = bf16[40,1024]{1,0:T(8,128)(2,1)S(1)} collective-permute-done((bf16[40,1024]{1,0:T(8,128)(2,1)S(1)}, bf16[40,1024]{1,0:T(8,128)(2,1)S(1)}, u32[]{:S(2)}, u32[]{:S(2)}) %collective-permute-start.1) | collective-permute-done | bytes 81952 | tf_op jit(solution)/shard_map/ppermute | solution.py:222
  45.7 3.4 %collective-permute-start.3 = (bf16[120,1024]{1,0:T(8,128)(2,1)S(1)}, bf16[120,1024]{1,0:T(8,128)(2,1)S(1)}, u32[]{:S(2)}, u32[]{:S(2)}) collective-permute-start(bf16[120,1024]{1,0:T(8,128)(2,1)S(1)} %get-tuple-element.67), channel_id=1, source_target_pairs={{60,0},{0,4},{4,8},{8,12},{12,16},{16,20},{20,24},{24,28},{28,32},... | collective-permute-start | bytes 737288 | tf_op jit(solution)/shard_map/ppermute | solution.py:222
  51.4 4.5 %collective-permute-start.5 = (bf16[120,1024]{1,0:T(8,128)(2,1)S(1)}, bf16[120,1024]{1,0:T(8,128)(2,1)S(1)}, u32[]{:S(2)}, u32[]{:S(2)}) collective-permute-start(bf16[120,1024]{1,0:T(8,128)(2,1)S(1)} %get-tuple-element.67), channel_id=1, source_target_pairs={{56,0},{60,4},{0,8},{4,12},{8,16},{12,20},{16,24},{20,28},{24,32},... | collective-permute-start | bytes 737288 | tf_op jit(solution)/shard_map/ppermute | solution.py:222
  56.0 3.1 %collective-permute-start.6 = (bf16[40,1024]{1,0:T(8,128)(2,1)S(1)}, bf16[40,1024]{1,0:T(8,128)(2,1)S(1)}, u32[]{:S(2)}, u32[]{:S(2)}) collective-permute-start(bf16[40,1024]{1,0:T(8,128)(2,1)S(1)} %collective-permute-done), channel_id=1, source_target_pairs={{12,0},{16,4},{20,8},{24,12},{28,16},{32,20},{36,24},{40,28},{44,3... | collective-permute-start | bytes 245768 | tf_op jit(solution)/shard_map/ppermute | solution.py:222
  59.1 7.6 %collective-permute-done.5 = bf16[120,1024]{1,0:T(8,128)(2,1)S(1)} collective-permute-done((bf16[120,1024]{1,0:T(8,128)(2,1)S(1)}, bf16[120,1024]{1,0:T(8,128)(2,1)S(1)}, u32[]{:S(2)}, u32[]{:S(2)}) %collective-permute-start.5) | collective-permute-done | bytes 245792 | tf_op jit(solution)/shard_map/ppermute | solution.py:222
  70.1 4.1 %collective-permute-start.8 = (bf16[320,1024]{1,0:T(8,128)(2,1)S(1)}, bf16[320,1024]{1,0:T(8,128)(2,1)S(1)}, u32[]{:S(2)}, u32[]{:S(2)}) collective-permute-start(bf16[320,1024]{1,0:T(8,128)(2,1)S(1)} %get-tuple-element.40), channel_id=1, source_target_pairs={{1,2},{2,1},{3,0},{0,3},{5,6},{6,5},{7,4},{4,7},{9,10},{10,9},{11,... | collective-permute-start | bytes 1966088 | tf_op jit(solution)/shard_map/ppermute | solution.py:234
  74.2 10.4 %collective-permute-done.8.far = bf16[320,1024]{1,0:T(8,128)(2,1)S(1)} collective-permute-done((bf16[320,1024]{1,0:T(8,128)(2,1)S(1)}, bf16[320,1024]{1,0:T(8,128)(2,1)S(1)}, u32[]{:S(2)}, u32[]{:S(2)}) %collective-permute-start.8) | collective-permute-done | bytes 655392 | tf_op jit(solution)/shard_map/ppermute | solution.py:234
  88.3 3.9 %collective-permute-done.9.got = bf16[320,3072]{1,0:T(8,128)(2,1)S(1)} collective-permute-done((bf16[320,3072]{1,0:T(8,128)(2,1)S(1)}, bf16[320,3072]{1,0:T(8,128)(2,1)S(1)}, u32[]{:S(2)}, u32[]{:S(2)}) %collective-permute-start.9) | collective-permute-done | bytes 1966112 | tf_op jit(solution)/shard_map/ppermute | solution.py:226
  95.2 4.8 %all-to-all-start = ((bf16[4,80,3072]{2,1,0:T(8,128)(2,1)}), bf16[4,80,3072]{2,1,0:T(8,128)(2,1)}, u32[]{:S(2)}, u32[]{:S(2)}) async-start(bf16[4,80,3072]{2,1,0:T(8,128)(2,1)} %bitcast.21), calls=%async_computation | async-start | bytes 3932160 | tf_op jit(solution)/shard_map/all_to_all | solution.py:238
  101.6 22.0 %all-to-all-done.pieces = bf16[4,80,3072]{2,1,0:T(8,128)(2,1)} async-done(((bf16[4,80,3072]{2,1,0:T(8,128)(2,1)}), bf16[4,80,3072]{2,1,0:T(8,128)(2,1)}, u32[]{:S(2)}, u32[]{:S(2)}) %all-to-all-start) | async-done | bytes 1966112 | tf_op jit(solution)/shard_map/all_to_all | solution.py:238
  125.8 21.0 %all_to_all.15 = bf16[4,80,2176]{2,1,0:T(8,128)(2,1)S(1)} all-to-all(bf16[4,80,2176]{2,1,0:T(8,128)(2,1)S(1)} %get-tuple-element.43), channel_id=1, replica_groups=mesh['x'=4,'core'=2,'z'=16,'y'=4] {'x'}, dimensions={0} | all-to-all | bytes 2785280 | tf_op jit(solution)/shard_map/all_to_all | solution.py:238
  148.8 14.2 %all_to_all.16 = bf16[4,80,1024]{2,1,0:T(8,128)(2,1)S(1)} all-to-all(bf16[4,80,1024]{2,1,0:T(8,128)(2,1)S(1)} %get-tuple-element.56), channel_id=1, replica_groups=mesh['x'=4,'core'=2,'z'=16,'y'=4] {'x'}, dimensions={0} | all-to-all | bytes 1310720 | tf_op jit(solution)/shard_map/all_to_all | solution.py:238
  167.0 4.0 %shard_map.118 = (f32[448,1536]{1,0:T(8,128)S(1)}, bf16[448,1536]{1,0:T(8,128)(2,1)S(1)}) custom-call(s32[4]{0:T(128)S(1)} %pad_add_fusion.sc, bf16[320,1024]{1,0:T(8,128)(2,1)S(1)} %copy-done.2, bf16[320,1024]{1,0:T(8,128)(2,1)S(1)} %copy-done.4, bf16[320,2176]{1,0:T(8,128)(2,1)S(1)} %bitcast.23, bf16[320,2176]{1,0:T(8,128)(2,1)S(1)} %collective-permute-done.10.go, ...), custom_call_target="tpu_custom_call" | custom-call | flops 2013265920 | bytes 5406720 | tf_op jit(solution)/shard_map/pallas_call | solution.py:34
  173.0 3.6 %shard_map.115 = (bf16[320,512]{1,0:T(8,128)(2,1)S(1)}, bf16[320,512]{1,0:T(8,128)(2,1)S(1)}) custom-call(s32[4]{0:T(128)S(1)} %pad_add_fusion.sc, bf16[320,2176]{1,0:T(8,128)(2,1)S(1)} %bitcast.24, bf16[320,2176]{1,0:T(8,128)(2,1)S(1)} %collective-permute-done.10.go, bf16[512,1536]{1,0:T(8,128)(2,1)S(1)} %get-tuple-element.37.w, ...), custom_call_target="tpu_custom_call" | custom-call | bytes 5931008 | tf_op jit(solution)/shard_map/pallas_call | solution.py:34
  176.6 4.2 %collective-permute-start.11 = (bf16[320,512]{1,0:T(8,128)(2,1)S(1)}, bf16[320,512]{1,0:T(8,128)(2,1)S(1)}, u32[]{:S(2)}, u32[]{:S(2)}) collective-permute-start(bf16[320,512]{1,0:T(8,128)(2,1)S(1)} %get-tuple-element.46), channel_id=1, source_target_pairs={{1,2},{2,1},{3,0},{0,3},{5,6},{6,5},{7,4},{4,7},{9,10},{10,9},{11,... | collective-permute-start | bytes 983048 | tf_op jit(solution)/shard_map/ppermute | solution.py:234
  181.7 7.7 %collective-permute-done.11.oth = bf16[320,512]{1,0:T(8,128)(2,1)S(1)} collective-permute-done((bf16[320,512]{1,0:T(8,128)(2,1)S(1)}, bf16[320,512]{1,0:T(8,128)(2,1)S(1)}, u32[]{:S(2)}, u32[]{:S(2)}) %collective-permute-start.11) | collective-permute-done | bytes 327712 | tf_op jit(solution)/shard_map/ppermute | solution.py:234
  190.9 9.4 %collective-permute-start.16 = (bf16[40,512]{1,0:T(8,128)(2,1)S(1)}, bf16[40,512]{1,0:T(8,128)(2,1)S(1)}, u32[]{:S(2)}, u32[]{:S(2)}) collective-permute-start(bf16[40,512]{1,0:T(8,128)(2,1)S(1)} %get-tuple-element.52), channel_id=1, source_target_pairs={{52,0},{56,4},{60,8},{0,12},{4,16},{8,20},{12,24},{16,28},{20,32},... | collective-permute-start | bytes 122888 | tf_op jit(solution)/shard_map/ppermute | solution.py:222
  202.3 5.1 %collective-permute-start.13 = (bf16[120,512]{1,0:T(8,128)(2,1)S(1)}, bf16[120,512]{1,0:T(8,128)(2,1)S(1)}, u32[]{:S(2)}, u32[]{:S(2)}) collective-permute-start(bf16[120,512]{1,0:T(8,128)(2,1)S(1)} %get-tuple-element.49), channel_id=1, source_target_pairs={{4,0},{8,4},{12,8},{16,12},{20,16},{24,20},{28,24},{32,28},{36,32}... | collective-permute-start | bytes 368648 | tf_op jit(solution)/shard_map/ppermute | solution.py:222
  209.3 6.0 %collective-permute-start.15 = (bf16[120,512]{1,0:T(8,128)(2,1)S(1)}, bf16[120,512]{1,0:T(8,128)(2,1)S(1)}, u32[]{:S(2)}, u32[]{:S(2)}) collective-permute-start(bf16[120,512]{1,0:T(8,128)(2,1)S(1)} %get-tuple-element.51), channel_id=1, source_target_pairs={{8,0},{12,4},{16,8},{20,12},{24,16},{28,20},{32,24},{36,28},{40,32... | collective-permute-start | bytes 368648 | tf_op jit(solution)/shard_map/ppermute | solution.py:222
  219.0 2.6 %collective-permute-start.17 = (bf16[40,512]{1,0:T(8,128)(2,1)S(1)}, bf16[40,512]{1,0:T(8,128)(2,1)S(1)}, u32[]{:S(2)}, u32[]{:S(2)}) collective-permute-start(bf16[40,512]{1,0:T(8,128)(2,1)S(1)} %get-tuple-element.54), channel_id=1, source_target_pairs={{44,0},{48,4},{52,8},{56,12},{60,16},{0,20},{4,24},{8,28},{12,32},... | collective-permute-start | bytes 122888 | tf_op jit(solution)/shard_map/ppermute | solution.py:222
  221.6 9.3 %collective-permute-start.18 = (bf16[40,512]{1,0:T(8,128)(2,1)S(1)}, bf16[40,512]{1,0:T(8,128)(2,1)S(1)}, u32[]{:S(2)}, u32[]{:S(2)}) collective-permute-start(bf16[40,512]{1,0:T(8,128)(2,1)S(1)} %get-tuple-element.55), channel_id=1, source_target_pairs={{20,0},{24,4},{28,8},{32,12},{36,16},{40,20},{44,24},{48,28},{52,3... | collective-permute-start | bytes 122888 | tf_op jit(solution)/shard_map/ppermute | solution.py:222
  (74 shorter events, 51.0 us)
Async XLA Ops:
  7.6 60.6 %collective-permute-start.7 = (bf16[512,1536]{1,0:T(8,128)(2,1)S(1)}, bf16[512,1536]{1,0:T(8,128)(2,1)S(1)}, u32[]{:S(2)}, u32[]{:S(2)}) collective-permute-start(bf16[512,1536]{1,0:T(8,128)(2,1)S(1)} %get-tuple-element.37.w), channel_id=1, source_target_pairs={{0,1},{1,0},{2,3},{3,2},{4,5},{5,4},{6,7},{7,6},{8,9},{9,8},{10,11... | collective-permute-start | bytes 4718600 | tf_op jit(solution)/shard_map/ppermute | solution.py:230
  11.1 22.1 %collective-permute-start = (bf16[40,1024]{1,0:T(8,128)(2,1)S(1)}, bf16[40,1024]{1,0:T(8,128)(2,1)S(1)}, u32[]{:S(2)}, u32[]{:S(2)}) collective-permute-start(bf16[40,1024]{1,0:T(8,128)(2,1)S(1)} %get-tuple-element.36), channel_id=1, source_target_pairs={{20,0},{24,4},{28,8},{32,12},{36,16},{40,20},{44,24},{48,28},{52,3... | collective-permute-start | bytes 245768 | tf_op jit(solution)/shard_map/ppermute | solution.py:222
  25.5 17.9 %collective-permute-start.1 = (bf16[40,1024]{1,0:T(8,128)(2,1)S(1)}, bf16[40,1024]{1,0:T(8,128)(2,1)S(1)}, u32[]{:S(2)}, u32[]{:S(2)}) collective-permute-start(bf16[40,1024]{1,0:T(8,128)(2,1)S(1)} %get-tuple-element.36), channel_id=1, source_target_pairs={{44,0},{48,4},{52,8},{56,12},{60,16},{0,20},{4,24},{8,28},{12,32},... | collective-permute-start | bytes 245768 | tf_op jit(solution)/shard_map/ppermute | solution.py:222
  43.3 12.6 %collective-permute-start.2 = (bf16[120,1024]{1,0:T(8,128)(2,1)S(1)}, bf16[120,1024]{1,0:T(8,128)(2,1)S(1)}, u32[]{:S(2)}, u32[]{:S(2)}) collective-permute-start(bf16[120,1024]{1,0:T(8,128)(2,1)S(1)} %get-tuple-element.67), channel_id=1, source_target_pairs={{4,0},{8,4},{12,8},{16,12},{20,16},{24,20},{28,24},{32,28},{36,32}... | collective-permute-start | bytes 737288 | tf_op jit(solution)/shard_map/ppermute | solution.py:222
  45.7 13.3 %collective-permute-start.3 = (bf16[120,1024]{1,0:T(8,128)(2,1)S(1)}, bf16[120,1024]{1,0:T(8,128)(2,1)S(1)}, u32[]{:S(2)}, u32[]{:S(2)}) collective-permute-start(bf16[120,1024]{1,0:T(8,128)(2,1)S(1)} %get-tuple-element.67), channel_id=1, source_target_pairs={{60,0},{0,4},{4,8},{8,12},{12,16},{16,20},{20,24},{24,28},{28,32},... | collective-permute-start | bytes 737288 | tf_op jit(solution)/shard_map/ppermute | solution.py:222
  49.2 9.9 %collective-permute-start.4 = (bf16[120,1024]{1,0:T(8,128)(2,1)S(1)}, bf16[120,1024]{1,0:T(8,128)(2,1)S(1)}, u32[]{:S(2)}, u32[]{:S(2)}) collective-permute-start(bf16[120,1024]{1,0:T(8,128)(2,1)S(1)} %get-tuple-element.67), channel_id=1, source_target_pairs={{8,0},{12,4},{16,8},{20,12},{24,16},{28,20},{32,24},{36,28},{40,32... | collective-permute-start | bytes 737288 | tf_op jit(solution)/shard_map/ppermute | solution.py:222
  51.4 15.3 %collective-permute-start.5 = (bf16[120,1024]{1,0:T(8,128)(2,1)S(1)}, bf16[120,1024]{1,0:T(8,128)(2,1)S(1)}, u32[]{:S(2)}, u32[]{:S(2)}) collective-permute-start(bf16[120,1024]{1,0:T(8,128)(2,1)S(1)} %get-tuple-element.67), channel_id=1, source_target_pairs={{56,0},{60,4},{0,8},{4,12},{8,16},{12,20},{16,24},{20,28},{24,32},... | collective-permute-start | bytes 737288 | tf_op jit(solution)/shard_map/ppermute | solution.py:222
  56.0 12.2 %collective-permute-start.6 = (bf16[40,1024]{1,0:T(8,128)(2,1)S(1)}, bf16[40,1024]{1,0:T(8,128)(2,1)S(1)}, u32[]{:S(2)}, u32[]{:S(2)}) collective-permute-start(bf16[40,1024]{1,0:T(8,128)(2,1)S(1)} %collective-permute-done), channel_id=1, source_target_pairs={{12,0},{16,4},{20,8},{24,12},{28,16},{32,20},{36,24},{40,28},{44,3... | collective-permute-start | bytes 245768 | tf_op jit(solution)/shard_map/ppermute | solution.py:222
  70.1 22.1 %copy-start.1 = (bf16[320,1024]{1,0:T(8,128)(2,1)}, bf16[320,1024]{1,0:T(8,128)(2,1)S(1)}, u32[]{:S(2)}) copy-start(bf16[320,1024]{1,0:T(8,128)(2,1)S(1)} %get-tuple-element.39.near) | copy-start | bytes 1966084
  70.1 14.5 %collective-permute-start.8 = (bf16[320,1024]{1,0:T(8,128)(2,1)S(1)}, bf16[320,1024]{1,0:T(8,128)(2,1)S(1)}, u32[]{:S(2)}, u32[]{:S(2)}) collective-permute-start(bf16[320,1024]{1,0:T(8,128)(2,1)S(1)} %get-tuple-element.40), channel_id=1, source_target_pairs={{1,2},{2,1},{3,0},{0,3},{5,6},{6,5},{7,4},{4,7},{9,10},{10,9},{11,... | collective-permute-start | bytes 1966088 | tf_op jit(solution)/shard_map/ppermute | solution.py:234
  86.3 5.9 %collective-permute-start.9 = (bf16[320,3072]{1,0:T(8,128)(2,1)S(1)}, bf16[320,3072]{1,0:T(8,128)(2,1)S(1)}, u32[]{:S(2)}, u32[]{:S(2)}) collective-permute-start(bf16[320,3072]{1,0:T(8,128)(2,1)S(1)} %shard_map.112), channel_id=1, source_target_pairs={{0,64},{64,0},{1,65},{65,1},{2,66},{66,2},{3,67},{67,3},{4,68},{68... | collective-permute-start | bytes 5898248 | tf_op jit(solution)/shard_map/ppermute | solution.py:226
  95.2 28.4 %all-to-all-start = ((bf16[4,80,3072]{2,1,0:T(8,128)(2,1)}), bf16[4,80,3072]{2,1,0:T(8,128)(2,1)}, u32[]{:S(2)}, u32[]{:S(2)}) async-start(bf16[4,80,3072]{2,1,0:T(8,128)(2,1)} %bitcast.21), calls=%async_computation | async-start | bytes 3932160 | tf_op jit(solution)/shard_map/all_to_all | solution.py:238
  146.8 20.3 %collective-permute-start.10 = (bf16[320,2176]{1,0:T(8,128)(2,1)S(1)}, bf16[320,2176]{1,0:T(8,128)(2,1)S(1)}, u32[]{:S(2)}, u32[]{:S(2)}) collective-permute-start(bf16[320,2176]{1,0:T(8,128)(2,1)S(1)} %bitcast.22), channel_id=1, source_target_pairs={{0,64},{64,0},{1,65},{65,1},{2,66},{66,2},{3,67},{67,3},{4,68},{68... | collective-permute-start | bytes 4177928 | tf_op jit(solution)/shard_map/ppermute | solution.py:226
  163.0 4.0 %collective-permute-start.19 = (bf16[320,1024]{1,0:T(8,128)(2,1)S(1)}, bf16[320,1024]{1,0:T(8,128)(2,1)S(1)}, u32[]{:S(2)}, u32[]{:S(2)}) collective-permute-start(bf16[320,1024]{1,0:T(8,128)(2,1)S(1)} %bitcast.25), channel_id=1, source_target_pairs={{0,64},{64,0},{1,65},{65,1},{2,66},{66,2},{3,67},{67,3},{4,68},{68... | collective-permute-start | bytes 1966088 | tf_op jit(solution)/shard_map/ppermute | solution.py:226
  171.1 62.2 %collective-permute-start.20 = (bf16[448,1536]{1,0:T(8,128)(2,1)S(1)}, bf16[448,1536]{1,0:T(8,128)(2,1)S(1)}, u32[]{:S(2)}, u32[]{:S(2)}) collective-permute-start(bf16[448,1536]{1,0:T(8,128)(2,1)S(1)} %get-tuple-element.57), channel_id=1, source_target_pairs={{0,1},{1,0},{2,3},{3,2},{4,5},{5,4},{6,7},{7,6},{8,9},{9,8},{10,11... | collective-permute-start | bytes 4128776 | tf_op jit(solution)/shard_map/ppermute | solution.py:230
  176.6 56.7 %copy-start.12 = (s32[40,8]{0,1:T(8,128)S(1)}, s32[40,8]{0,1:T(8,128)}, u32[]{:S(2)}) copy-start(s32[40,8]{0,1:T(8,128)} %param.9) | copy-start | bytes 3844
  176.6 12.9 %collective-permute-start.11 = (bf16[320,512]{1,0:T(8,128)(2,1)S(1)}, bf16[320,512]{1,0:T(8,128)(2,1)S(1)}, u32[]{:S(2)}, u32[]{:S(2)}) collective-permute-start(bf16[320,512]{1,0:T(8,128)(2,1)S(1)} %get-tuple-element.46), channel_id=1, source_target_pairs={{1,2},{2,1},{3,0},{0,3},{5,6},{6,5},{7,4},{4,7},{9,10},{10,9},{11,... | collective-permute-start | bytes 983048 | tf_op jit(solution)/shard_map/ppermute | solution.py:234
  190.9 18.4 %collective-permute-start.16 = (bf16[40,512]{1,0:T(8,128)(2,1)S(1)}, bf16[40,512]{1,0:T(8,128)(2,1)S(1)}, u32[]{:S(2)}, u32[]{:S(2)}) collective-permute-start(bf16[40,512]{1,0:T(8,128)(2,1)S(1)} %get-tuple-element.52), channel_id=1, source_target_pairs={{52,0},{56,4},{60,8},{0,12},{4,16},{8,20},{12,24},{16,28},{20,32},... | collective-permute-start | bytes 122888 | tf_op jit(solution)/shard_map/ppermute | solution.py:222
  200.3 15.1 %collective-permute-start.12 = (bf16[120,512]{1,0:T(8,128)(2,1)S(1)}, bf16[120,512]{1,0:T(8,128)(2,1)S(1)}, u32[]{:S(2)}, u32[]{:S(2)}) collective-permute-start(bf16[120,512]{1,0:T(8,128)(2,1)S(1)} %get-tuple-element.48), channel_id=1, source_target_pairs={{60,0},{0,4},{4,8},{8,12},{12,16},{16,20},{20,24},{24,28},{28,32},... | collective-permute-start | bytes 368648 | tf_op jit(solution)/shard_map/ppermute | solution.py:222
  202.3 13.1 %collective-permute-start.13 = (bf16[120,512]{1,0:T(8,128)(2,1)S(1)}, bf16[120,512]{1,0:T(8,128)(2,1)S(1)}, u32[]{:S(2)}, u32[]{:S(2)}) collective-permute-start(bf16[120,512]{1,0:T(8,128)(2,1)S(1)} %get-tuple-element.49), channel_id=1, source_target_pairs={{4,0},{8,4},{12,8},{16,12},{20,16},{24,20},{28,24},{32,28},{36,32}... | collective-permute-start | bytes 368648 | tf_op jit(solution)/shard_map/ppermute | solution.py:222
  207.4 10.3 %collective-permute-start.14 = (bf16[120,512]{1,0:T(8,128)(2,1)S(1)}, bf16[120,512]{1,0:T(8,128)(2,1)S(1)}, u32[]{:S(2)}, u32[]{:S(2)}) collective-permute-start(bf16[120,512]{1,0:T(8,128)(2,1)S(1)} %get-tuple-element.50), channel_id=1, source_target_pairs={{56,0},{60,4},{0,8},{4,12},{8,16},{12,20},{16,24},{20,28},{24,32},... | collective-permute-start | bytes 368648 | tf_op jit(solution)/shard_map/ppermute | solution.py:222
  209.3 9.0 %collective-permute-start.15 = (bf16[120,512]{1,0:T(8,128)(2,1)S(1)}, bf16[120,512]{1,0:T(8,128)(2,1)S(1)}, u32[]{:S(2)}, u32[]{:S(2)}) collective-permute-start(bf16[120,512]{1,0:T(8,128)(2,1)S(1)} %get-tuple-element.51), channel_id=1, source_target_pairs={{8,0},{12,4},{16,8},{20,12},{24,16},{28,20},{32,24},{36,28},{40,32... | collective-permute-start | bytes 368648 | tf_op jit(solution)/shard_map/ppermute | solution.py:222
  219.0 12.0 %collective-permute-start.17 = (bf16[40,512]{1,0:T(8,128)(2,1)S(1)}, bf16[40,512]{1,0:T(8,128)(2,1)S(1)}, u32[]{:S(2)}, u32[]{:S(2)}) collective-permute-start(bf16[40,512]{1,0:T(8,128)(2,1)S(1)} %get-tuple-element.54), channel_id=1, source_target_pairs={{44,0},{48,4},{52,8},{56,12},{60,16},{0,20},{4,24},{8,28},{12,32},... | collective-permute-start | bytes 122888 | tf_op jit(solution)/shard_map/ppermute | solution.py:222
  221.6 11.7 %collective-permute-start.18 = (bf16[40,512]{1,0:T(8,128)(2,1)S(1)}, bf16[40,512]{1,0:T(8,128)(2,1)S(1)}, u32[]{:S(2)}, u32[]{:S(2)}) collective-permute-start(bf16[40,512]{1,0:T(8,128)(2,1)S(1)} %get-tuple-element.55), channel_id=1, source_target_pairs={{20,0},{24,4},{28,8},{32,12},{36,16},{40,20},{44,24},{48,28},{52,3... | collective-permute-start | bytes 122888 | tf_op jit(solution)/shard_map/ppermute | solution.py:222
  (12 other events, 57.3 us)

commit v3 on v2

--- a/solution.py
+++ b/solution.py
@@ -27,17 +27,21 @@
 FIRST = ((0,), (0,))
 
 
-def call(body, outs, *args, scratch=(), flops=0):
+def call(body, outs, *args, flops=0, own_copies=False):
     moved = sum(a.size * a.dtype.itemsize for a in args[1:])
-    specs = [pl.BlockSpec(memory_space=pltpu.SMEM)]
-    specs += [pl.BlockSpec(memory_space=pltpu.VMEM)] * (len(args) - 1)
+
+    def whole(shape):
+        if own_copies:
+            return pl.BlockSpec(shape, lambda i: (0,) * len(shape))
+        return pl.BlockSpec(memory_space=pltpu.VMEM)
+
     return pl.pallas_call(
         body,
+        grid=(1,) if own_copies else (),
         out_shape=[jax.ShapeDtypeStruct(s, d) for s, d in outs],
-        in_specs=specs,
-        out_specs=[pl.BlockSpec(memory_space=pltpu.VMEM)] * len(outs),
-        scratch_shapes=list(scratch),
-        compiler_params=pltpu.CompilerParams(vmem_limit_bytes=24 << 20),
+        in_specs=[pl.BlockSpec(memory_space=pltpu.SMEM)] + [whole(a.shape) for a in args[1:]],
+        out_specs=[whole(shape) for shape, _ in outs],
+        compiler_params=pltpu.CompilerParams(vmem_limit_bytes=(52 if own_copies else 24) << 20),
         cost_estimate=pl.CostEstimate(flops=flops, bytes_accessed=moved, transcendentals=0),
     )(*args)
 
@@ -46,7 +50,7 @@
     return lax.broadcasted_iota(I32, shape, axis)
 
 
-def pack(sc, tok, cot, ids, wts, gate, up, down, out, w):
+def pack(sc, tok, cot, ids, wts, out):
     wts_f = wts[...].astype(F32)
     named = jnp.zeros((EXP, TOK), F32)
     weight = jnp.zeros((EXP, TOK), F32)
@@ -64,6 +68,9 @@
     out[:, 384:512] = jnp.where(low, out[:, 384:512], meta)
     out[:, 512 : 512 + FEAT] = cot[...]
     out[:, 896:1024] = jnp.where(low, out[:, 896:1024], jnp.zeros((TOK, 128), BF))
+
+
+def pack_weights(sc, gate, up, down, w):
     w[0:FEAT, 0:512] = gate[...]
     w[0:FEAT, 512:1024] = up[...]
     w[0:FEAT, 1024:1536] = down[...]
@@ -88,25 +95,26 @@
         out[...] = dot(one_hot, every[...]).astype(BF)
 
 
-def products(a, b, w, wf, lo):
-    x = jnp.concatenate([a[lo : lo + PART, 0:512], b[lo : lo + PART, 0:512]], 0)
-    dy = jnp.concatenate([a[lo : lo + PART, 512:1024], b[lo : lo + PART, 512:1024]], 0)
+def products(rows, w, wf, lo):
+    x, dy = rows[lo : lo + PART, 0:512], rows[lo : lo + PART, 512:1024]
     for h, ref in ((0, w), (1, wf)):
         for c, left in ((0, x), (1, x), (2, dy)):
             yield 1536 * h + 512 * c, dot(left, ref[:, 512 * c : 512 * c + 512])
 
 
-def forward_others(sc, near, far, w, wf, out):
-    for at, value in products(near, far, w, wf, PART):
+def forward_others(sc, rows, w, wf, out):
+    for at, value in products(rows, w, wf, PART):
         out[:, at : at + 512] = value.astype(BF)
 
 
-def forward_mine(sc, near, far, w, wf, got, out):
-    for at, value in products(near, far, w, wf, 0):
-        out[:, at : at + 512] = (value + got[:, at : at + 512].astype(F32)).astype(BF)
-
-
-def activate(sc, pieces, near_tile, far_tile, g_out, s_out):
+def forward_mine(sc, near, far, w, wf, got_near, got_far, out):
+    for lo, rows, got in ((0, near, got_near), (PART, far, got_far)):
+        for at, value in products(rows, w, wf, 0):
+            total = value + got[:, at : at + 512].astype(F32)
+            out[lo : lo + PART, at : at + 512] = total.astype(BF)
+
+
+def activate(sc, pieces, near_tile, far_tile, g_out):
     q = ROWS // 4
     start = pl.multiple_of((sc[3] % 2) * q, 16)
     a = near_tile[pl.ds(start, q), :].astype(F32)
@@ -134,42 +142,40 @@
         for k in range(4):
             g_out[k, :, 1024 * h : 1024 * h + 512] = gate_g
             g_out[k, :, 1024 * h + 512 : 1024 * h + 1024] = up_g
-            s_out[k, :, 512 * h : 512 * h + 512] = scaled
+            g_out[k, :, 2176 + 512 * h : 2688 + 512 * h] = scaled
     dot_tile = jnp.where(lane == 0, dots, 0.0).astype(BF)
     for k in range(4):
         g_out[k, :, 2048:2176] = dot_tile
 
 
-def backward(sc, g, go, w, wf, keep, send):
-    put = (iota((128, WIDE), 0) == 0) & (iota((128, WIDE), 1) == FEAT + sc[0])
-    put = put.astype(BF)
-    for lo, out in ((PART, send), (0, keep)):
+def backward(lo):
+    def body(sc, g, go, w, wf, out):
+        put = (iota((128, WIDE), 0) == 0) & (iota((128, WIDE), 1) == FEAT + sc[0])
+        put = put.astype(BF)
         for at, ref in ((0, g), (PART, go)):
             t = dot(ref[lo : lo + PART, 0:1024], w[:, 0:1024], LAST)
             t += dot(ref[lo : lo + PART, 1024:2048], wf[:, 0:1024], LAST)
             t += dot(ref[lo : lo + PART, 2048:2176], put)
             out[at : at + PART, :] = t.astype(BF)
 
-
-def weight_grads(sc, near, far, g, go, s, so, mine, partner):
+    return body
+
+
+def weight_grads(sc, near, far, g, go, mine, partner):
     for c in range(3):
         at = 0 if c < 2 else 512
-        total = [None, None]
-        for rows, lo, right, right_s in (
-            (near, 0, g, s),
-            (far, 0, g, s),
-            (near, PART, go, so),
-            (far, PART, go, so),
-        ):
-            at_r = 0 if rows is near else PART
-            left = rows[lo : lo + PART, at : at + 512]
-            for h in range(2):
-                r = right if c < 2 else right_s
-                col = 1024 * h + 512 * c if c < 2 else 512 * h
-                t = dot(left, r[at_r : at_r + PART, col : col + 512], FIRST)
-                total[h] = t if total[h] is None else total[h] + t
-        mine[:, 512 * c : 512 * c + 512] = total[0][:FEAT]
-        partner[:, 512 * c : 512 * c + 512] = total[1][:FEAT].astype(BF)
+        for h in range(2):
+            col = 1024 * h + 512 * c if c < 2 else 2176 + 512 * h
+            cols = slice(col, col + 512)
+            t = dot(near[0:PART, at : at + 512], g[0:PART, cols], FIRST)
+            t += dot(far[0:PART, at : at + 512], g[PART:ROWS, cols], FIRST)
+            t += dot(near[PART:ROWS, at : at + 512], go[0:PART, cols], FIRST)
+            t += dot(far[PART:ROWS, at : at + 512], go[PART:ROWS, cols], FIRST)
+            out = slice(512 * c, 512 * c + 512)
+            if h == 0:
+                mine[:, out] = t[:FEAT]
+            else:
+                partner[:, out] = t[:FEAT].astype(BF)
 
 
 def scatter(sc, tile, own, oth, *outs):
@@ -206,9 +212,12 @@
     tok[...] = total[:, :FEAT].astype(BF)
     sel = (iota((EXP, 128), 0) + 64 == iota((EXP, 128), 1)).astype(BF)
     dots = dot(sel, total[:, 384:512].astype(BF), LAST)
+    out = jnp.zeros((8, TOK), F32)
     for k in range(8):
         match = iota((EXP, TOK), 0) == ids[k : k + 1, :]
-        route[k : k + 1, :] = jnp.sum(jnp.where(match, dots, 0.0), axis=0, keepdims=True)
+        row = jnp.sum(jnp.where(match, dots, 0.0), axis=0, keepdims=True)
+        out += jnp.where(iota((8, TOK), 0) == k, row, 0.0)
+    route[...] = out.astype(BF)
 
 
 def finish_weights(sc, mine, got, gate, up, down):
@@ -244,12 +253,13 @@
     z = lax.axis_index("z")
     sc = jnp.stack([2 * z + high, 2 * z + 1 - high, core, lax.axis_index("x")]).astype(I32)
     ids_t = expert_ids.T
-    payload, w = call(
-        pack,
-        [((TOK, 1024), BF), ((WIDE, 1536), BF)],
-        sc, tokens, cotangent, ids_t, route_weight.T,
-        gate_weight[0], up_weight[0], down_weight[0].T,
-    )
+    (payload,) = call(
+        pack, [((TOK, 1024), BF)], sc, tokens, cotangent, ids_t, route_weight.T, own_copies=True
+    )
+    payload, gate_m, up_m, down_m = lax.optimization_barrier(
+        (payload, gate_weight[0], up_weight[0], down_weight[0].T)
+    )
+    (w,) = call(pack_weights, [((WIDE, 1536), BF)], sc, gate_m, up_m, down_m, own_copies=True)
     five = take(payload, "z", 5)
     minus = take(payload, "z", -5)
     group = jnp.concatenate([five, payload, minus], 0)
@@ -257,53 +267,53 @@
     eight = take(five, "z", 3)
     w_far = swap_half(w)
     every = jnp.concatenate([group] + near_z + [eight], 0)
-    every, w_far = lax.optimization_barrier((every, w_far))
     near, send = call(
-        choose, [((ROWS, 1024), BF)] * 2, sc, every, flops=4 * ROWS * ALL * 1024
+        choose, [((ROWS, 1024), BF)] * 2, sc, every, flops=0
     )
     far = swap_expert(send)
-    flops = 2 * ROWS * WIDE * 3072
-    others = call(
-        forward_others, [((ROWS, 3072), BF)], sc, near, far, w, w_far, flops=flops
-    )[0]
-    pair = call(
-        forward_mine, [((ROWS, 3072), BF)], sc, near, far, w, w_far, swap_core(others), flops=flops
-    )[0]
+    flops = 2 * PART * WIDE * 3072
+    out = [((PART, 3072), BF)]
+    (near_others,) = call(forward_others, out, sc, near, w, w_far, flops=flops)
+    (far_others,) = call(forward_others, out, sc, far, w, w_far, flops=flops)
+    (pair,) = call(
+        forward_mine, [((ROWS, 3072), BF)],
+        sc, near, far, w, w_far, swap_core(near_others), swap_core(far_others), flops=2 * flops,
+    )
     q = ROWS // 4
     pieces = trade(pair.reshape(4, q, 3072), "x")
-    g_out, s_out = call(
-        activate, [((4, q, 2176), BF), ((4, q, 1024), BF)],
-        sc, pieces, near[:PART, 384:512], far[:PART, 384:512],
-    )
-    g = trade(g_out, "x")
-    s_out, g = lax.optimization_barrier((s_out, g))
-    s = trade(s_out, "x").reshape(ROWS, 1024)
-    g = g.reshape(ROWS, 2176)
+    (g_out,) = call(
+        activate, [((4, q, 3200), BF)], sc, pieces, near[:PART, 384:512], far[:PART, 384:512]
+    )
+    g = trade(g_out, "x").reshape(ROWS, 3200)
     g_far = swap_core(g)
-    keep, away = call(backward, [((ROWS, WIDE), BF)] * 2, sc, g, g_far, w, w_far)
+    (away,) = call(backward(PART), [((ROWS, WIDE), BF)], sc, g, g_far, w, w_far)
     back = swap_expert(away)
-    s_far = swap_core(s)
+    near_w, far_w, g, _ = lax.optimization_barrier((near, far, g, away))
+    (keep,) = call(backward(0), [((ROWS, WIDE), BF)], sc, g, g_far, w, w_far)
     mine_w, partner_w = call(
         weight_grads, [((FEAT, 1536), F32), ((FEAT, 1536), BF)],
-        sc, near, far, g, g_far, s, s_far, flops=8 * ROWS * WIDE * 1536,
+        sc, near_w, far_w, g, g_far, flops=8 * ROWS * WIDE * 1536,
     )
     got_w = swap_half(partner_w)
     sums = call(
         scatter, [((3 * TOK, WIDE), BF)] * 5 + [((TOK, WIDE), BF)],
-        sc, every[:, 384:512], keep, back, flops=2 * ALL * ALL * WIDE,
+        sc, every[:, 384:512], keep, back, flops=30 * 10**9,
     )
     moved = [take(a, "z", -step) for a, step in zip(sums[1:5], (1, -1, 2, -2))]
     moved.append(take(sums[5], "z", -3))
     first, mid, last = call(
         add_near, [((TOK, WIDE), BF), ((TOK, WIDE), F32), ((TOK, WIDE), BF)], sc, sums[0], *moved
     )
+    got_w, mid = lax.optimization_barrier((got_w, mid))
+    gate, up, down = call(finish_weights, [((FEAT, 512), BF)] * 3, sc, mine_w, got_w)
     from_first, from_last = take(first, "z", -5), take(last, "z", 5)
-    from_first, from_last, got_w = lax.optimization_barrier((from_first, from_last, got_w))
+    from_first, from_last, gate, up, down = lax.optimization_barrier(
+        (from_first, from_last, gate, up, down)
+    )
     tok, route = call(
-        finish_tokens, [((TOK, FEAT), BF), ((8, TOK), F32)], sc, mid, from_first, from_last, ids_t
-    )
-    gate, up, down = call(finish_weights, [((FEAT, 512), BF)] * 3, sc, mine_w, got_w)
-    return (tok, route.astype(BF).T, gate[None], up[None], down.T[None])
+        finish_tokens, [((TOK, FEAT), BF), ((8, TOK), BF)], sc, mid, from_first, from_last, ids_t
+    )
+    return (tok, route.T, gate[None], up[None], down.T[None])
 
 
 def solution(mesh):

time: 240 us -> 216 us (0.900)
  waiting for transfers between devices: 76.4 us -> 56.2 us
  blocking collectives: 35.2 us -> 28 us
  Pallas kernels: 21 us -> 24.5 us
    ppermute x2, waiting for transfers between devices: 18.1 us -> 6.52 us  [swap_expert(): return lax.ppermute(a, 'y', [(1, 2), (2, 1), (3, 0), (0, 3)])]
    ppermute x14, waiting for transfers between devices: 30.3 us -> 21.1 us  [take(): return lax.ppermute(a, axis, [((i + step) % n, i) for i in range(n)])]
    all_to_all x2 -> x1, blocking collectives: 35.2 us -> 28 us  [trade(): return lax.all_to_all(a, axis, split_axis=0, concat_axis=0, tiled=True)]
    pallas_call x11 -> x14, Pallas kernels: 21 us -> 24.5 us  [call(): pl.pallas_call(body, grid=(1,) if own_copies else (), out_shape=[jax.Shap...]
    unnamed x34 -> x36, local copies, waits for them, and re-layouts: 7.38 us -> 7.35 us
  transfers between devices with their start and end apart: 22 -> 22, of which waited for: 13 -> 10; matrix products, arithmetic and copies ran while one was open for 1% -> 1% of each run, Pallas kernels for 2% -> 8%
where the time goes in v3:
time: 216 us; the launch traced here: 214 us
  starting transfers between devices  94 us (44%)
  waiting for transfers between devices  56.2 us (26%)
  blocking collectives  28 us (13%)
  Pallas kernels  24.5 us (11%)
  local copies, waits for them, and re-layouts  9.86 us (5%)
    ppermute x14, starting transfers between devices, take(): return lax.ppermute(a, axis, [((i + step) % n, i) for i in range(n)])  68.1 us
    all_to_all x1, blocking collectives, trade(): return lax.all_to_all(a, axis, split_axis=0, concat_axis=0, tiled=True)  28 us
    pallas_call x14, Pallas kernels, call(): pl.pallas_call(body, grid=(1,) if own_copies else (), out_shape=[jax.Shap...  24.5 us
    all_to_all x1, waiting for transfers between devices, trade(): return lax.all_to_all(a, axis, split_axis=0, concat_axis=0, tiled=True)  22 us
    ppermute x14, waiting for transfers between devices, take(): return lax.ppermute(a, axis, [((i + step) % n, i) for i in range(n)])  21.1 us
    ppermute x2, starting transfers between devices, swap_expert(): return lax.ppermute(a, 'y', [(1, 2), (2, 1), (3, 0), (0, 3)])  9.79 us
    unnamed x36, local copies, waits for them, and re-layouts  7.35 us
    ppermute x3, waiting for transfers between devices, swap_core(): return lax.ppermute(a, 'core', [(0, 1), (1, 0)])  6.58 us
  transfers between devices with their start and end apart: 22, of which 10 were waited for; matrix products, arithmetic and copies ran while one was open for 1% of the time, Pallas kernels for 8%

profile of v3, /device:TPU:6, one launch (start us, length us, event | category | flops | bytes accessed | tf_op | source)
XLA Modules:
  0.0 213.8 jit_solution(4427371039455114457)
XLA Ops:
  4.5 14.4 %collective-permute-start = (bf16[40,1024]{1,0:T(8,128)(2,1)S(1)}, bf16[40,1024]{1,0:T(8,128)(2,1)S(1)}, u32[]{:S(2)}, u32[]{:S(2)}) collective-permute-start(bf16[40,1024]{1,0:T(8,128)(2,1)S(1)} %shard_map.110), channel_id=1, source_target_pairs={{20,0},{24,4},{28,8},{32,12},{36,16},{40,20},{44,24},{48,28},{52,3... | collective-permute-start | bytes 245768 | tf_op jit(solution)/shard_map/ppermute | solution.py:231
  25.7 3.5 %collective-permute-start.8 = (bf16[512,1536]{1,0:T(8,128)(2,1)}, bf16[512,1536]{1,0:T(8,128)(2,1)S(1)}, u32[]{:S(2)}, u32[]{:S(2)}) collective-permute-start(bf16[512,1536]{1,0:T(8,128)(2,1)} %shard_map.112.w), channel_id=1, source_target_pairs={{0,1},{1,0},{2,3},{3,2},{4,5},{5,4},{6,7},{7,6},{8,9},{9,8},{10,11... | collective-permute-start | bytes 4718600 | tf_op jit(solution)/shard_map/ppermute | solution.py:239
  29.3 7.8 %collective-permute-done.1 = bf16[40,1024]{1,0:T(8,128)(2,1)S(1)} collective-permute-done((bf16[40,1024]{1,0:T(8,128)(2,1)S(1)}, bf16[40,1024]{1,0:T(8,128)(2,1)S(1)}, u32[]{:S(2)}, u32[]{:S(2)}) %collective-permute-start.1) | collective-permute-done | bytes 81952 | tf_op jit(solution)/shard_map/ppermute | solution.py:231
  37.1 2.4 %collective-permute-start.2 = (bf16[120,1024]{1,0:T(8,128)(2,1)S(1)}, bf16[120,1024]{1,0:T(8,128)(2,1)S(1)}, u32[]{:S(2)}, u32[]{:S(2)}) collective-permute-start(bf16[120,1024]{1,0:T(8,128)(2,1)S(1)} %get-tuple-element.69), channel_id=1, source_target_pairs={{4,0},{8,4},{12,8},{16,12},{20,16},{24,20},{28,24},{32,28},{36,32}... | collective-permute-start | bytes 737288 | tf_op jit(solution)/shard_map/ppermute | solution.py:231
  39.5 3.4 %collective-permute-start.3 = (bf16[120,1024]{1,0:T(8,128)(2,1)S(1)}, bf16[120,1024]{1,0:T(8,128)(2,1)S(1)}, u32[]{:S(2)}, u32[]{:S(2)}) collective-permute-start(bf16[120,1024]{1,0:T(8,128)(2,1)S(1)} %get-tuple-element.69), channel_id=1, source_target_pairs={{60,0},{0,4},{4,8},{8,12},{12,16},{16,20},{20,24},{24,28},{28,32},... | collective-permute-start | bytes 737288 | tf_op jit(solution)/shard_map/ppermute | solution.py:231
  42.9 2.2 %collective-permute-start.4 = (bf16[120,1024]{1,0:T(8,128)(2,1)S(1)}, bf16[120,1024]{1,0:T(8,128)(2,1)S(1)}, u32[]{:S(2)}, u32[]{:S(2)}) collective-permute-start(bf16[120,1024]{1,0:T(8,128)(2,1)S(1)} %get-tuple-element.69), channel_id=1, source_target_pairs={{8,0},{12,4},{16,8},{20,12},{24,16},{28,20},{32,24},{36,28},{40,32... | collective-permute-start | bytes 737288 | tf_op jit(solution)/shard_map/ppermute | solution.py:231
  45.2 4.5 %collective-permute-start.5 = (bf16[120,1024]{1,0:T(8,128)(2,1)S(1)}, bf16[120,1024]{1,0:T(8,128)(2,1)S(1)}, u32[]{:S(2)}, u32[]{:S(2)}) collective-permute-start(bf16[120,1024]{1,0:T(8,128)(2,1)S(1)} %get-tuple-element.69), channel_id=1, source_target_pairs={{56,0},{60,4},{0,8},{4,12},{8,16},{12,20},{16,24},{20,28},{24,32},... | collective-permute-start | bytes 737288 | tf_op jit(solution)/shard_map/ppermute | solution.py:231
  49.7 3.1 %collective-permute-start.6 = (bf16[40,1024]{1,0:T(8,128)(2,1)S(1)}, bf16[40,1024]{1,0:T(8,128)(2,1)S(1)}, u32[]{:S(2)}, u32[]{:S(2)}) collective-permute-start(bf16[40,1024]{1,0:T(8,128)(2,1)S(1)} %collective-permute-done), channel_id=1, source_target_pairs={{12,0},{16,4},{20,8},{24,12},{28,16},{32,20},{36,24},{40,28},{44,3... | collective-permute-start | bytes 245768 | tf_op jit(solution)/shard_map/ppermute | solution.py:231
  52.9 7.6 %collective-permute-done.5 = bf16[120,1024]{1,0:T(8,128)(2,1)S(1)} collective-permute-done((bf16[120,1024]{1,0:T(8,128)(2,1)S(1)}, bf16[120,1024]{1,0:T(8,128)(2,1)S(1)}, u32[]{:S(2)}, u32[]{:S(2)}) %collective-permute-start.5) | collective-permute-done | bytes 245792 | tf_op jit(solution)/shard_map/ppermute | solution.py:231
  63.8 4.9 %collective-permute-start.7 = (bf16[320,1024]{1,0:T(8,128)(2,1)S(1)}, bf16[320,1024]{1,0:T(8,128)(2,1)S(1)}, u32[]{:S(2)}, u32[]{:S(2)}) collective-permute-start(bf16[320,1024]{1,0:T(8,128)(2,1)S(1)} %get-tuple-element.39), channel_id=1, source_target_pairs={{1,2},{2,1},{3,0},{0,3},{5,6},{6,5},{7,4},{4,7},{9,10},{10,9},{11,... | collective-permute-start | bytes 1966088 | tf_op jit(solution)/shard_map/ppermute | solution.py:243
  71.9 6.5 %collective-permute-done.7.rows.far = bf16[320,1024]{1,0:T(8,128)(2,1)S(1)} collective-permute-done((bf16[320,1024]{1,0:T(8,128)(2,1)S(1)}, bf16[320,1024]{1,0:T(8,128)(2,1)S(1)}, u32[]{:S(2)}, u32[]{:S(2)}) %collective-permute-start.7) | collective-permute-done | bytes 655392 | tf_op jit(solution)/shard_map/ppermute | solution.py:243
  81.6 2.5 %collective-permute-done.10.got_far = bf16[160,3072]{1,0:T(8,128)(2,1)S(1)} collective-permute-done((bf16[160,3072]{1,0:T(8,128)(2,1)S(1)}, bf16[160,3072]{1,0:T(8,128)(2,1)S(1)}, u32[]{:S(2)}, u32[]{:S(2)}) %collective-permute-start.10) | collective-permute-done | bytes 983072 | tf_op jit(solution)/shard_map/ppermute | solution.py:235
  87.2 4.9 %all-to-all-start = ((bf16[4,80,3072]{2,1,0:T(8,128)(2,1)}), bf16[4,80,3072]{2,1,0:T(8,128)(2,1)}, u32[]{:S(2)}, u32[]{:S(2)}) async-start(bf16[4,80,3072]{2,1,0:T(8,128)(2,1)} %bitcast.23), calls=%async_computation | async-start | bytes 3932160 | tf_op jit(solution)/shard_map/all_to_all | solution.py:247
  93.6 22.0 %all-to-all-done.pieces = bf16[4,80,3072]{2,1,0:T(8,128)(2,1)} async-done(((bf16[4,80,3072]{2,1,0:T(8,128)(2,1)}), bf16[4,80,3072]{2,1,0:T(8,128)(2,1)}, u32[]{:S(2)}, u32[]{:S(2)}) %all-to-all-start) | async-done | bytes 1966112 | tf_op jit(solution)/shard_map/all_to_all | solution.py:247
  115.6 2.2 %shard_map.116 = bf16[4,80,3200]{2,1,0:T(8,128)(2,1)S(1)} custom-call(s32[4]{0:T(128)S(1)} %pad_add_fusion.sc, bf16[4,80,3072]{2,1,0:T(8,128)(2,1)} %all-to-all-done.pieces, bf16[160,128]{1,0:T(8,128)(2,1)S(1)} %slice.9.near_tile, bf16[160,128]{1,0:T(8,128)(2,1)S(1)} %slice.12.far_tile), custom_call_target="tpu_custom_call" | custom-call | bytes 2048000 | tf_op jit(solution)/shard_map/pallas_call | solution.py:38
  117.8 28.0 %all_to_all.10 = bf16[4,80,3200]{2,1,0:T(8,128)(2,1)S(1)} all-to-all(bf16[4,80,3200]{2,1,0:T(8,128)(2,1)S(1)} %shard_map.116), channel_id=1, replica_groups=mesh['x'=4,'core'=2,'z'=16,'y'=4] {'x'}, dimensions={0} | all-to-all | bytes 4096000 | tf_op jit(solution)/shard_map/all_to_all | solution.py:247
  147.8 4.1 %collective-permute-done.11.go = bf16[320,3200]{1,0:T(8,128)(2,1)S(1)} collective-permute-done((bf16[320,3200]{1,0:T(8,128)(2,1)S(1)}, bf16[320,3200]{1,0:T(8,128)(2,1)S(1)}, u32[]{:S(2)}, u32[]{:S(2)}) %collective-permute-start.11) | collective-permute-done | bytes 2048032 | tf_op jit(solution)/shard_map/ppermute | solution.py:235
  154.0 4.9 %collective-permute-start.13 = (bf16[320,512]{1,0:T(8,128)(2,1)S(1)}, bf16[320,512]{1,0:T(8,128)(2,1)S(1)}, u32[]{:S(2)}, u32[]{:S(2)}) collective-permute-start(bf16[320,512]{1,0:T(8,128)(2,1)S(1)} %shard_map.117), channel_id=1, source_target_pairs={{1,2},{2,1},{3,0},{0,3},{5,6},{6,5},{7,4},{4,7},{9,10},{10,9},{11,... | collective-permute-start | bytes 983048 | tf_op jit(solution)/shard_map/ppermute | solution.py:243
  159.9 4.1 %shard_map.118 = (f32[448,1536]{1,0:T(8,128)S(1)}, bf16[448,1536]{1,0:T(8,128)(2,1)S(1)}) custom-call(s32[4]{0:T(128)S(1)} %pad_add_fusion.sc, bf16[320,1024]{1,0:T(8,128)(2,1)S(1)} %copy-done.3, bf16[320,1024]{1,0:T(8,128)(2,1)S(1)} %copy-done.5, bf16[320,3200]{1,0:T(8,128)(2,1)S(1)} %bitcast.21, bf16[320,3200]{1,0:T(8,128)(2,1)S(1)} %collective-permute-done.11.go), custom_call_target="tpu_custom_call" | custom-call | flops 2013265920 | bytes 5406720 | tf_op jit(solution)/shard_map/pallas_call | solution.py:38
  169.5 9.3 %collective-permute-start.18 = (bf16[40,512]{1,0:T(8,128)(2,1)S(1)}, bf16[40,512]{1,0:T(8,128)(2,1)S(1)}, u32[]{:S(2)}, u32[]{:S(2)}) collective-permute-start(bf16[40,512]{1,0:T(8,128)(2,1)S(1)} %get-tuple-element.52), channel_id=1, source_target_pairs={{52,0},{56,4},{60,8},{0,12},{4,16},{8,20},{12,24},{16,28},{20,32},... | collective-permute-start | bytes 122888 | tf_op jit(solution)/shard_map/ppermute | solution.py:231
  180.7 5.1 %collective-permute-start.15 = (bf16[120,512]{1,0:T(8,128)(2,1)S(1)}, bf16[120,512]{1,0:T(8,128)(2,1)S(1)}, u32[]{:S(2)}, u32[]{:S(2)}) collective-permute-start(bf16[120,512]{1,0:T(8,128)(2,1)S(1)} %get-tuple-element.49), channel_id=1, source_target_pairs={{4,0},{8,4},{12,8},{16,12},{20,16},{24,20},{28,24},{32,28},{36,32}... | collective-permute-start | bytes 368648 | tf_op jit(solution)/shard_map/ppermute | solution.py:231
  187.8 6.0 %collective-permute-start.17 = (bf16[120,512]{1,0:T(8,128)(2,1)S(1)}, bf16[120,512]{1,0:T(8,128)(2,1)S(1)}, u32[]{:S(2)}, u32[]{:S(2)}) collective-permute-start(bf16[120,512]{1,0:T(8,128)(2,1)S(1)} %get-tuple-element.51), channel_id=1, source_target_pairs={{8,0},{12,4},{16,8},{20,12},{24,16},{28,20},{32,24},{36,28},{40,32... | collective-permute-start | bytes 368648 | tf_op jit(solution)/shard_map/ppermute | solution.py:231
  197.7 2.5 %collective-permute-start.19 = (bf16[40,512]{1,0:T(8,128)(2,1)S(1)}, bf16[40,512]{1,0:T(8,128)(2,1)S(1)}, u32[]{:S(2)}, u32[]{:S(2)}) collective-permute-start(bf16[40,512]{1,0:T(8,128)(2,1)S(1)} %get-tuple-element.55), channel_id=1, source_target_pairs={{44,0},{48,4},{52,8},{56,12},{60,16},{0,20},{4,24},{8,28},{12,32},... | collective-permute-start | bytes 122888 | tf_op jit(solution)/shard_map/ppermute | solution.py:231
  200.2 9.4 %collective-permute-start.20 = (bf16[40,512]{1,0:T(8,128)(2,1)S(1)}, bf16[40,512]{1,0:T(8,128)(2,1)S(1)}, u32[]{:S(2)}, u32[]{:S(2)}) collective-permute-start(bf16[40,512]{1,0:T(8,128)(2,1)S(1)} %get-tuple-element.56), channel_id=1, source_target_pairs={{20,0},{24,4},{28,8},{32,12},{36,16},{40,20},{44,24},{48,28},{52,3... | collective-permute-start | bytes 122888 | tf_op jit(solution)/shard_map/ppermute | solution.py:231
  (77 shorter events, 47.5 us)
Async XLA Ops:
  4.5 24.7 %collective-permute-start = (bf16[40,1024]{1,0:T(8,128)(2,1)S(1)}, bf16[40,1024]{1,0:T(8,128)(2,1)S(1)}, u32[]{:S(2)}, u32[]{:S(2)}) collective-permute-start(bf16[40,1024]{1,0:T(8,128)(2,1)S(1)} %shard_map.110), channel_id=1, source_target_pairs={{20,0},{24,4},{28,8},{32,12},{36,16},{40,20},{44,24},{48,28},{52,3... | collective-permute-start | bytes 245768 | tf_op jit(solution)/shard_map/ppermute | solution.py:231
  18.9 18.1 %collective-permute-start.1 = (bf16[40,1024]{1,0:T(8,128)(2,1)S(1)}, bf16[40,1024]{1,0:T(8,128)(2,1)S(1)}, u32[]{:S(2)}, u32[]{:S(2)}) collective-permute-start(bf16[40,1024]{1,0:T(8,128)(2,1)S(1)} %shard_map.110), channel_id=1, source_target_pairs={{44,0},{48,4},{52,8},{56,12},{60,16},{0,20},{4,24},{8,28},{12,32},... | collective-permute-start | bytes 245768 | tf_op jit(solution)/shard_map/ppermute | solution.py:231
  25.7 43.0 %collective-permute-start.8 = (bf16[512,1536]{1,0:T(8,128)(2,1)}, bf16[512,1536]{1,0:T(8,128)(2,1)S(1)}, u32[]{:S(2)}, u32[]{:S(2)}) collective-permute-start(bf16[512,1536]{1,0:T(8,128)(2,1)} %shard_map.112.w), channel_id=1, source_target_pairs={{0,1},{1,0},{2,3},{3,2},{4,5},{5,4},{6,7},{7,6},{8,9},{9,8},{10,11... | collective-permute-start | bytes 4718600 | tf_op jit(solution)/shard_map/ppermute | solution.py:239
  37.1 12.6 %collective-permute-start.2 = (bf16[120,1024]{1,0:T(8,128)(2,1)S(1)}, bf16[120,1024]{1,0:T(8,128)(2,1)S(1)}, u32[]{:S(2)}, u32[]{:S(2)}) collective-permute-start(bf16[120,1024]{1,0:T(8,128)(2,1)S(1)} %get-tuple-element.69), channel_id=1, source_target_pairs={{4,0},{8,4},{12,8},{16,12},{20,16},{24,20},{28,24},{32,28},{36,32}... | collective-permute-start | bytes 737288 | tf_op jit(solution)/shard_map/ppermute | solution.py:231
  39.5 13.3 %collective-permute-start.3 = (bf16[120,1024]{1,0:T(8,128)(2,1)S(1)}, bf16[120,1024]{1,0:T(8,128)(2,1)S(1)}, u32[]{:S(2)}, u32[]{:S(2)}) collective-permute-start(bf16[120,1024]{1,0:T(8,128)(2,1)S(1)} %get-tuple-element.69), channel_id=1, source_target_pairs={{60,0},{0,4},{4,8},{8,12},{12,16},{16,20},{20,24},{24,28},{28,32},... | collective-permute-start | bytes 737288 | tf_op jit(solution)/shard_map/ppermute | solution.py:231
  42.9 9.9 %collective-permute-start.4 = (bf16[120,1024]{1,0:T(8,128)(2,1)S(1)}, bf16[120,1024]{1,0:T(8,128)(2,1)S(1)}, u32[]{:S(2)}, u32[]{:S(2)}) collective-permute-start(bf16[120,1024]{1,0:T(8,128)(2,1)S(1)} %get-tuple-element.69), channel_id=1, source_target_pairs={{8,0},{12,4},{16,8},{20,12},{24,16},{28,20},{32,24},{36,28},{40,32... | collective-permute-start | bytes 737288 | tf_op jit(solution)/shard_map/ppermute | solution.py:231
  45.2 15.3 %collective-permute-start.5 = (bf16[120,1024]{1,0:T(8,128)(2,1)S(1)}, bf16[120,1024]{1,0:T(8,128)(2,1)S(1)}, u32[]{:S(2)}, u32[]{:S(2)}) collective-permute-start(bf16[120,1024]{1,0:T(8,128)(2,1)S(1)} %get-tuple-element.69), channel_id=1, source_target_pairs={{56,0},{60,4},{0,8},{4,12},{8,16},{12,20},{16,24},{20,28},{24,32},... | collective-permute-start | bytes 737288 | tf_op jit(solution)/shard_map/ppermute | solution.py:231
  49.7 12.2 %collective-permute-start.6 = (bf16[40,1024]{1,0:T(8,128)(2,1)S(1)}, bf16[40,1024]{1,0:T(8,128)(2,1)S(1)}, u32[]{:S(2)}, u32[]{:S(2)}) collective-permute-start(bf16[40,1024]{1,0:T(8,128)(2,1)S(1)} %collective-permute-done), channel_id=1, source_target_pairs={{12,0},{16,4},{20,8},{24,12},{28,16},{32,20},{36,24},{40,28},{44,3... | collective-permute-start | bytes 245768 | tf_op jit(solution)/shard_map/ppermute | solution.py:231
  52.8 15.9 %copy-start = (bf16[512,1536]{1,0:T(8,128)(2,1)S(1)}, bf16[512,1536]{1,0:T(8,128)(2,1)}, u32[]{:S(2)}) copy-start(bf16[512,1536]{1,0:T(8,128)(2,1)} %shard_map.112.w) | copy-start | bytes 4718596
  63.8 20.4 %copy-start.2 = (bf16[320,1024]{1,0:T(8,128)(2,1)}, bf16[320,1024]{1,0:T(8,128)(2,1)S(1)}, u32[]{:S(2)}) copy-start(bf16[320,1024]{1,0:T(8,128)(2,1)S(1)} %get-tuple-element.43.rows.near) | copy-start | bytes 1966084
  63.8 14.6 %collective-permute-start.7 = (bf16[320,1024]{1,0:T(8,128)(2,1)S(1)}, bf16[320,1024]{1,0:T(8,128)(2,1)S(1)}, u32[]{:S(2)}, u32[]{:S(2)}) collective-permute-start(bf16[320,1024]{1,0:T(8,128)(2,1)S(1)} %get-tuple-element.39), channel_id=1, source_target_pairs={{1,2},{2,1},{3,0},{0,3},{5,6},{6,5},{7,4},{4,7},{9,10},{10,9},{11,... | collective-permute-start | bytes 1966088 | tf_op jit(solution)/shard_map/ppermute | solution.py:243
  70.0 11.6 %collective-permute-start.9 = (bf16[160,3072]{1,0:T(8,128)(2,1)S(1)}, bf16[160,3072]{1,0:T(8,128)(2,1)S(1)}, u32[]{:S(2)}, u32[]{:S(2)}) collective-permute-start(bf16[160,3072]{1,0:T(8,128)(2,1)S(1)} %shard_map.113), channel_id=1, source_target_pairs={{0,64},{64,0},{1,65},{65,1},{2,66},{66,2},{3,67},{67,3},{4,68},{68... | collective-permute-start | bytes 2949128 | tf_op jit(solution)/shard_map/ppermute | solution.py:235
  79.7 4.5 %collective-permute-start.10 = (bf16[160,3072]{1,0:T(8,128)(2,1)S(1)}, bf16[160,3072]{1,0:T(8,128)(2,1)S(1)}, u32[]{:S(2)}, u32[]{:S(2)}) collective-permute-start(bf16[160,3072]{1,0:T(8,128)(2,1)S(1)} %shard_map.114), channel_id=1, source_target_pairs={{0,64},{64,0},{1,65},{65,1},{2,66},{66,2},{3,67},{67,3},{4,68},{68... | collective-permute-start | bytes 2949128 | tf_op jit(solution)/shard_map/ppermute | solution.py:235
  87.2 28.4 %all-to-all-start = ((bf16[4,80,3072]{2,1,0:T(8,128)(2,1)}), bf16[4,80,3072]{2,1,0:T(8,128)(2,1)}, u32[]{:S(2)}, u32[]{:S(2)}) async-start(bf16[4,80,3072]{2,1,0:T(8,128)(2,1)} %bitcast.23), calls=%async_computation | async-start | bytes 3932160 | tf_op jit(solution)/shard_map/all_to_all | solution.py:247
  145.8 6.1 %collective-permute-start.11 = (bf16[320,3200]{1,0:T(8,128)(2,1)S(1)}, bf16[320,3200]{1,0:T(8,128)(2,1)S(1)}, u32[]{:S(2)}, u32[]{:S(2)}) collective-permute-start(bf16[320,3200]{1,0:T(8,128)(2,1)S(1)} %bitcast.19), channel_id=1, source_target_pairs={{0,64},{64,0},{1,65},{65,1},{2,66},{66,2},{3,67},{67,3},{4,68},{68... | collective-permute-start | bytes 6144008 | tf_op jit(solution)/shard_map/ppermute | solution.py:235
  154.0 14.0 %collective-permute-start.13 = (bf16[320,512]{1,0:T(8,128)(2,1)S(1)}, bf16[320,512]{1,0:T(8,128)(2,1)S(1)}, u32[]{:S(2)}, u32[]{:S(2)}) collective-permute-start(bf16[320,512]{1,0:T(8,128)(2,1)S(1)} %shard_map.117), channel_id=1, source_target_pairs={{1,2},{2,1},{3,0},{0,3},{5,6},{6,5},{7,4},{4,7},{9,10},{10,9},{11,... | collective-permute-start | bytes 983048 | tf_op jit(solution)/shard_map/ppermute | solution.py:243
  164.0 45.6 %collective-permute-start.12 = (bf16[448,1536]{1,0:T(8,128)(2,1)S(1)}, bf16[448,1536]{1,0:T(8,128)(2,1)S(1)}, u32[]{:S(2)}, u32[]{:S(2)}) collective-permute-start(bf16[448,1536]{1,0:T(8,128)(2,1)S(1)} %get-tuple-element.46), channel_id=1, source_target_pairs={{0,1},{1,0},{2,3},{3,2},{4,5},{5,4},{6,7},{7,6},{8,9},{9,8},{10,11... | collective-permute-start | bytes 4128776 | tf_op jit(solution)/shard_map/ppermute | solution.py:239
  169.5 18.3 %collective-permute-start.18 = (bf16[40,512]{1,0:T(8,128)(2,1)S(1)}, bf16[40,512]{1,0:T(8,128)(2,1)S(1)}, u32[]{:S(2)}, u32[]{:S(2)}) collective-permute-start(bf16[40,512]{1,0:T(8,128)(2,1)S(1)} %get-tuple-element.52), channel_id=1, source_target_pairs={{52,0},{56,4},{60,8},{0,12},{4,16},{8,20},{12,24},{16,28},{20,32},... | collective-permute-start | bytes 122888 | tf_op jit(solution)/shard_map/ppermute | solution.py:231
  178.8 15.1 %collective-permute-start.14 = (bf16[120,512]{1,0:T(8,128)(2,1)S(1)}, bf16[120,512]{1,0:T(8,128)(2,1)S(1)}, u32[]{:S(2)}, u32[]{:S(2)}) collective-permute-start(bf16[120,512]{1,0:T(8,128)(2,1)S(1)} %get-tuple-element.48), channel_id=1, source_target_pairs={{60,0},{0,4},{4,8},{8,12},{12,16},{16,20},{20,24},{24,28},{28,32},... | collective-permute-start | bytes 368648 | tf_op jit(solution)/shard_map/ppermute | solution.py:231
  180.7 13.1 %collective-permute-start.15 = (bf16[120,512]{1,0:T(8,128)(2,1)S(1)}, bf16[120,512]{1,0:T(8,128)(2,1)S(1)}, u32[]{:S(2)}, u32[]{:S(2)}) collective-permute-start(bf16[120,512]{1,0:T(8,128)(2,1)S(1)} %get-tuple-element.49), channel_id=1, source_target_pairs={{4,0},{8,4},{12,8},{16,12},{20,16},{24,20},{28,24},{32,28},{36,32}... | collective-permute-start | bytes 368648 | tf_op jit(solution)/shard_map/ppermute | solution.py:231
  185.9 9.7 %collective-permute-start.16 = (bf16[120,512]{1,0:T(8,128)(2,1)S(1)}, bf16[120,512]{1,0:T(8,128)(2,1)S(1)}, u32[]{:S(2)}, u32[]{:S(2)}) collective-permute-start(bf16[120,512]{1,0:T(8,128)(2,1)S(1)} %get-tuple-element.50), channel_id=1, source_target_pairs={{56,0},{60,4},{0,8},{4,12},{8,16},{12,20},{16,24},{20,28},{24,32},... | collective-permute-start | bytes 368648 | tf_op jit(solution)/shard_map/ppermute | solution.py:231
  187.8 9.2 %collective-permute-start.17 = (bf16[120,512]{1,0:T(8,128)(2,1)S(1)}, bf16[120,512]{1,0:T(8,128)(2,1)S(1)}, u32[]{:S(2)}, u32[]{:S(2)}) collective-permute-start(bf16[120,512]{1,0:T(8,128)(2,1)S(1)} %get-tuple-element.51), channel_id=1, source_target_pairs={{8,0},{12,4},{16,8},{20,12},{24,16},{28,20},{32,24},{36,28},{40,32... | collective-permute-start | bytes 368648 | tf_op jit(solution)/shard_map/ppermute | solution.py:231
  197.7 13.7 %collective-permute-start.19 = (bf16[40,512]{1,0:T(8,128)(2,1)S(1)}, bf16[40,512]{1,0:T(8,128)(2,1)S(1)}, u32[]{:S(2)}, u32[]{:S(2)}) collective-permute-start(bf16[40,512]{1,0:T(8,128)(2,1)S(1)} %get-tuple-element.55), channel_id=1, source_target_pairs={{44,0},{48,4},{52,8},{56,12},{60,16},{0,20},{4,24},{8,28},{12,32},... | collective-permute-start | bytes 122888 | tf_op jit(solution)/shard_map/ppermute | solution.py:231
  200.2 12.3 %collective-permute-start.20 = (bf16[40,512]{1,0:T(8,128)(2,1)S(1)}, bf16[40,512]{1,0:T(8,128)(2,1)S(1)}, u32[]{:S(2)}, u32[]{:S(2)}) collective-permute-start(bf16[40,512]{1,0:T(8,128)(2,1)S(1)} %get-tuple-element.56), channel_id=1, source_target_pairs={{20,0},{24,4},{28,8},{32,12},{36,16},{40,20},{44,24},{48,28},{52,3... | collective-permute-start | bytes 122888 | tf_op jit(solution)/shard_map/ppermute | solution.py:231
  (13 other events, 52.1 us)

commit v4 on v3

--- a/solution.py
+++ b/solution.py
@@ -50,23 +50,22 @@
     return lax.broadcasted_iota(I32, shape, axis)
 
 
-def pack(sc, tok, cot, ids, wts, out):
-    wts_f = wts[...].astype(F32)
+def pack(sc, both, slots, out):
     named = jnp.zeros((EXP, TOK), F32)
     weight = jnp.zeros((EXP, TOK), F32)
     for k in range(8):
-        match = iota((EXP, TOK), 0) == ids[k : k + 1, :]
+        match = iota((EXP, TOK), 0).astype(F32) == slots[k : k + 1, :]
         named += jnp.where(match, 1.0, 0.0)
-        weight += jnp.where(match, wts_f[k : k + 1, :], 0.0)
+        weight += jnp.where(match, slots[8 + k : 9 + k, :], 0.0)
     before = (iota((TOK, TOK), 0) < iota((TOK, TOK), 1)).astype(BF)
     rank = dot(named.astype(BF), before)
     code = jnp.concatenate([named * (rank + 1.0), weight], 0).astype(BF)
     spread = (iota((64, 128), 0) + 64 == iota((64, 128), 1)).astype(BF)
     meta = dot(code, spread, FIRST).astype(BF)
     low = iota((TOK, 128), 1) < 64
-    out[:, 0:FEAT] = tok[...]
+    out[:, 0:FEAT] = both[:, 0:FEAT]
     out[:, 384:512] = jnp.where(low, out[:, 384:512], meta)
-    out[:, 512 : 512 + FEAT] = cot[...]
+    out[:, 512 : 512 + FEAT] = both[:, 512 : 512 + FEAT]
     out[:, 896:1024] = jnp.where(low, out[:, 896:1024], jnp.zeros((TOK, 128), BF))
 
 
@@ -148,15 +147,22 @@
         g_out[k, :, 2048:2176] = dot_tile
 
 
-def backward(lo):
-    def body(sc, g, go, w, wf, out):
-        put = (iota((128, WIDE), 0) == 0) & (iota((128, WIDE), 1) == FEAT + sc[0])
-        put = put.astype(BF)
-        for at, ref in ((0, g), (PART, go)):
-            t = dot(ref[lo : lo + PART, 0:1024], w[:, 0:1024], LAST)
-            t += dot(ref[lo : lo + PART, 1024:2048], wf[:, 0:1024], LAST)
-            t += dot(ref[lo : lo + PART, 2048:2176], put)
-            out[at : at + PART, :] = t.astype(BF)
+def back_rows(sc, g, lo, rows, w, wf):
+    put = (iota((128, WIDE), 0) == 0) & (iota((128, WIDE), 1) == FEAT + sc[0])
+    t = dot(g[lo : lo + rows, 0:1024], w[:, 0:1024], LAST)
+    t += dot(g[lo : lo + rows, 1024:2048], wf[:, 0:1024], LAST)
+    t += dot(g[lo : lo + rows, 2048:2176], put.astype(BF))
+    return t.astype(BF)
+
+
+def backward_mine(sc, g, w, wf, out):
+    out[...] = back_rows(sc, g, 0, ROWS, w, wf)
+
+
+def backward_others(lo):
+    def body(sc, go, w, wf, mine, out):
+        out[0:PART, :] = mine[lo : lo + PART, :]
+        out[PART:ROWS, :] = back_rows(sc, go, lo, PART, w, wf)
 
     return body
 
@@ -253,9 +259,9 @@
     z = lax.axis_index("z")
     sc = jnp.stack([2 * z + high, 2 * z + 1 - high, core, lax.axis_index("x")]).astype(I32)
     ids_t = expert_ids.T
-    (payload,) = call(
-        pack, [((TOK, 1024), BF)], sc, tokens, cotangent, ids_t, route_weight.T, own_copies=True
-    )
+    both = jnp.concatenate([tokens, jnp.zeros((TOK, 64), BF), cotangent], 1)
+    slots = jnp.concatenate([ids_t.astype(F32), route_weight.T.astype(F32)], 0)
+    (payload,) = call(pack, [((TOK, 1024), BF)], sc, both, slots)
     payload, gate_m, up_m, down_m = lax.optimization_barrier(
         (payload, gate_weight[0], up_weight[0], down_weight[0].T)
     )
@@ -286,10 +292,12 @@
     )
     g = trade(g_out, "x").reshape(ROWS, 3200)
     g_far = swap_core(g)
-    (away,) = call(backward(PART), [((ROWS, WIDE), BF)], sc, g, g_far, w, w_far)
+    (back_mine,) = call(backward_mine, [((ROWS, WIDE), BF)], sc, g, w, w_far)
+    out = [((ROWS, WIDE), BF)]
+    (away,) = call(backward_others(PART), out, sc, g_far, w, w_far, back_mine)
     back = swap_expert(away)
     near_w, far_w, g, _ = lax.optimization_barrier((near, far, g, away))
-    (keep,) = call(backward(0), [((ROWS, WIDE), BF)], sc, g, g_far, w, w_far)
+    (keep,) = call(backward_others(0), out, sc, g_far, w, w_far, back_mine)
     mine_w, partner_w = call(
         weight_grads, [((FEAT, 1536), F32), ((FEAT, 1536), BF)],
         sc, near_w, far_w, g, g_far, flops=8 * ROWS * WIDE * 1536,
@@ -299,8 +307,8 @@
         scatter, [((3 * TOK, WIDE), BF)] * 5 + [((TOK, WIDE), BF)],
         sc, every[:, 384:512], keep, back, flops=30 * 10**9,
     )
-    moved = [take(a, "z", -step) for a, step in zip(sums[1:5], (1, -1, 2, -2))]
-    moved.append(take(sums[5], "z", -3))
+    order = ((1, 1), (3, 2), (2, -1), (4, -2), (5, 3))
+    moved = [take(sums[slot], "z", -step) for slot, step in order]
     first, mid, last = call(
         add_near, [((TOK, WIDE), BF), ((TOK, WIDE), F32), ((TOK, WIDE), BF)], sc, sums[0], *moved
     )

time: 216 us -> 215 us (level)
  local copies, waits for them, and re-layouts: 9.86 us -> 7.02 us
  other arithmetic: 0.08 us -> 2.28 us
    unnamed x36 -> x28, local copies, waits for them, and re-layouts: 7.35 us -> 4.43 us
    pallas_call x14 -> x15, Pallas kernels: 24.5 us -> 24.5 us  [call(): pl.pallas_call(body, grid=(1,) if own_copies else (), out_shape=[jax.Shap...]
  transfers between devices with their start and end apart: 22 -> 22, of which waited for: 10 -> 9; matrix products, arithmetic and copies ran while one was open for 1% -> 1% of each run, Pallas kernels for 8% -> 8%
where the time goes in v4:
time: 215 us; the launch traced here: 211 us
  starting transfers between devices  92.6 us (43%)
  waiting for transfers between devices  55.6 us (26%)
  blocking collectives  28 us (13%)
  Pallas kernels  24.5 us (11%)
  local copies, waits for them, and re-layouts  7.02 us (3%)
  other arithmetic  2.28 us (1%)
    ppermute x14, starting transfers between devices, take(): return lax.ppermute(a, axis, [((i + step) % n, i) for i in range(n)])  66.9 us
    all_to_all x1, blocking collectives, trade(): return lax.all_to_all(a, axis, split_axis=0, concat_axis=0, tiled=True)  28 us
    pallas_call x15, Pallas kernels, call(): pl.pallas_call(body, grid=(1,) if own_copies else (), out_shape=[jax.Shap...  24.5 us
    ppermute x14, waiting for transfers between devices, take(): return lax.ppermute(a, axis, [((i + step) % n, i) for i in range(n)])  22 us
    all_to_all x1, waiting for transfers between devices, trade(): return lax.all_to_all(a, axis, split_axis=0, concat_axis=0, tiled=True)  22 us
    ppermute x2, starting transfers between devices, swap_expert(): return lax.ppermute(a, 'y', [(1, 2), (2, 1), (3, 0), (0, 3)])  9.73 us
    ppermute x2, waiting for transfers between devices, swap_expert(): return lax.ppermute(a, 'y', [(1, 2), (2, 1), (3, 0), (0, 3)])  6.59 us
    ppermute x3, starting transfers between devices, swap_core(): return lax.ppermute(a, 'core', [(0, 1), (1, 0)])  5.75 us
  transfers between devices with their start and end apart: 22, of which 9 were waited for; matrix products, arithmetic and copies ran while one was open for 1% of the time, Pallas kernels for 8%

profile of v4, /device:TPU:6, one launch (start us, length us, event | category | flops | bytes accessed | tf_op | source)
XLA Modules:
  0.0 211.2 jit_solution(2719948271673776758)
XLA Ops:
  3.9 14.4 %collective-permute-start = (bf16[40,1024]{1,0:T(8,128)(2,1)S(1)}, bf16[40,1024]{1,0:T(8,128)(2,1)S(1)}, u32[]{:S(2)}, u32[]{:S(2)}) collective-permute-start(bf16[40,1024]{1,0:T(8,128)(2,1)S(1)} %shard_map.110), channel_id=1, source_target_pairs={{20,0},{24,4},{28,8},{32,12},{36,16},{40,20},{44,24},{48,28},{52,3... | collective-permute-start | bytes 245768 | tf_op jit(solution)/shard_map/ppermute | solution.py:237
  25.1 3.5 %collective-permute-start.8 = (bf16[512,1536]{1,0:T(8,128)(2,1)}, bf16[512,1536]{1,0:T(8,128)(2,1)S(1)}, u32[]{:S(2)}, u32[]{:S(2)}) collective-permute-start(bf16[512,1536]{1,0:T(8,128)(2,1)} %shard_map.112.w), channel_id=1, source_target_pairs={{0,1},{1,0},{2,3},{3,2},{4,5},{5,4},{6,7},{7,6},{8,9},{9,8},{10,11... | collective-permute-start | bytes 4718600 | tf_op jit(solution)/shard_map/ppermute | solution.py:245
  28.6 7.8 %collective-permute-done.1 = bf16[40,1024]{1,0:T(8,128)(2,1)S(1)} collective-permute-done((bf16[40,1024]{1,0:T(8,128)(2,1)S(1)}, bf16[40,1024]{1,0:T(8,128)(2,1)S(1)}, u32[]{:S(2)}, u32[]{:S(2)}) %collective-permute-start.1) | collective-permute-done | bytes 81952 | tf_op jit(solution)/shard_map/ppermute | solution.py:237
  36.4 2.4 %collective-permute-start.2 = (bf16[120,1024]{1,0:T(8,128)(2,1)S(1)}, bf16[120,1024]{1,0:T(8,128)(2,1)S(1)}, u32[]{:S(2)}, u32[]{:S(2)}) collective-permute-start(bf16[120,1024]{1,0:T(8,128)(2,1)S(1)} %get-tuple-element.69), channel_id=1, source_target_pairs={{4,0},{8,4},{12,8},{16,12},{20,16},{24,20},{28,24},{32,28},{36,32}... | collective-permute-start | bytes 737288 | tf_op jit(solution)/shard_map/ppermute | solution.py:237
  38.8 3.4 %collective-permute-start.3 = (bf16[120,1024]{1,0:T(8,128)(2,1)S(1)}, bf16[120,1024]{1,0:T(8,128)(2,1)S(1)}, u32[]{:S(2)}, u32[]{:S(2)}) collective-permute-start(bf16[120,1024]{1,0:T(8,128)(2,1)S(1)} %get-tuple-element.69), channel_id=1, source_target_pairs={{60,0},{0,4},{4,8},{8,12},{12,16},{16,20},{20,24},{24,28},{28,32},... | collective-permute-start | bytes 737288 | tf_op jit(solution)/shard_map/ppermute | solution.py:237
  44.5 4.5 %collective-permute-start.5 = (bf16[120,1024]{1,0:T(8,128)(2,1)S(1)}, bf16[120,1024]{1,0:T(8,128)(2,1)S(1)}, u32[]{:S(2)}, u32[]{:S(2)}) collective-permute-start(bf16[120,1024]{1,0:T(8,128)(2,1)S(1)} %get-tuple-element.69), channel_id=1, source_target_pairs={{56,0},{60,4},{0,8},{4,12},{8,16},{12,20},{16,24},{20,28},{24,32},... | collective-permute-start | bytes 737288 | tf_op jit(solution)/shard_map/ppermute | solution.py:237
  49.0 3.1 %collective-permute-start.6 = (bf16[40,1024]{1,0:T(8,128)(2,1)S(1)}, bf16[40,1024]{1,0:T(8,128)(2,1)S(1)}, u32[]{:S(2)}, u32[]{:S(2)}) collective-permute-start(bf16[40,1024]{1,0:T(8,128)(2,1)S(1)} %collective-permute-done), channel_id=1, source_target_pairs={{12,0},{16,4},{20,8},{24,12},{28,16},{32,20},{36,24},{40,28},{44,3... | collective-permute-start | bytes 245768 | tf_op jit(solution)/shard_map/ppermute | solution.py:237
  52.2 7.6 %collective-permute-done.5 = bf16[120,1024]{1,0:T(8,128)(2,1)S(1)} collective-permute-done((bf16[120,1024]{1,0:T(8,128)(2,1)S(1)}, bf16[120,1024]{1,0:T(8,128)(2,1)S(1)}, u32[]{:S(2)}, u32[]{:S(2)}) %collective-permute-start.5) | collective-permute-done | bytes 245792 | tf_op jit(solution)/shard_map/ppermute | solution.py:237
  63.2 4.9 %collective-permute-start.7 = (bf16[320,1024]{1,0:T(8,128)(2,1)S(1)}, bf16[320,1024]{1,0:T(8,128)(2,1)S(1)}, u32[]{:S(2)}, u32[]{:S(2)}) collective-permute-start(bf16[320,1024]{1,0:T(8,128)(2,1)S(1)} %get-tuple-element.39), channel_id=1, source_target_pairs={{1,2},{2,1},{3,0},{0,3},{5,6},{6,5},{7,4},{4,7},{9,10},{10,9},{11,... | collective-permute-start | bytes 1966088 | tf_op jit(solution)/shard_map/ppermute | solution.py:249
  71.2 6.6 %collective-permute-done.7.rows.far = bf16[320,1024]{1,0:T(8,128)(2,1)S(1)} collective-permute-done((bf16[320,1024]{1,0:T(8,128)(2,1)S(1)}, bf16[320,1024]{1,0:T(8,128)(2,1)S(1)}, u32[]{:S(2)}, u32[]{:S(2)}) %collective-permute-start.7) | collective-permute-done | bytes 655392 | tf_op jit(solution)/shard_map/ppermute | solution.py:249
  81.0 2.5 %collective-permute-done.10.got_far = bf16[160,3072]{1,0:T(8,128)(2,1)S(1)} collective-permute-done((bf16[160,3072]{1,0:T(8,128)(2,1)S(1)}, bf16[160,3072]{1,0:T(8,128)(2,1)S(1)}, u32[]{:S(2)}, u32[]{:S(2)}) %collective-permute-start.10) | collective-permute-done | bytes 983072 | tf_op jit(solution)/shard_map/ppermute | solution.py:241
  86.6 4.8 %all-to-all-start = ((bf16[4,80,3072]{2,1,0:T(8,128)(2,1)}), bf16[4,80,3072]{2,1,0:T(8,128)(2,1)}, u32[]{:S(2)}, u32[]{:S(2)}) async-start(bf16[4,80,3072]{2,1,0:T(8,128)(2,1)} %bitcast.24), calls=%async_computation | async-start | bytes 3932160 | tf_op jit(solution)/shard_map/all_to_all | solution.py:253
  93.0 22.0 %all-to-all-done.pieces = bf16[4,80,3072]{2,1,0:T(8,128)(2,1)} async-done(((bf16[4,80,3072]{2,1,0:T(8,128)(2,1)}), bf16[4,80,3072]{2,1,0:T(8,128)(2,1)}, u32[]{:S(2)}, u32[]{:S(2)}) %all-to-all-start) | async-done | bytes 1966112 | tf_op jit(solution)/shard_map/all_to_all | solution.py:253
  117.2 28.0 %all_to_all.10 = bf16[4,80,3200]{2,1,0:T(8,128)(2,1)S(1)} all-to-all(bf16[4,80,3200]{2,1,0:T(8,128)(2,1)S(1)} %shard_map.116), channel_id=1, replica_groups=mesh['x'=4,'core'=2,'z'=16,'y'=4] {'x'}, dimensions={0} | all-to-all | bytes 4096000 | tf_op jit(solution)/shard_map/all_to_all | solution.py:253
  148.6 2.5 %collective-permute-done.11.go = bf16[320,3200]{1,0:T(8,128)(2,1)S(1)} collective-permute-done((bf16[320,3200]{1,0:T(8,128)(2,1)S(1)}, bf16[320,3200]{1,0:T(8,128)(2,1)S(1)}, u32[]{:S(2)}, u32[]{:S(2)}) %collective-permute-start.11) | collective-permute-done | bytes 2048032 | tf_op jit(solution)/shard_map/ppermute | solution.py:241
  152.6 4.9 %collective-permute-start.13 = (bf16[320,512]{1,0:T(8,128)(2,1)S(1)}, bf16[320,512]{1,0:T(8,128)(2,1)S(1)}, u32[]{:S(2)}, u32[]{:S(2)}) collective-permute-start(bf16[320,512]{1,0:T(8,128)(2,1)S(1)} %shard_map.118), channel_id=1, source_target_pairs={{1,2},{2,1},{3,0},{0,3},{5,6},{6,5},{7,4},{4,7},{9,10},{10,9},{11,... | collective-permute-start | bytes 983048 | tf_op jit(solution)/shard_map/ppermute | solution.py:249
  158.4 4.1 %shard_map.119 = (f32[448,1536]{1,0:T(8,128)S(1)}, bf16[448,1536]{1,0:T(8,128)(2,1)S(1)}) custom-call(s32[4]{0:T(128)S(1)} %pad_add_fusion.sc, bf16[320,1024]{1,0:T(8,128)(2,1)S(1)} %copy-done.3, bf16[320,1024]{1,0:T(8,128)(2,1)S(1)} %copy-done.5, bf16[320,3200]{1,0:T(8,128)(2,1)S(1)} %bitcast.23, bf16[320,3200]{1,0:T(8,128)(2,1)S(1)} %collective-permute-done.11.go), custom_call_target="tpu_custom_call" | custom-call | flops 2013265920 | bytes 5406720 | tf_op jit(solution)/shard_map/pallas_call | solution.py:38
  167.3 9.3 %collective-permute-start.18 = (bf16[40,512]{1,0:T(8,128)(2,1)S(1)}, bf16[40,512]{1,0:T(8,128)(2,1)S(1)}, u32[]{:S(2)}, u32[]{:S(2)}) collective-permute-start(bf16[40,512]{1,0:T(8,128)(2,1)S(1)} %get-tuple-element.52), channel_id=1, source_target_pairs={{52,0},{56,4},{60,8},{0,12},{4,16},{8,20},{12,24},{16,28},{20,32},... | collective-permute-start | bytes 122888 | tf_op jit(solution)/shard_map/ppermute | solution.py:237
  178.5 3.2 %collective-permute-start.15 = (bf16[120,512]{1,0:T(8,128)(2,1)S(1)}, bf16[120,512]{1,0:T(8,128)(2,1)S(1)}, u32[]{:S(2)}, u32[]{:S(2)}) collective-permute-start(bf16[120,512]{1,0:T(8,128)(2,1)S(1)} %get-tuple-element.49), channel_id=1, source_target_pairs={{56,0},{60,4},{0,8},{4,12},{8,16},{12,20},{16,24},{20,28},{24,32},... | collective-permute-start | bytes 368648 | tf_op jit(solution)/shard_map/ppermute | solution.py:237
  181.7 5.1 %collective-permute-start.16 = (bf16[120,512]{1,0:T(8,128)(2,1)S(1)}, bf16[120,512]{1,0:T(8,128)(2,1)S(1)}, u32[]{:S(2)}, u32[]{:S(2)}) collective-permute-start(bf16[120,512]{1,0:T(8,128)(2,1)S(1)} %get-tuple-element.50), channel_id=1, source_target_pairs={{4,0},{8,4},{12,8},{16,12},{20,16},{24,20},{28,24},{32,28},{36,32}... | collective-permute-start | bytes 368648 | tf_op jit(solution)/shard_map/ppermute | solution.py:237
  186.8 3.6 %collective-permute-start.17 = (bf16[120,512]{1,0:T(8,128)(2,1)S(1)}, bf16[120,512]{1,0:T(8,128)(2,1)S(1)}, u32[]{:S(2)}, u32[]{:S(2)}) collective-permute-start(bf16[120,512]{1,0:T(8,128)(2,1)S(1)} %get-tuple-element.51), channel_id=1, source_target_pairs={{8,0},{12,4},{16,8},{20,12},{24,16},{28,20},{32,24},{36,28},{40,32... | collective-permute-start | bytes 368648 | tf_op jit(solution)/shard_map/ppermute | solution.py:237
  190.4 4.5 %collective-permute-done.17.d = bf16[120,512]{1,0:T(8,128)(2,1)S(1)} collective-permute-done((bf16[120,512]{1,0:T(8,128)(2,1)S(1)}, bf16[120,512]{1,0:T(8,128)(2,1)S(1)}, u32[]{:S(2)}, u32[]{:S(2)}) %collective-permute-start.17) | collective-permute-done | bytes 122912 | tf_op jit(solution)/shard_map/ppermute | solution.py:237
  195.6 2.3 %collective-permute-start.19 = (bf16[40,512]{1,0:T(8,128)(2,1)S(1)}, bf16[40,512]{1,0:T(8,128)(2,1)S(1)}, u32[]{:S(2)}, u32[]{:S(2)}) collective-permute-start(bf16[40,512]{1,0:T(8,128)(2,1)S(1)} %get-tuple-element.55), channel_id=1, source_target_pairs={{44,0},{48,4},{52,8},{56,12},{60,16},{0,20},{4,24},{8,28},{12,32},... | collective-permute-start | bytes 122888 | tf_op jit(solution)/shard_map/ppermute | solution.py:237
  197.9 9.6 %collective-permute-start.20 = (bf16[40,512]{1,0:T(8,128)(2,1)S(1)}, bf16[40,512]{1,0:T(8,128)(2,1)S(1)}, u32[]{:S(2)}, u32[]{:S(2)}) collective-permute-start(bf16[40,512]{1,0:T(8,128)(2,1)S(1)} %get-tuple-element.56), channel_id=1, source_target_pairs={{20,0},{24,4},{28,8},{32,12},{36,16},{40,20},{44,24},{48,28},{52,3... | collective-permute-start | bytes 122888 | tf_op jit(solution)/shard_map/ppermute | solution.py:237
  (76 shorter events, 45.6 us)
Async XLA Ops:
  3.9 24.7 %collective-permute-start = (bf16[40,1024]{1,0:T(8,128)(2,1)S(1)}, bf16[40,1024]{1,0:T(8,128)(2,1)S(1)}, u32[]{:S(2)}, u32[]{:S(2)}) collective-permute-start(bf16[40,1024]{1,0:T(8,128)(2,1)S(1)} %shard_map.110), channel_id=1, source_target_pairs={{20,0},{24,4},{28,8},{32,12},{36,16},{40,20},{44,24},{48,28},{52,3... | collective-permute-start | bytes 245768 | tf_op jit(solution)/shard_map/ppermute | solution.py:237
  18.3 18.1 %collective-permute-start.1 = (bf16[40,1024]{1,0:T(8,128)(2,1)S(1)}, bf16[40,1024]{1,0:T(8,128)(2,1)S(1)}, u32[]{:S(2)}, u32[]{:S(2)}) collective-permute-start(bf16[40,1024]{1,0:T(8,128)(2,1)S(1)} %shard_map.110), channel_id=1, source_target_pairs={{44,0},{48,4},{52,8},{56,12},{60,16},{0,20},{4,24},{8,28},{12,32},... | collective-permute-start | bytes 245768 | tf_op jit(solution)/shard_map/ppermute | solution.py:237
  25.1 43.0 %collective-permute-start.8 = (bf16[512,1536]{1,0:T(8,128)(2,1)}, bf16[512,1536]{1,0:T(8,128)(2,1)S(1)}, u32[]{:S(2)}, u32[]{:S(2)}) collective-permute-start(bf16[512,1536]{1,0:T(8,128)(2,1)} %shard_map.112.w), channel_id=1, source_target_pairs={{0,1},{1,0},{2,3},{3,2},{4,5},{5,4},{6,7},{7,6},{8,9},{9,8},{10,11... | collective-permute-start | bytes 4718600 | tf_op jit(solution)/shard_map/ppermute | solution.py:245
  36.4 12.6 %collective-permute-start.2 = (bf16[120,1024]{1,0:T(8,128)(2,1)S(1)}, bf16[120,1024]{1,0:T(8,128)(2,1)S(1)}, u32[]{:S(2)}, u32[]{:S(2)}) collective-permute-start(bf16[120,1024]{1,0:T(8,128)(2,1)S(1)} %get-tuple-element.69), channel_id=1, source_target_pairs={{4,0},{8,4},{12,8},{16,12},{20,16},{24,20},{28,24},{32,28},{36,32}... | collective-permute-start | bytes 737288 | tf_op jit(solution)/shard_map/ppermute | solution.py:237
  38.8 13.3 %collective-permute-start.3 = (bf16[120,1024]{1,0:T(8,128)(2,1)S(1)}, bf16[120,1024]{1,0:T(8,128)(2,1)S(1)}, u32[]{:S(2)}, u32[]{:S(2)}) collective-permute-start(bf16[120,1024]{1,0:T(8,128)(2,1)S(1)} %get-tuple-element.69), channel_id=1, source_target_pairs={{60,0},{0,4},{4,8},{8,12},{12,16},{16,20},{20,24},{24,28},{28,32},... | collective-permute-start | bytes 737288 | tf_op jit(solution)/shard_map/ppermute | solution.py:237
  42.3 9.9 %collective-permute-start.4 = (bf16[120,1024]{1,0:T(8,128)(2,1)S(1)}, bf16[120,1024]{1,0:T(8,128)(2,1)S(1)}, u32[]{:S(2)}, u32[]{:S(2)}) collective-permute-start(bf16[120,1024]{1,0:T(8,128)(2,1)S(1)} %get-tuple-element.69), channel_id=1, source_target_pairs={{8,0},{12,4},{16,8},{20,12},{24,16},{28,20},{32,24},{36,28},{40,32... | collective-permute-start | bytes 737288 | tf_op jit(solution)/shard_map/ppermute | solution.py:237
  44.5 15.3 %collective-permute-start.5 = (bf16[120,1024]{1,0:T(8,128)(2,1)S(1)}, bf16[120,1024]{1,0:T(8,128)(2,1)S(1)}, u32[]{:S(2)}, u32[]{:S(2)}) collective-permute-start(bf16[120,1024]{1,0:T(8,128)(2,1)S(1)} %get-tuple-element.69), channel_id=1, source_target_pairs={{56,0},{60,4},{0,8},{4,12},{8,16},{12,20},{16,24},{20,28},{24,32},... | collective-permute-start | bytes 737288 | tf_op jit(solution)/shard_map/ppermute | solution.py:237
  49.0 12.2 %collective-permute-start.6 = (bf16[40,1024]{1,0:T(8,128)(2,1)S(1)}, bf16[40,1024]{1,0:T(8,128)(2,1)S(1)}, u32[]{:S(2)}, u32[]{:S(2)}) collective-permute-start(bf16[40,1024]{1,0:T(8,128)(2,1)S(1)} %collective-permute-done), channel_id=1, source_target_pairs={{12,0},{16,4},{20,8},{24,12},{28,16},{32,20},{36,24},{40,28},{44,3... | collective-permute-start | bytes 245768 | tf_op jit(solution)/shard_map/ppermute | solution.py:237
  52.2 15.9 %copy-start = (bf16[512,1536]{1,0:T(8,128)(2,1)S(1)}, bf16[512,1536]{1,0:T(8,128)(2,1)}, u32[]{:S(2)}) copy-start(bf16[512,1536]{1,0:T(8,128)(2,1)} %shard_map.112.w) | copy-start | bytes 4718596
  63.1 20.4 %copy-start.2 = (bf16[320,1024]{1,0:T(8,128)(2,1)}, bf16[320,1024]{1,0:T(8,128)(2,1)S(1)}, u32[]{:S(2)}) copy-start(bf16[320,1024]{1,0:T(8,128)(2,1)S(1)} %get-tuple-element.43.rows.near) | copy-start | bytes 1966084
  63.2 14.7 %collective-permute-start.7 = (bf16[320,1024]{1,0:T(8,128)(2,1)S(1)}, bf16[320,1024]{1,0:T(8,128)(2,1)S(1)}, u32[]{:S(2)}, u32[]{:S(2)}) collective-permute-start(bf16[320,1024]{1,0:T(8,128)(2,1)S(1)} %get-tuple-element.39), channel_id=1, source_target_pairs={{1,2},{2,1},{3,0},{0,3},{5,6},{6,5},{7,4},{4,7},{9,10},{10,9},{11,... | collective-permute-start | bytes 1966088 | tf_op jit(solution)/shard_map/ppermute | solution.py:249
  69.3 11.7 %collective-permute-start.9 = (bf16[160,3072]{1,0:T(8,128)(2,1)S(1)}, bf16[160,3072]{1,0:T(8,128)(2,1)S(1)}, u32[]{:S(2)}, u32[]{:S(2)}) collective-permute-start(bf16[160,3072]{1,0:T(8,128)(2,1)S(1)} %shard_map.113), channel_id=1, source_target_pairs={{0,64},{64,0},{1,65},{65,1},{2,66},{66,2},{3,67},{67,3},{4,68},{68... | collective-permute-start | bytes 2949128 | tf_op jit(solution)/shard_map/ppermute | solution.py:241
  79.0 4.5 %collective-permute-start.10 = (bf16[160,3072]{1,0:T(8,128)(2,1)S(1)}, bf16[160,3072]{1,0:T(8,128)(2,1)S(1)}, u32[]{:S(2)}, u32[]{:S(2)}) collective-permute-start(bf16[160,3072]{1,0:T(8,128)(2,1)S(1)} %shard_map.114), channel_id=1, source_target_pairs={{0,64},{64,0},{1,65},{65,1},{2,66},{66,2},{3,67},{67,3},{4,68},{68... | collective-permute-start | bytes 2949128 | tf_op jit(solution)/shard_map/ppermute | solution.py:241
  86.6 28.4 %all-to-all-start = ((bf16[4,80,3072]{2,1,0:T(8,128)(2,1)}), bf16[4,80,3072]{2,1,0:T(8,128)(2,1)}, u32[]{:S(2)}, u32[]{:S(2)}) async-start(bf16[4,80,3072]{2,1,0:T(8,128)(2,1)} %bitcast.24), calls=%async_computation | async-start | bytes 3932160 | tf_op jit(solution)/shard_map/all_to_all | solution.py:253
  145.2 6.0 %collective-permute-start.11 = (bf16[320,3200]{1,0:T(8,128)(2,1)S(1)}, bf16[320,3200]{1,0:T(8,128)(2,1)S(1)}, u32[]{:S(2)}, u32[]{:S(2)}) collective-permute-start(bf16[320,3200]{1,0:T(8,128)(2,1)S(1)} %bitcast.21), channel_id=1, source_target_pairs={{0,64},{64,0},{1,65},{65,1},{2,66},{66,2},{3,67},{67,3},{4,68},{68... | collective-permute-start | bytes 6144008 | tf_op jit(solution)/shard_map/ppermute | solution.py:241
  152.6 13.3 %collective-permute-start.13 = (bf16[320,512]{1,0:T(8,128)(2,1)S(1)}, bf16[320,512]{1,0:T(8,128)(2,1)S(1)}, u32[]{:S(2)}, u32[]{:S(2)}) collective-permute-start(bf16[320,512]{1,0:T(8,128)(2,1)S(1)} %shard_map.118), channel_id=1, source_target_pairs={{1,2},{2,1},{3,0},{0,3},{5,6},{6,5},{7,4},{4,7},{9,10},{10,9},{11,... | collective-permute-start | bytes 983048 | tf_op jit(solution)/shard_map/ppermute | solution.py:249
  162.5 45.0 %collective-permute-start.12 = (bf16[448,1536]{1,0:T(8,128)(2,1)S(1)}, bf16[448,1536]{1,0:T(8,128)(2,1)S(1)}, u32[]{:S(2)}, u32[]{:S(2)}) collective-permute-start(bf16[448,1536]{1,0:T(8,128)(2,1)S(1)} %get-tuple-element.46), channel_id=1, source_target_pairs={{0,1},{1,0},{2,3},{3,2},{4,5},{5,4},{6,7},{7,6},{8,9},{9,8},{10,11... | collective-permute-start | bytes 4128776 | tf_op jit(solution)/shard_map/ppermute | solution.py:245
  167.3 19.5 %collective-permute-start.18 = (bf16[40,512]{1,0:T(8,128)(2,1)S(1)}, bf16[40,512]{1,0:T(8,128)(2,1)S(1)}, u32[]{:S(2)}, u32[]{:S(2)}) collective-permute-start(bf16[40,512]{1,0:T(8,128)(2,1)S(1)} %get-tuple-element.52), channel_id=1, source_target_pairs={{52,0},{56,4},{60,8},{0,12},{4,16},{8,20},{12,24},{16,28},{20,32},... | collective-permute-start | bytes 122888 | tf_op jit(solution)/shard_map/ppermute | solution.py:237
  176.6 13.8 %collective-permute-start.14 = (bf16[120,512]{1,0:T(8,128)(2,1)S(1)}, bf16[120,512]{1,0:T(8,128)(2,1)S(1)}, u32[]{:S(2)}, u32[]{:S(2)}) collective-permute-start(bf16[120,512]{1,0:T(8,128)(2,1)S(1)} %get-tuple-element.48), channel_id=1, source_target_pairs={{60,0},{0,4},{4,8},{8,12},{12,16},{16,20},{20,24},{24,28},{28,32},... | collective-permute-start | bytes 368648 | tf_op jit(solution)/shard_map/ppermute | solution.py:237
  178.5 11.9 %collective-permute-start.15 = (bf16[120,512]{1,0:T(8,128)(2,1)S(1)}, bf16[120,512]{1,0:T(8,128)(2,1)S(1)}, u32[]{:S(2)}, u32[]{:S(2)}) collective-permute-start(bf16[120,512]{1,0:T(8,128)(2,1)S(1)} %get-tuple-element.49), channel_id=1, source_target_pairs={{56,0},{60,4},{0,8},{4,12},{8,16},{12,20},{16,24},{20,28},{24,32},... | collective-permute-start | bytes 368648 | tf_op jit(solution)/shard_map/ppermute | solution.py:237
  181.7 8.7 %collective-permute-start.16 = (bf16[120,512]{1,0:T(8,128)(2,1)S(1)}, bf16[120,512]{1,0:T(8,128)(2,1)S(1)}, u32[]{:S(2)}, u32[]{:S(2)}) collective-permute-start(bf16[120,512]{1,0:T(8,128)(2,1)S(1)} %get-tuple-element.50), channel_id=1, source_target_pairs={{4,0},{8,4},{12,8},{16,12},{20,16},{24,20},{28,24},{32,28},{36,32}... | collective-permute-start | bytes 368648 | tf_op jit(solution)/shard_map/ppermute | solution.py:237
  186.8 8.1 %collective-permute-start.17 = (bf16[120,512]{1,0:T(8,128)(2,1)S(1)}, bf16[120,512]{1,0:T(8,128)(2,1)S(1)}, u32[]{:S(2)}, u32[]{:S(2)}) collective-permute-start(bf16[120,512]{1,0:T(8,128)(2,1)S(1)} %get-tuple-element.51), channel_id=1, source_target_pairs={{8,0},{12,4},{16,8},{20,12},{24,16},{28,20},{32,24},{36,28},{40,32... | collective-permute-start | bytes 368648 | tf_op jit(solution)/shard_map/ppermute | solution.py:237
  195.6 13.7 %collective-permute-start.19 = (bf16[40,512]{1,0:T(8,128)(2,1)S(1)}, bf16[40,512]{1,0:T(8,128)(2,1)S(1)}, u32[]{:S(2)}, u32[]{:S(2)}) collective-permute-start(bf16[40,512]{1,0:T(8,128)(2,1)S(1)} %get-tuple-element.55), channel_id=1, source_target_pairs={{44,0},{48,4},{52,8},{56,12},{60,16},{0,20},{4,24},{8,28},{12,32},... | collective-permute-start | bytes 122888 | tf_op jit(solution)/shard_map/ppermute | solution.py:237
  197.9 12.1 %collective-permute-start.20 = (bf16[40,512]{1,0:T(8,128)(2,1)S(1)}, bf16[40,512]{1,0:T(8,128)(2,1)S(1)}, u32[]{:S(2)}, u32[]{:S(2)}) collective-permute-start(bf16[40,512]{1,0:T(8,128)(2,1)S(1)} %get-tuple-element.56), channel_id=1, source_target_pairs={{20,0},{24,4},{28,8},{32,12},{36,16},{40,20},{44,24},{48,28},{52,3... | collective-permute-start | bytes 122888 | tf_op jit(solution)/shard_map/ppermute | solution.py:237
  (9 other events, 40.1 us)

commit v5 on v4

--- a/solution.py
+++ b/solution.py
@@ -116,8 +116,8 @@
 def activate(sc, pieces, near_tile, far_tile, g_out):
     q = ROWS // 4
     start = pl.multiple_of((sc[3] % 2) * q, 16)
-    a = near_tile[pl.ds(start, q), :].astype(F32)
-    b = far_tile[pl.ds(start, q), :].astype(F32)
+    a = near_tile[pl.ds(start, q), 384:512].astype(F32)
+    b = far_tile[pl.ds(start, q), 384:512].astype(F32)
     tile = jnp.where(sc[3] < 2, a, b)
     lane = iota((q, 128), 1)
     scale = jnp.sum(jnp.where(lane == 96 + sc[0], tile, 0.0), axis=1, keepdims=True)
@@ -288,7 +288,7 @@
     q = ROWS // 4
     pieces = trade(pair.reshape(4, q, 3072), "x")
     (g_out,) = call(
-        activate, [((4, q, 3200), BF)], sc, pieces, near[:PART, 384:512], far[:PART, 384:512]
+        activate, [((4, q, 3200), BF)], sc, pieces, near, far
     )
     g = trade(g_out, "x").reshape(ROWS, 3200)
     g_far = swap_core(g)

time: 215 us -> 211 us (0.981)
  the two profiles are of different devices: /device:TPU:6 before, /device:TPU:40 now
where the time goes in v5:
time: 211 us; the launch traced here: 210 us
  starting transfers between devices  87.9 us (42%)
  blocking collectives  56.7 us (27%)
  waiting for transfers between devices  35.4 us (17%)
  Pallas kernels  23.5 us (11%)
  local copies, waits for them, and re-layouts  3.3 us (2%)
  other arithmetic  2.28 us (1%)
    ppermute x14, starting transfers between devices, take(): return lax.ppermute(a, axis, [((i + step) % n, i) for i in range(n)])  67 us
    all_to_all x2, blocking collectives, trade(): return lax.all_to_all(a, axis, split_axis=0, concat_axis=0, tiled=True)  56.7 us
    pallas_call x15, Pallas kernels, call(): pl.pallas_call(body, grid=(1,) if own_copies else (), out_shape=[jax.Shap...  23.5 us
    ppermute x14, waiting for transfers between devices, take(): return lax.ppermute(a, axis, [((i + step) % n, i) for i in range(n)])  20.2 us
    ppermute x2, waiting for transfers between devices, swap_expert(): return lax.ppermute(a, 'y', [(1, 2), (2, 1), (3, 0), (0, 3)])  10.1 us
    ppermute x2, starting transfers between devices, swap_half(): return lax.ppermute(a, 'y', [(0, 1), (1, 0), (2, 3), (3, 2)])  8.26 us
    ppermute x2, starting transfers between devices, swap_expert(): return lax.ppermute(a, 'y', [(1, 2), (2, 1), (3, 0), (0, 3)])  6.89 us
    ppermute x3, starting transfers between devices, swap_core(): return lax.ppermute(a, 'core', [(0, 1), (1, 0)])  5.75 us
  transfers between devices with their start and end apart: 21, of which 10 were waited for; matrix products, arithmetic and copies ran while one was open for 0% of the time, Pallas kernels for 8%

profile of v5, /device:TPU:40, one launch (start us, length us, event | category | flops | bytes accessed | tf_op | source)
XLA Modules:
  0.0 210.2 jit_solution(9852019373645102450)
XLA Ops:
  3.9 12.3 %collective-permute-start = (bf16[40,1024]{1,0:T(8,128)(2,1)S(1)}, bf16[40,1024]{1,0:T(8,128)(2,1)S(1)}, u32[]{:S(2)}, u32[]{:S(2)}) collective-permute-start(bf16[40,1024]{1,0:T(8,128)(2,1)S(1)} %shard_map.110), channel_id=1, source_target_pairs={{20,0},{24,4},{28,8},{32,12},{36,16},{40,20},{44,24},{48,28},{52,3... | collective-permute-start | bytes 245768 | tf_op jit(solution)/shard_map/ppermute | solution.py:237
  25.4 3.8 %collective-permute-done.1 = bf16[40,1024]{1,0:T(8,128)(2,1)S(1)} collective-permute-done((bf16[40,1024]{1,0:T(8,128)(2,1)S(1)}, bf16[40,1024]{1,0:T(8,128)(2,1)S(1)}, u32[]{:S(2)}, u32[]{:S(2)}) %collective-permute-start.1) | collective-permute-done | bytes 81952 | tf_op jit(solution)/shard_map/ppermute | solution.py:237
  29.1 9.3 %collective-permute-start.2 = (bf16[120,1024]{1,0:T(8,128)(2,1)S(1)}, bf16[120,1024]{1,0:T(8,128)(2,1)S(1)}, u32[]{:S(2)}, u32[]{:S(2)}) collective-permute-start(bf16[120,1024]{1,0:T(8,128)(2,1)S(1)} %get-tuple-element.69), channel_id=1, source_target_pairs={{4,0},{8,4},{12,8},{16,12},{20,16},{24,20},{28,24},{32,28},{36,32}... | collective-permute-start | bytes 737288 | tf_op jit(solution)/shard_map/ppermute | solution.py:237
  40.4 5.1 %collective-permute-start.4 = (bf16[120,1024]{1,0:T(8,128)(2,1)S(1)}, bf16[120,1024]{1,0:T(8,128)(2,1)S(1)}, u32[]{:S(2)}, u32[]{:S(2)}) collective-permute-start(bf16[120,1024]{1,0:T(8,128)(2,1)S(1)} %get-tuple-element.69), channel_id=1, source_target_pairs={{8,0},{12,4},{16,8},{20,12},{24,16},{28,20},{32,24},{36,28},{40,32... | collective-permute-start | bytes 737288 | tf_op jit(solution)/shard_map/ppermute | solution.py:237
  47.4 4.7 %collective-permute-start.6 = (bf16[40,1024]{1,0:T(8,128)(2,1)S(1)}, bf16[40,1024]{1,0:T(8,128)(2,1)S(1)}, u32[]{:S(2)}, u32[]{:S(2)}) collective-permute-start(bf16[40,1024]{1,0:T(8,128)(2,1)S(1)} %collective-permute-done), channel_id=1, source_target_pairs={{12,0},{16,4},{20,8},{24,12},{28,16},{32,20},{36,24},{40,28},{44,3... | collective-permute-start | bytes 245768 | tf_op jit(solution)/shard_map/ppermute | solution.py:237
  52.1 3.3 %collective-permute-done.4 = bf16[120,1024]{1,0:T(8,128)(2,1)S(1)} collective-permute-done((bf16[120,1024]{1,0:T(8,128)(2,1)S(1)}, bf16[120,1024]{1,0:T(8,128)(2,1)S(1)}, u32[]{:S(2)}, u32[]{:S(2)}) %collective-permute-start.4) | collective-permute-done | bytes 245792 | tf_op jit(solution)/shard_map/ppermute | solution.py:237
  56.6 2.4 %collective-permute-done.6 = bf16[40,1024]{1,0:T(8,128)(2,1)S(1)} collective-permute-done((bf16[40,1024]{1,0:T(8,128)(2,1)S(1)}, bf16[40,1024]{1,0:T(8,128)(2,1)S(1)}, u32[]{:S(2)}, u32[]{:S(2)}) %collective-permute-start.6) | collective-permute-done | bytes 81952 | tf_op jit(solution)/shard_map/ppermute | solution.py:237
  60.8 4.1 %collective-permute-start.7 = (bf16[320,1024]{1,0:T(8,128)(2,1)S(1)}, bf16[320,1024]{1,0:T(8,128)(2,1)S(1)}, u32[]{:S(2)}, u32[]{:S(2)}) collective-permute-start(bf16[320,1024]{1,0:T(8,128)(2,1)S(1)} %get-tuple-element.39), channel_id=1, source_target_pairs={{1,2},{2,1},{3,0},{0,3},{5,6},{6,5},{7,4},{4,7},{9,10},{10,9},{11,... | collective-permute-start | bytes 1966088 | tf_op jit(solution)/shard_map/ppermute | solution.py:249
  68.2 10.0 %collective-permute-done.7.rows.far.far_tile = bf16[320,1024]{1,0:T(8,128)(2,1)S(1)} collective-permute-done((bf16[320,1024]{1,0:T(8,128)(2,1)S(1)}, bf16[320,1024]{1,0:T(8,128)(2,1)S(1)}, u32[]{:S(2)}, u32[]{:S(2)}) %collective-permute-start.7) | collective-permute-done | bytes 655392 | tf_op jit(solution)/shard_map/ppermute | solution.py:249
  81.4 2.5 %collective-permute-done.10.got_far = bf16[160,3072]{1,0:T(8,128)(2,1)S(1)} collective-permute-done((bf16[160,3072]{1,0:T(8,128)(2,1)S(1)}, bf16[160,3072]{1,0:T(8,128)(2,1)S(1)}, u32[]{:S(2)}, u32[]{:S(2)}) %collective-permute-start.10) | collective-permute-done | bytes 983072 | tf_op jit(solution)/shard_map/ppermute | solution.py:241
  85.7 29.3 %all_to_all.10.pieces = bf16[4,80,3072]{2,1,0:T(8,128)(2,1)S(1)} all-to-all(bf16[4,80,3072]{2,1,0:T(8,128)(2,1)S(1)} %bitcast.24), channel_id=1, replica_groups=mesh['x'=4,'core'=2,'z'=16,'y'=4] {'x'}, dimensions={0} | all-to-all | bytes 3932160 | tf_op jit(solution)/shard_map/all_to_all | solution.py:253
  116.2 27.4 %all_to_all.11 = bf16[4,80,3200]{2,1,0:T(8,128)(2,1)S(1)} all-to-all(bf16[4,80,3200]{2,1,0:T(8,128)(2,1)S(1)} %shard_map.116), channel_id=1, replica_groups=mesh['x'=4,'core'=2,'z'=16,'y'=4] {'x'}, dimensions={0} | all-to-all | bytes 4096000 | tf_op jit(solution)/shard_map/all_to_all | solution.py:253
  147.0 2.6 %collective-permute-done.11.go = bf16[320,3200]{1,0:T(8,128)(2,1)S(1)} collective-permute-done((bf16[320,3200]{1,0:T(8,128)(2,1)S(1)}, bf16[320,3200]{1,0:T(8,128)(2,1)S(1)}, u32[]{:S(2)}, u32[]{:S(2)}) %collective-permute-start.11) | collective-permute-done | bytes 2048032 | tf_op jit(solution)/shard_map/ppermute | solution.py:241
  151.0 2.7 %collective-permute-start.13 = (bf16[320,512]{1,0:T(8,128)(2,1)S(1)}, bf16[320,512]{1,0:T(8,128)(2,1)S(1)}, u32[]{:S(2)}, u32[]{:S(2)}) collective-permute-start(bf16[320,512]{1,0:T(8,128)(2,1)S(1)} %shard_map.118), channel_id=1, source_target_pairs={{1,2},{2,1},{3,0},{0,3},{5,6},{6,5},{7,4},{4,7},{9,10},{10,9},{11,... | collective-permute-start | bytes 983048 | tf_op jit(solution)/shard_map/ppermute | solution.py:249
  153.8 4.1 %shard_map.119 = (f32[448,1536]{1,0:T(8,128)S(1)}, bf16[448,1536]{1,0:T(8,128)(2,1)S(1)}) custom-call(s32[4]{0:T(128)S(1)} %pad_add_fusion.sc, bf16[320,1024]{1,0:T(8,128)(2,1)S(1)} %get-tuple-element.43.rows.near.near_tile, bf16[320,1024]{1,0:T(8,128)(2,1)S(1)} %collective-permute-done.7.rows.far.far_tile, bf16[320,3200]{1,0:T(8,128)(2,1)S(1)} %bitcast.23, ...), custom_call_target="tpu_custom_call" | custom-call | flops 2013265920 | bytes 5406720 | tf_op jit(solution)/shard_map/pallas_call | solution.py:38
  157.9 5.9 %collective-permute-start.12 = (bf16[448,1536]{1,0:T(8,128)(2,1)S(1)}, bf16[448,1536]{1,0:T(8,128)(2,1)S(1)}, u32[]{:S(2)}, u32[]{:S(2)}) collective-permute-start(bf16[448,1536]{1,0:T(8,128)(2,1)S(1)} %get-tuple-element.46), channel_id=1, source_target_pairs={{0,1},{1,0},{2,3},{3,2},{4,5},{5,4},{6,7},{7,6},{8,9},{9,8},{10,11... | collective-permute-start | bytes 4128776 | tf_op jit(solution)/shard_map/ppermute | solution.py:245
  166.7 4.9 %collective-permute-start.18 = (bf16[40,512]{1,0:T(8,128)(2,1)S(1)}, bf16[40,512]{1,0:T(8,128)(2,1)S(1)}, u32[]{:S(2)}, u32[]{:S(2)}) collective-permute-start(bf16[40,512]{1,0:T(8,128)(2,1)S(1)} %get-tuple-element.52), channel_id=1, source_target_pairs={{52,0},{56,4},{60,8},{0,12},{4,16},{8,20},{12,24},{16,28},{20,32},... | collective-permute-start | bytes 122888 | tf_op jit(solution)/shard_map/ppermute | solution.py:237
  171.6 4.4 %collective-permute-start.14 = (bf16[120,512]{1,0:T(8,128)(2,1)S(1)}, bf16[120,512]{1,0:T(8,128)(2,1)S(1)}, u32[]{:S(2)}, u32[]{:S(2)}) collective-permute-start(bf16[120,512]{1,0:T(8,128)(2,1)S(1)} %get-tuple-element.48), channel_id=1, source_target_pairs={{60,0},{0,4},{4,8},{8,12},{12,16},{16,20},{20,24},{24,28},{28,32},... | collective-permute-start | bytes 368648 | tf_op jit(solution)/shard_map/ppermute | solution.py:237
  177.9 3.4 %collective-permute-start.16 = (bf16[120,512]{1,0:T(8,128)(2,1)S(1)}, bf16[120,512]{1,0:T(8,128)(2,1)S(1)}, u32[]{:S(2)}, u32[]{:S(2)}) collective-permute-start(bf16[120,512]{1,0:T(8,128)(2,1)S(1)} %get-tuple-element.50), channel_id=1, source_target_pairs={{4,0},{8,4},{12,8},{16,12},{20,16},{24,20},{28,24},{32,28},{36,32}... | collective-permute-start | bytes 368648 | tf_op jit(solution)/shard_map/ppermute | solution.py:237
  181.3 4.8 %collective-permute-start.17 = (bf16[120,512]{1,0:T(8,128)(2,1)S(1)}, bf16[120,512]{1,0:T(8,128)(2,1)S(1)}, u32[]{:S(2)}, u32[]{:S(2)}) collective-permute-start(bf16[120,512]{1,0:T(8,128)(2,1)S(1)} %get-tuple-element.51), channel_id=1, source_target_pairs={{8,0},{12,4},{16,8},{20,12},{24,16},{28,20},{32,24},{36,28},{40,32... | collective-permute-start | bytes 368648 | tf_op jit(solution)/shard_map/ppermute | solution.py:237
  186.7 4.4 %collective-permute-done.17.d = bf16[120,512]{1,0:T(8,128)(2,1)S(1)} collective-permute-done((bf16[120,512]{1,0:T(8,128)(2,1)S(1)}, bf16[120,512]{1,0:T(8,128)(2,1)S(1)}, u32[]{:S(2)}, u32[]{:S(2)}) %collective-permute-start.17) | collective-permute-done | bytes 122912 | tf_op jit(solution)/shard_map/ppermute | solution.py:237
  191.7 4.4 %collective-permute-start.19 = (bf16[40,512]{1,0:T(8,128)(2,1)S(1)}, bf16[40,512]{1,0:T(8,128)(2,1)S(1)}, u32[]{:S(2)}, u32[]{:S(2)}) collective-permute-start(bf16[40,512]{1,0:T(8,128)(2,1)S(1)} %get-tuple-element.55), channel_id=1, source_target_pairs={{44,0},{48,4},{52,8},{56,12},{60,16},{0,20},{4,24},{8,28},{12,32},... | collective-permute-start | bytes 122888 | tf_op jit(solution)/shard_map/ppermute | solution.py:237
  196.1 6.3 %collective-permute-start.20 = (bf16[40,512]{1,0:T(8,128)(2,1)S(1)}, bf16[40,512]{1,0:T(8,128)(2,1)S(1)}, u32[]{:S(2)}, u32[]{:S(2)}) collective-permute-start(bf16[40,512]{1,0:T(8,128)(2,1)S(1)} %get-tuple-element.56), channel_id=1, source_target_pairs={{20,0},{24,4},{28,8},{32,12},{36,16},{40,20},{44,24},{48,28},{52,3... | collective-permute-start | bytes 122888 | tf_op jit(solution)/shard_map/ppermute | solution.py:237
  204.2 4.7 %collective-permute-done.20.b = bf16[40,512]{1,0:T(8,128)(2,1)S(1)} collective-permute-done((bf16[40,512]{1,0:T(8,128)(2,1)S(1)}, bf16[40,512]{1,0:T(8,128)(2,1)S(1)}, u32[]{:S(2)}, u32[]{:S(2)}) %collective-permute-start.20) | collective-permute-done | bytes 40992 | tf_op jit(solution)/shard_map/ppermute | solution.py:237
  (61 shorter events, 42.6 us)
Async XLA Ops:
  3.9 21.5 %collective-permute-start = (bf16[40,1024]{1,0:T(8,128)(2,1)S(1)}, bf16[40,1024]{1,0:T(8,128)(2,1)S(1)}, u32[]{:S(2)}, u32[]{:S(2)}) collective-permute-start(bf16[40,1024]{1,0:T(8,128)(2,1)S(1)} %shard_map.110), channel_id=1, source_target_pairs={{20,0},{24,4},{28,8},{32,12},{36,16},{40,20},{44,24},{48,28},{52,3... | collective-permute-start | bytes 245768 | tf_op jit(solution)/shard_map/ppermute | solution.py:237
  16.2 13.0 %collective-permute-start.1 = (bf16[40,1024]{1,0:T(8,128)(2,1)S(1)}, bf16[40,1024]{1,0:T(8,128)(2,1)S(1)}, u32[]{:S(2)}, u32[]{:S(2)}) collective-permute-start(bf16[40,1024]{1,0:T(8,128)(2,1)S(1)} %shard_map.110), channel_id=1, source_target_pairs={{44,0},{48,4},{52,8},{56,12},{60,16},{0,20},{4,24},{8,28},{12,32},... | collective-permute-start | bytes 245768 | tf_op jit(solution)/shard_map/ppermute | solution.py:237
  18.1 1.0 copy-start.1
  23.0 42.0 %collective-permute-start.8 = (bf16[512,1536]{1,0:T(8,128)(2,1)}, bf16[512,1536]{1,0:T(8,128)(2,1)S(1)}, u32[]{:S(2)}, u32[]{:S(2)}) collective-permute-start(bf16[512,1536]{1,0:T(8,128)(2,1)} %shard_map.112.w), channel_id=1, source_target_pairs={{0,1},{1,0},{2,3},{3,2},{4,5},{5,4},{6,7},{7,6},{8,9},{9,8},{10,11... | collective-permute-start | bytes 4718600 | tf_op jit(solution)/shard_map/ppermute | solution.py:245
  29.1 18.2 %collective-permute-start.2 = (bf16[120,1024]{1,0:T(8,128)(2,1)S(1)}, bf16[120,1024]{1,0:T(8,128)(2,1)S(1)}, u32[]{:S(2)}, u32[]{:S(2)}) collective-permute-start(bf16[120,1024]{1,0:T(8,128)(2,1)S(1)} %get-tuple-element.69), channel_id=1, source_target_pairs={{4,0},{8,4},{12,8},{16,12},{20,16},{24,20},{28,24},{32,28},{36,32}... | collective-permute-start | bytes 737288 | tf_op jit(solution)/shard_map/ppermute | solution.py:237
  38.4 13.6 %collective-permute-start.3 = (bf16[120,1024]{1,0:T(8,128)(2,1)S(1)}, bf16[120,1024]{1,0:T(8,128)(2,1)S(1)}, u32[]{:S(2)}, u32[]{:S(2)}) collective-permute-start(bf16[120,1024]{1,0:T(8,128)(2,1)S(1)} %get-tuple-element.69), channel_id=1, source_target_pairs={{60,0},{0,4},{4,8},{8,12},{12,16},{16,20},{20,24},{24,28},{28,32},... | collective-permute-start | bytes 737288 | tf_op jit(solution)/shard_map/ppermute | solution.py:237
  40.4 15.0 %collective-permute-start.4 = (bf16[120,1024]{1,0:T(8,128)(2,1)S(1)}, bf16[120,1024]{1,0:T(8,128)(2,1)S(1)}, u32[]{:S(2)}, u32[]{:S(2)}) collective-permute-start(bf16[120,1024]{1,0:T(8,128)(2,1)S(1)} %get-tuple-element.69), channel_id=1, source_target_pairs={{8,0},{12,4},{16,8},{20,12},{24,16},{28,20},{32,24},{36,28},{40,32... | collective-permute-start | bytes 737288 | tf_op jit(solution)/shard_map/ppermute | solution.py:237
  45.4 11.1 %collective-permute-start.5 = (bf16[120,1024]{1,0:T(8,128)(2,1)S(1)}, bf16[120,1024]{1,0:T(8,128)(2,1)S(1)}, u32[]{:S(2)}, u32[]{:S(2)}) collective-permute-start(bf16[120,1024]{1,0:T(8,128)(2,1)S(1)} %get-tuple-element.69), channel_id=1, source_target_pairs={{56,0},{60,4},{0,8},{4,12},{8,16},{12,20},{16,24},{20,28},{24,32},... | collective-permute-start | bytes 737288 | tf_op jit(solution)/shard_map/ppermute | solution.py:237
  47.4 11.6 %collective-permute-start.6 = (bf16[40,1024]{1,0:T(8,128)(2,1)S(1)}, bf16[40,1024]{1,0:T(8,128)(2,1)S(1)}, u32[]{:S(2)}, u32[]{:S(2)}) collective-permute-start(bf16[40,1024]{1,0:T(8,128)(2,1)S(1)} %collective-permute-done), channel_id=1, source_target_pairs={{12,0},{16,4},{20,8},{24,12},{28,16},{32,20},{36,24},{40,28},{44,3... | collective-permute-start | bytes 245768 | tf_op jit(solution)/shard_map/ppermute | solution.py:237
  52.1 12.9 %copy-start = (bf16[512,1536]{1,0:T(8,128)(2,1)S(1)}, bf16[512,1536]{1,0:T(8,128)(2,1)}, u32[]{:S(2)}) copy-start(bf16[512,1536]{1,0:T(8,128)(2,1)} %shard_map.112.w) | copy-start | bytes 4718596
  60.8 17.4 %collective-permute-start.7 = (bf16[320,1024]{1,0:T(8,128)(2,1)S(1)}, bf16[320,1024]{1,0:T(8,128)(2,1)S(1)}, u32[]{:S(2)}, u32[]{:S(2)}) collective-permute-start(bf16[320,1024]{1,0:T(8,128)(2,1)S(1)} %get-tuple-element.39), channel_id=1, source_target_pairs={{1,2},{2,1},{3,0},{0,3},{5,6},{6,5},{7,4},{4,7},{9,10},{10,9},{11,... | collective-permute-start | bytes 1966088 | tf_op jit(solution)/shard_map/ppermute | solution.py:249
  66.2 15.1 %collective-permute-start.9 = (bf16[160,3072]{1,0:T(8,128)(2,1)S(1)}, bf16[160,3072]{1,0:T(8,128)(2,1)S(1)}, u32[]{:S(2)}, u32[]{:S(2)}) collective-permute-start(bf16[160,3072]{1,0:T(8,128)(2,1)S(1)} %shard_map.113), channel_id=1, source_target_pairs={{0,64},{64,0},{1,65},{65,1},{2,66},{66,2},{3,67},{67,3},{4,68},{68... | collective-permute-start | bytes 2949128 | tf_op jit(solution)/shard_map/ppermute | solution.py:241
  79.4 4.5 %collective-permute-start.10 = (bf16[160,3072]{1,0:T(8,128)(2,1)S(1)}, bf16[160,3072]{1,0:T(8,128)(2,1)S(1)}, u32[]{:S(2)}, u32[]{:S(2)}) collective-permute-start(bf16[160,3072]{1,0:T(8,128)(2,1)S(1)} %shard_map.114), channel_id=1, source_target_pairs={{0,64},{64,0},{1,65},{65,1},{2,66},{66,2},{3,67},{67,3},{4,68},{68... | collective-permute-start | bytes 2949128 | tf_op jit(solution)/shard_map/ppermute | solution.py:241
  143.6 6.0 %collective-permute-start.11 = (bf16[320,3200]{1,0:T(8,128)(2,1)S(1)}, bf16[320,3200]{1,0:T(8,128)(2,1)S(1)}, u32[]{:S(2)}, u32[]{:S(2)}) collective-permute-start(bf16[320,3200]{1,0:T(8,128)(2,1)S(1)} %bitcast.21), channel_id=1, source_target_pairs={{0,64},{64,0},{1,65},{65,1},{2,66},{66,2},{3,67},{67,3},{4,68},{68... | collective-permute-start | bytes 6144008 | tf_op jit(solution)/shard_map/ppermute | solution.py:241
  151.0 14.3 %collective-permute-start.13 = (bf16[320,512]{1,0:T(8,128)(2,1)S(1)}, bf16[320,512]{1,0:T(8,128)(2,1)S(1)}, u32[]{:S(2)}, u32[]{:S(2)}) collective-permute-start(bf16[320,512]{1,0:T(8,128)(2,1)S(1)} %shard_map.118), channel_id=1, source_target_pairs={{1,2},{2,1},{3,0},{0,3},{5,6},{6,5},{7,4},{4,7},{9,10},{10,9},{11,... | collective-permute-start | bytes 983048 | tf_op jit(solution)/shard_map/ppermute | solution.py:249
  157.9 44.5 %collective-permute-start.12 = (bf16[448,1536]{1,0:T(8,128)(2,1)S(1)}, bf16[448,1536]{1,0:T(8,128)(2,1)S(1)}, u32[]{:S(2)}, u32[]{:S(2)}) collective-permute-start(bf16[448,1536]{1,0:T(8,128)(2,1)S(1)} %get-tuple-element.46), channel_id=1, source_target_pairs={{0,1},{1,0},{2,3},{3,2},{4,5},{5,4},{6,7},{7,6},{8,9},{9,8},{10,11... | collective-permute-start | bytes 4128776 | tf_op jit(solution)/shard_map/ppermute | solution.py:245
  166.7 14.6 %collective-permute-start.18 = (bf16[40,512]{1,0:T(8,128)(2,1)S(1)}, bf16[40,512]{1,0:T(8,128)(2,1)S(1)}, u32[]{:S(2)}, u32[]{:S(2)}) collective-permute-start(bf16[40,512]{1,0:T(8,128)(2,1)S(1)} %get-tuple-element.52), channel_id=1, source_target_pairs={{52,0},{56,4},{60,8},{0,12},{4,16},{8,20},{12,24},{16,28},{20,32},... | collective-permute-start | bytes 122888 | tf_op jit(solution)/shard_map/ppermute | solution.py:237
  171.6 14.5 %collective-permute-start.14 = (bf16[120,512]{1,0:T(8,128)(2,1)S(1)}, bf16[120,512]{1,0:T(8,128)(2,1)S(1)}, u32[]{:S(2)}, u32[]{:S(2)}) collective-permute-start(bf16[120,512]{1,0:T(8,128)(2,1)S(1)} %get-tuple-element.48), channel_id=1, source_target_pairs={{60,0},{0,4},{4,8},{8,12},{12,16},{16,20},{20,24},{24,28},{28,32},... | collective-permute-start | bytes 368648 | tf_op jit(solution)/shard_map/ppermute | solution.py:237
  176.0 10.8 %collective-permute-start.15 = (bf16[120,512]{1,0:T(8,128)(2,1)S(1)}, bf16[120,512]{1,0:T(8,128)(2,1)S(1)}, u32[]{:S(2)}, u32[]{:S(2)}) collective-permute-start(bf16[120,512]{1,0:T(8,128)(2,1)S(1)} %get-tuple-element.49), channel_id=1, source_target_pairs={{56,0},{60,4},{0,8},{4,12},{8,16},{12,20},{16,24},{20,28},{24,32},... | collective-permute-start | bytes 368648 | tf_op jit(solution)/shard_map/ppermute | solution.py:237
  177.9 8.8 %collective-permute-start.16 = (bf16[120,512]{1,0:T(8,128)(2,1)S(1)}, bf16[120,512]{1,0:T(8,128)(2,1)S(1)}, u32[]{:S(2)}, u32[]{:S(2)}) collective-permute-start(bf16[120,512]{1,0:T(8,128)(2,1)S(1)} %get-tuple-element.50), channel_id=1, source_target_pairs={{4,0},{8,4},{12,8},{16,12},{20,16},{24,20},{28,24},{32,28},{36,32}... | collective-permute-start | bytes 368648 | tf_op jit(solution)/shard_map/ppermute | solution.py:237
  181.3 9.8 %collective-permute-start.17 = (bf16[120,512]{1,0:T(8,128)(2,1)S(1)}, bf16[120,512]{1,0:T(8,128)(2,1)S(1)}, u32[]{:S(2)}, u32[]{:S(2)}) collective-permute-start(bf16[120,512]{1,0:T(8,128)(2,1)S(1)} %get-tuple-element.51), channel_id=1, source_target_pairs={{8,0},{12,4},{16,8},{20,12},{24,16},{28,20},{32,24},{36,28},{40,32... | collective-permute-start | bytes 368648 | tf_op jit(solution)/shard_map/ppermute | solution.py:237
  191.7 12.5 %collective-permute-start.19 = (bf16[40,512]{1,0:T(8,128)(2,1)S(1)}, bf16[40,512]{1,0:T(8,128)(2,1)S(1)}, u32[]{:S(2)}, u32[]{:S(2)}) collective-permute-start(bf16[40,512]{1,0:T(8,128)(2,1)S(1)} %get-tuple-element.55), channel_id=1, source_target_pairs={{44,0},{48,4},{52,8},{56,12},{60,16},{0,20},{4,24},{8,28},{12,32},... | collective-permute-start | bytes 122888 | tf_op jit(solution)/shard_map/ppermute | solution.py:237
  196.1 12.8 %collective-permute-start.20 = (bf16[40,512]{1,0:T(8,128)(2,1)S(1)}, bf16[40,512]{1,0:T(8,128)(2,1)S(1)}, u32[]{:S(2)}, u32[]{:S(2)}) collective-permute-start(bf16[40,512]{1,0:T(8,128)(2,1)S(1)} %get-tuple-element.56), channel_id=1, source_target_pairs={{20,0},{24,4},{28,8},{32,12},{36,16},{40,20},{44,24},{48,28},{52,3... | collective-permute-start | bytes 122888 | tf_op jit(solution)/shard_map/ppermute | solution.py:237
  202.4 6.5 %copy-start.4 = (s32[40,8]{0,1:T(8,128)S(1)}, s32[40,8]{0,1:T(8,128)}, u32[]{:S(2)}) copy-start(s32[40,8]{0,1:T(8,128)} %param.9) | copy-start | bytes 3844
  (2 other events, 2.0 us)

commit v6 on v5

--- a/solution.py
+++ b/solution.py
@@ -82,16 +82,16 @@
     return jnp.where(code > 0.5, place, -1)
 
 
-def choose(sc, every, near, send):
-    lanes = iota((8, 128), 1) - 64
-    row = iota((8, 128), 0)
-    sel = ((row == 0) & (lanes == sc[0])) | ((row == 1) & (lanes == sc[1]))
-    codes = dot(sel.astype(BF), every[:, 384:512], LAST)
-    block = (iota((1, ALL), 1) * 1639) >> 16
-    for k, out in ((0, near), (1, send)):
-        place = placed(codes[k : k + 1, :], block, sc[2])
+def choose(k):
+    def body(sc, every, out):
+        lanes = iota((8, 128), 1) - 64
+        codes = dot((lanes == sc[k]).astype(BF), every[:, 384:512], LAST)
+        block = (iota((1, ALL), 1) * 1639) >> 16
+        place = placed(codes[0:1, :], block, sc[2])
         one_hot = (iota((ROWS, ALL), 0) == place).astype(BF)
         out[...] = dot(one_hot, every[...]).astype(BF)
+
+    return body
 
 
 def products(rows, w, wf, lo):
@@ -273,9 +273,10 @@
     eight = take(five, "z", 3)
     w_far = swap_half(w)
     every = jnp.concatenate([group] + near_z + [eight], 0)
-    near, send = call(
-        choose, [((ROWS, 1024), BF)] * 2, sc, every, flops=0
-    )
+    picked = [((ROWS, 1024), BF)]
+    (send,) = call(choose(1), picked, sc, every)
+    later, send = lax.optimization_barrier((every, send))
+    (near,) = call(choose(0), picked, sc, later)
     far = swap_expert(send)
     flops = 2 * PART * WIDE * 3072
     out = [((PART, 3072), BF)]

time: 211 us -> 210 us (level)
  the two profiles are of different devices: /device:TPU:40 before, /device:TPU:6 now
where the time goes in v6:
time: 210 us; the launch traced here: 206 us
  starting transfers between devices  88 us (42%)
  blocking collectives  55.1 us (26%)
  waiting for transfers between devices  32.3 us (15%)
  Pallas kernels  24.4 us (12%)
  local copies, waits for them, and re-layouts  3.3 us (2%)
  other arithmetic  2.28 us (1%)
    ppermute x14, starting transfers between devices, take(): return lax.ppermute(a, axis, [((i + step) % n, i) for i in range(n)])  67 us
    all_to_all x2, blocking collectives, trade(): return lax.all_to_all(a, axis, split_axis=0, concat_axis=0, tiled=True)  55.1 us
    pallas_call x16, Pallas kernels, call(): pl.pallas_call(body, grid=(1,) if own_copies else (), out_shape=[jax.Shap...  24.4 us
    ppermute x14, waiting for transfers between devices, take(): return lax.ppermute(a, axis, [((i + step) % n, i) for i in range(n)])  21.5 us
    ppermute x2, starting transfers between devices, swap_expert(): return lax.ppermute(a, 'y', [(1, 2), (2, 1), (3, 0), (0, 3)])  9.9 us
    ppermute x3, starting transfers between devices, swap_core(): return lax.ppermute(a, 'core', [(0, 1), (1, 0)])  5.75 us
    ppermute x2, waiting for transfers between devices, swap_expert(): return lax.ppermute(a, 'y', [(1, 2), (2, 1), (3, 0), (0, 3)])  5.67 us
    ppermute x2, starting transfers between devices, swap_half(): return lax.ppermute(a, 'y', [(0, 1), (1, 0), (2, 3), (3, 2)])  5.39 us
  transfers between devices with their start and end apart: 21, of which 10 were waited for; matrix products, arithmetic and copies ran while one was open for 0% of the time, Pallas kernels for 9%

profile of v6, /device:TPU:6, one launch (start us, length us, event | category | flops | bytes accessed | tf_op | source)
XLA Modules:
  0.0 206.4 jit_solution(8493533714592711907)
XLA Ops:
  3.9 14.4 %collective-permute-start = (bf16[40,1024]{1,0:T(8,128)(2,1)S(1)}, bf16[40,1024]{1,0:T(8,128)(2,1)S(1)}, u32[]{:S(2)}, u32[]{:S(2)}) collective-permute-start(bf16[40,1024]{1,0:T(8,128)(2,1)S(1)} %shard_map.110), channel_id=1, source_target_pairs={{20,0},{24,4},{28,8},{32,12},{36,16},{40,20},{44,24},{48,28},{52,3... | collective-permute-start | bytes 245768 | tf_op jit(solution)/shard_map/ppermute | solution.py:237
  25.1 3.5 %collective-permute-start.8 = (bf16[512,1536]{1,0:T(8,128)(2,1)}, bf16[512,1536]{1,0:T(8,128)(2,1)S(1)}, u32[]{:S(2)}, u32[]{:S(2)}) collective-permute-start(bf16[512,1536]{1,0:T(8,128)(2,1)} %shard_map.113.w), channel_id=1, source_target_pairs={{0,1},{1,0},{2,3},{3,2},{4,5},{5,4},{6,7},{7,6},{8,9},{9,8},{10,11... | collective-permute-start | bytes 4718600 | tf_op jit(solution)/shard_map/ppermute | solution.py:245
  28.6 7.8 %collective-permute-done.1 = bf16[40,1024]{1,0:T(8,128)(2,1)S(1)} collective-permute-done((bf16[40,1024]{1,0:T(8,128)(2,1)S(1)}, bf16[40,1024]{1,0:T(8,128)(2,1)S(1)}, u32[]{:S(2)}, u32[]{:S(2)}) %collective-permute-start.1) | collective-permute-done | bytes 81952 | tf_op jit(solution)/shard_map/ppermute | solution.py:237
  36.4 2.4 %collective-permute-start.2 = (bf16[120,1024]{1,0:T(8,128)(2,1)S(1)}, bf16[120,1024]{1,0:T(8,128)(2,1)S(1)}, u32[]{:S(2)}, u32[]{:S(2)}) collective-permute-start(bf16[120,1024]{1,0:T(8,128)(2,1)S(1)} %get-tuple-element.69), channel_id=1, source_target_pairs={{4,0},{8,4},{12,8},{16,12},{20,16},{24,20},{28,24},{32,28},{36,32}... | collective-permute-start | bytes 737288 | tf_op jit(solution)/shard_map/ppermute | solution.py:237
  38.8 3.4 %collective-permute-start.3 = (bf16[120,1024]{1,0:T(8,128)(2,1)S(1)}, bf16[120,1024]{1,0:T(8,128)(2,1)S(1)}, u32[]{:S(2)}, u32[]{:S(2)}) collective-permute-start(bf16[120,1024]{1,0:T(8,128)(2,1)S(1)} %get-tuple-element.69), channel_id=1, source_target_pairs={{60,0},{0,4},{4,8},{8,12},{12,16},{16,20},{20,24},{24,28},{28,32},... | collective-permute-start | bytes 737288 | tf_op jit(solution)/shard_map/ppermute | solution.py:237
  42.3 2.2 %collective-permute-start.4 = (bf16[120,1024]{1,0:T(8,128)(2,1)S(1)}, bf16[120,1024]{1,0:T(8,128)(2,1)S(1)}, u32[]{:S(2)}, u32[]{:S(2)}) collective-permute-start(bf16[120,1024]{1,0:T(8,128)(2,1)S(1)} %get-tuple-element.69), channel_id=1, source_target_pairs={{8,0},{12,4},{16,8},{20,12},{24,16},{28,20},{32,24},{36,28},{40,32... | collective-permute-start | bytes 737288 | tf_op jit(solution)/shard_map/ppermute | solution.py:237
  44.5 4.5 %collective-permute-start.5 = (bf16[120,1024]{1,0:T(8,128)(2,1)S(1)}, bf16[120,1024]{1,0:T(8,128)(2,1)S(1)}, u32[]{:S(2)}, u32[]{:S(2)}) collective-permute-start(bf16[120,1024]{1,0:T(8,128)(2,1)S(1)} %get-tuple-element.69), channel_id=1, source_target_pairs={{56,0},{60,4},{0,8},{4,12},{8,16},{12,20},{16,24},{20,28},{24,32},... | collective-permute-start | bytes 737288 | tf_op jit(solution)/shard_map/ppermute | solution.py:237
  49.0 3.1 %collective-permute-start.6 = (bf16[40,1024]{1,0:T(8,128)(2,1)S(1)}, bf16[40,1024]{1,0:T(8,128)(2,1)S(1)}, u32[]{:S(2)}, u32[]{:S(2)}) collective-permute-start(bf16[40,1024]{1,0:T(8,128)(2,1)S(1)} %collective-permute-done), channel_id=1, source_target_pairs={{12,0},{16,4},{20,8},{24,12},{28,16},{32,20},{36,24},{40,28},{44,3... | collective-permute-start | bytes 245768 | tf_op jit(solution)/shard_map/ppermute | solution.py:237
  52.2 7.6 %collective-permute-done.5 = bf16[120,1024]{1,0:T(8,128)(2,1)S(1)} collective-permute-done((bf16[120,1024]{1,0:T(8,128)(2,1)S(1)}, bf16[120,1024]{1,0:T(8,128)(2,1)S(1)}, u32[]{:S(2)}, u32[]{:S(2)}) %collective-permute-start.5) | collective-permute-done | bytes 245792 | tf_op jit(solution)/shard_map/ppermute | solution.py:237
  62.6 5.1 %collective-permute-start.7 = (bf16[320,1024]{1,0:T(8,128)(2,1)S(1)}, bf16[320,1024]{1,0:T(8,128)(2,1)S(1)}, u32[]{:S(2)}, u32[]{:S(2)}) collective-permute-start(bf16[320,1024]{1,0:T(8,128)(2,1)S(1)} %shard_map.111), channel_id=1, source_target_pairs={{1,2},{2,1},{3,0},{0,3},{5,6},{6,5},{7,4},{4,7},{9,10},{10,9},{11,... | collective-permute-start | bytes 1966088 | tf_op jit(solution)/shard_map/ppermute | solution.py:249
  72.2 5.2 %collective-permute-done.7.rows.far.far_tile = bf16[320,1024]{1,0:T(8,128)(2,1)S(1)} collective-permute-done((bf16[320,1024]{1,0:T(8,128)(2,1)S(1)}, bf16[320,1024]{1,0:T(8,128)(2,1)S(1)}, u32[]{:S(2)}, u32[]{:S(2)}) %collective-permute-start.7) | collective-permute-done | bytes 655392 | tf_op jit(solution)/shard_map/ppermute | solution.py:249
  80.6 2.5 %collective-permute-done.10.got_far = bf16[160,3072]{1,0:T(8,128)(2,1)S(1)} collective-permute-done((bf16[160,3072]{1,0:T(8,128)(2,1)S(1)}, bf16[160,3072]{1,0:T(8,128)(2,1)S(1)}, u32[]{:S(2)}, u32[]{:S(2)}) %collective-permute-start.10) | collective-permute-done | bytes 983072 | tf_op jit(solution)/shard_map/ppermute | solution.py:241
  84.9 27.7 %all_to_all.10.pieces = bf16[4,80,3072]{2,1,0:T(8,128)(2,1)S(1)} all-to-all(bf16[4,80,3072]{2,1,0:T(8,128)(2,1)S(1)} %bitcast.24), channel_id=1, replica_groups=mesh['x'=4,'core'=2,'z'=16,'y'=4] {'x'}, dimensions={0} | all-to-all | bytes 3932160 | tf_op jit(solution)/shard_map/all_to_all | solution.py:253
  113.8 27.4 %all_to_all.11 = bf16[4,80,3200]{2,1,0:T(8,128)(2,1)S(1)} all-to-all(bf16[4,80,3200]{2,1,0:T(8,128)(2,1)S(1)} %shard_map.117), channel_id=1, replica_groups=mesh['x'=4,'core'=2,'z'=16,'y'=4] {'x'}, dimensions={0} | all-to-all | bytes 4096000 | tf_op jit(solution)/shard_map/all_to_all | solution.py:253
  144.6 2.6 %collective-permute-done.11.go = bf16[320,3200]{1,0:T(8,128)(2,1)S(1)} collective-permute-done((bf16[320,3200]{1,0:T(8,128)(2,1)S(1)}, bf16[320,3200]{1,0:T(8,128)(2,1)S(1)}, u32[]{:S(2)}, u32[]{:S(2)}) %collective-permute-start.11) | collective-permute-done | bytes 2048032 | tf_op jit(solution)/shard_map/ppermute | solution.py:241
  148.6 4.8 %collective-permute-start.13 = (bf16[320,512]{1,0:T(8,128)(2,1)S(1)}, bf16[320,512]{1,0:T(8,128)(2,1)S(1)}, u32[]{:S(2)}, u32[]{:S(2)}) collective-permute-start(bf16[320,512]{1,0:T(8,128)(2,1)S(1)} %shard_map.119), channel_id=1, source_target_pairs={{1,2},{2,1},{3,0},{0,3},{5,6},{6,5},{7,4},{4,7},{9,10},{10,9},{11,... | collective-permute-start | bytes 983048 | tf_op jit(solution)/shard_map/ppermute | solution.py:249
  153.5 4.1 %shard_map.120 = (f32[448,1536]{1,0:T(8,128)S(1)}, bf16[448,1536]{1,0:T(8,128)(2,1)S(1)}) custom-call(s32[4]{0:T(128)S(1)} %pad_add_fusion.sc, bf16[320,1024]{1,0:T(8,128)(2,1)S(1)} %shard_map.112.rows.near.near_tile, bf16[320,1024]{1,0:T(8,128)(2,1)S(1)} %collective-permute-done.7.rows.far.far_tile, bf16[320,3200]{1,0:T(8,128)(2,1)S(1)} %bitcast.23, ...), custom_call_target="tpu_custom_call" | custom-call | flops 2013265920 | bytes 5406720 | tf_op jit(solution)/shard_map/pallas_call | solution.py:38
  162.9 9.4 %collective-permute-start.18 = (bf16[40,512]{1,0:T(8,128)(2,1)S(1)}, bf16[40,512]{1,0:T(8,128)(2,1)S(1)}, u32[]{:S(2)}, u32[]{:S(2)}) collective-permute-start(bf16[40,512]{1,0:T(8,128)(2,1)S(1)} %get-tuple-element.52), channel_id=1, source_target_pairs={{52,0},{56,4},{60,8},{0,12},{4,16},{8,20},{12,24},{16,28},{20,32},... | collective-permute-start | bytes 122888 | tf_op jit(solution)/shard_map/ppermute | solution.py:237
  174.2 3.1 %collective-permute-start.15 = (bf16[120,512]{1,0:T(8,128)(2,1)S(1)}, bf16[120,512]{1,0:T(8,128)(2,1)S(1)}, u32[]{:S(2)}, u32[]{:S(2)}) collective-permute-start(bf16[120,512]{1,0:T(8,128)(2,1)S(1)} %get-tuple-element.49), channel_id=1, source_target_pairs={{56,0},{60,4},{0,8},{4,12},{8,16},{12,20},{16,24},{20,28},{24,32},... | collective-permute-start | bytes 368648 | tf_op jit(solution)/shard_map/ppermute | solution.py:237
  177.3 5.1 %collective-permute-start.16 = (bf16[120,512]{1,0:T(8,128)(2,1)S(1)}, bf16[120,512]{1,0:T(8,128)(2,1)S(1)}, u32[]{:S(2)}, u32[]{:S(2)}) collective-permute-start(bf16[120,512]{1,0:T(8,128)(2,1)S(1)} %get-tuple-element.50), channel_id=1, source_target_pairs={{4,0},{8,4},{12,8},{16,12},{20,16},{24,20},{28,24},{32,28},{36,32}... | collective-permute-start | bytes 368648 | tf_op jit(solution)/shard_map/ppermute | solution.py:237
  182.4 3.6 %collective-permute-start.17 = (bf16[120,512]{1,0:T(8,128)(2,1)S(1)}, bf16[120,512]{1,0:T(8,128)(2,1)S(1)}, u32[]{:S(2)}, u32[]{:S(2)}) collective-permute-start(bf16[120,512]{1,0:T(8,128)(2,1)S(1)} %get-tuple-element.51), channel_id=1, source_target_pairs={{8,0},{12,4},{16,8},{20,12},{24,16},{28,20},{32,24},{36,28},{40,32... | collective-permute-start | bytes 368648 | tf_op jit(solution)/shard_map/ppermute | solution.py:237
  186.5 3.8 %collective-permute-done.17.d = bf16[120,512]{1,0:T(8,128)(2,1)S(1)} collective-permute-done((bf16[120,512]{1,0:T(8,128)(2,1)S(1)}, bf16[120,512]{1,0:T(8,128)(2,1)S(1)}, u32[]{:S(2)}, u32[]{:S(2)}) %collective-permute-start.17) | collective-permute-done | bytes 122912 | tf_op jit(solution)/shard_map/ppermute | solution.py:237
  191.0 2.1 %collective-permute-start.19 = (bf16[40,512]{1,0:T(8,128)(2,1)S(1)}, bf16[40,512]{1,0:T(8,128)(2,1)S(1)}, u32[]{:S(2)}, u32[]{:S(2)}) collective-permute-start(bf16[40,512]{1,0:T(8,128)(2,1)S(1)} %get-tuple-element.55), channel_id=1, source_target_pairs={{44,0},{48,4},{52,8},{56,12},{60,16},{0,20},{4,24},{8,28},{12,32},... | collective-permute-start | bytes 122888 | tf_op jit(solution)/shard_map/ppermute | solution.py:237
  193.1 9.8 %collective-permute-start.20 = (bf16[40,512]{1,0:T(8,128)(2,1)S(1)}, bf16[40,512]{1,0:T(8,128)(2,1)S(1)}, u32[]{:S(2)}, u32[]{:S(2)}) collective-permute-start(bf16[40,512]{1,0:T(8,128)(2,1)S(1)} %get-tuple-element.56), channel_id=1, source_target_pairs={{20,0},{24,4},{28,8},{32,12},{36,16},{40,20},{44,24},{48,28},{52,3... | collective-permute-start | bytes 122888 | tf_op jit(solution)/shard_map/ppermute | solution.py:237
  (62 shorter events, 40.2 us)
Async XLA Ops:
  3.9 24.7 %collective-permute-start = (bf16[40,1024]{1,0:T(8,128)(2,1)S(1)}, bf16[40,1024]{1,0:T(8,128)(2,1)S(1)}, u32[]{:S(2)}, u32[]{:S(2)}) collective-permute-start(bf16[40,1024]{1,0:T(8,128)(2,1)S(1)} %shard_map.110), channel_id=1, source_target_pairs={{20,0},{24,4},{28,8},{32,12},{36,16},{40,20},{44,24},{48,28},{52,3... | collective-permute-start | bytes 245768 | tf_op jit(solution)/shard_map/ppermute | solution.py:237
  18.3 18.1 %collective-permute-start.1 = (bf16[40,1024]{1,0:T(8,128)(2,1)S(1)}, bf16[40,1024]{1,0:T(8,128)(2,1)S(1)}, u32[]{:S(2)}, u32[]{:S(2)}) collective-permute-start(bf16[40,1024]{1,0:T(8,128)(2,1)S(1)} %shard_map.110), channel_id=1, source_target_pairs={{44,0},{48,4},{52,8},{56,12},{60,16},{0,20},{4,24},{8,28},{12,32},... | collective-permute-start | bytes 245768 | tf_op jit(solution)/shard_map/ppermute | solution.py:237
  20.2 1.0 copy-start.1
  25.1 44.0 %collective-permute-start.8 = (bf16[512,1536]{1,0:T(8,128)(2,1)}, bf16[512,1536]{1,0:T(8,128)(2,1)S(1)}, u32[]{:S(2)}, u32[]{:S(2)}) collective-permute-start(bf16[512,1536]{1,0:T(8,128)(2,1)} %shard_map.113.w), channel_id=1, source_target_pairs={{0,1},{1,0},{2,3},{3,2},{4,5},{5,4},{6,7},{7,6},{8,9},{9,8},{10,11... | collective-permute-start | bytes 4718600 | tf_op jit(solution)/shard_map/ppermute | solution.py:245
  36.4 12.6 %collective-permute-start.2 = (bf16[120,1024]{1,0:T(8,128)(2,1)S(1)}, bf16[120,1024]{1,0:T(8,128)(2,1)S(1)}, u32[]{:S(2)}, u32[]{:S(2)}) collective-permute-start(bf16[120,1024]{1,0:T(8,128)(2,1)S(1)} %get-tuple-element.69), channel_id=1, source_target_pairs={{4,0},{8,4},{12,8},{16,12},{20,16},{24,20},{28,24},{32,28},{36,32}... | collective-permute-start | bytes 737288 | tf_op jit(solution)/shard_map/ppermute | solution.py:237
  38.8 13.3 %collective-permute-start.3 = (bf16[120,1024]{1,0:T(8,128)(2,1)S(1)}, bf16[120,1024]{1,0:T(8,128)(2,1)S(1)}, u32[]{:S(2)}, u32[]{:S(2)}) collective-permute-start(bf16[120,1024]{1,0:T(8,128)(2,1)S(1)} %get-tuple-element.69), channel_id=1, source_target_pairs={{60,0},{0,4},{4,8},{8,12},{12,16},{16,20},{20,24},{24,28},{28,32},... | collective-permute-start | bytes 737288 | tf_op jit(solution)/shard_map/ppermute | solution.py:237
  42.3 9.9 %collective-permute-start.4 = (bf16[120,1024]{1,0:T(8,128)(2,1)S(1)}, bf16[120,1024]{1,0:T(8,128)(2,1)S(1)}, u32[]{:S(2)}, u32[]{:S(2)}) collective-permute-start(bf16[120,1024]{1,0:T(8,128)(2,1)S(1)} %get-tuple-element.69), channel_id=1, source_target_pairs={{8,0},{12,4},{16,8},{20,12},{24,16},{28,20},{32,24},{36,28},{40,32... | collective-permute-start | bytes 737288 | tf_op jit(solution)/shard_map/ppermute | solution.py:237
  44.5 15.3 %collective-permute-start.5 = (bf16[120,1024]{1,0:T(8,128)(2,1)S(1)}, bf16[120,1024]{1,0:T(8,128)(2,1)S(1)}, u32[]{:S(2)}, u32[]{:S(2)}) collective-permute-start(bf16[120,1024]{1,0:T(8,128)(2,1)S(1)} %get-tuple-element.69), channel_id=1, source_target_pairs={{56,0},{60,4},{0,8},{4,12},{8,16},{12,20},{16,24},{20,28},{24,32},... | collective-permute-start | bytes 737288 | tf_op jit(solution)/shard_map/ppermute | solution.py:237
  49.0 12.2 %collective-permute-start.6 = (bf16[40,1024]{1,0:T(8,128)(2,1)S(1)}, bf16[40,1024]{1,0:T(8,128)(2,1)S(1)}, u32[]{:S(2)}, u32[]{:S(2)}) collective-permute-start(bf16[40,1024]{1,0:T(8,128)(2,1)S(1)} %collective-permute-done), channel_id=1, source_target_pairs={{12,0},{16,4},{20,8},{24,12},{28,16},{32,20},{36,24},{40,28},{44,3... | collective-permute-start | bytes 245768 | tf_op jit(solution)/shard_map/ppermute | solution.py:237
  62.6 6.4 %copy-start = (bf16[512,1536]{1,0:T(8,128)(2,1)S(1)}, bf16[512,1536]{1,0:T(8,128)(2,1)}, u32[]{:S(2)}) copy-start(bf16[512,1536]{1,0:T(8,128)(2,1)} %shard_map.113.w) | copy-start | bytes 4718596
  62.6 14.8 %collective-permute-start.7 = (bf16[320,1024]{1,0:T(8,128)(2,1)S(1)}, bf16[320,1024]{1,0:T(8,128)(2,1)S(1)}, u32[]{:S(2)}, u32[]{:S(2)}) collective-permute-start(bf16[320,1024]{1,0:T(8,128)(2,1)S(1)} %shard_map.111), channel_id=1, source_target_pairs={{1,2},{2,1},{3,0},{0,3},{5,6},{6,5},{7,4},{4,7},{9,10},{10,9},{11,... | collective-permute-start | bytes 1966088 | tf_op jit(solution)/shard_map/ppermute | solution.py:249
  70.3 10.3 %collective-permute-start.9 = (bf16[160,3072]{1,0:T(8,128)(2,1)S(1)}, bf16[160,3072]{1,0:T(8,128)(2,1)S(1)}, u32[]{:S(2)}, u32[]{:S(2)}) collective-permute-start(bf16[160,3072]{1,0:T(8,128)(2,1)S(1)} %shard_map.114), channel_id=1, source_target_pairs={{0,64},{64,0},{1,65},{65,1},{2,66},{66,2},{3,67},{67,3},{4,68},{68... | collective-permute-start | bytes 2949128 | tf_op jit(solution)/shard_map/ppermute | solution.py:241
  78.6 4.5 %collective-permute-start.10 = (bf16[160,3072]{1,0:T(8,128)(2,1)S(1)}, bf16[160,3072]{1,0:T(8,128)(2,1)S(1)}, u32[]{:S(2)}, u32[]{:S(2)}) collective-permute-start(bf16[160,3072]{1,0:T(8,128)(2,1)S(1)} %shard_map.115), channel_id=1, source_target_pairs={{0,64},{64,0},{1,65},{65,1},{2,66},{66,2},{3,67},{67,3},{4,68},{68... | collective-permute-start | bytes 2949128 | tf_op jit(solution)/shard_map/ppermute | solution.py:241
  141.2 6.0 %collective-permute-start.11 = (bf16[320,3200]{1,0:T(8,128)(2,1)S(1)}, bf16[320,3200]{1,0:T(8,128)(2,1)S(1)}, u32[]{:S(2)}, u32[]{:S(2)}) collective-permute-start(bf16[320,3200]{1,0:T(8,128)(2,1)S(1)} %bitcast.21), channel_id=1, source_target_pairs={{0,64},{64,0},{1,65},{65,1},{2,66},{66,2},{3,67},{67,3},{4,68},{68... | collective-permute-start | bytes 6144008 | tf_op jit(solution)/shard_map/ppermute | solution.py:241
  148.6 12.9 %collective-permute-start.13 = (bf16[320,512]{1,0:T(8,128)(2,1)S(1)}, bf16[320,512]{1,0:T(8,128)(2,1)S(1)}, u32[]{:S(2)}, u32[]{:S(2)}) collective-permute-start(bf16[320,512]{1,0:T(8,128)(2,1)S(1)} %shard_map.119), channel_id=1, source_target_pairs={{1,2},{2,1},{3,0},{0,3},{5,6},{6,5},{7,4},{4,7},{9,10},{10,9},{11,... | collective-permute-start | bytes 983048 | tf_op jit(solution)/shard_map/ppermute | solution.py:249
  157.6 45.3 %collective-permute-start.12 = (bf16[448,1536]{1,0:T(8,128)(2,1)S(1)}, bf16[448,1536]{1,0:T(8,128)(2,1)S(1)}, u32[]{:S(2)}, u32[]{:S(2)}) collective-permute-start(bf16[448,1536]{1,0:T(8,128)(2,1)S(1)} %get-tuple-element.46), channel_id=1, source_target_pairs={{0,1},{1,0},{2,3},{3,2},{4,5},{5,4},{6,7},{7,6},{8,9},{9,8},{10,11... | collective-permute-start | bytes 4128776 | tf_op jit(solution)/shard_map/ppermute | solution.py:245
  162.9 19.5 %collective-permute-start.18 = (bf16[40,512]{1,0:T(8,128)(2,1)S(1)}, bf16[40,512]{1,0:T(8,128)(2,1)S(1)}, u32[]{:S(2)}, u32[]{:S(2)}) collective-permute-start(bf16[40,512]{1,0:T(8,128)(2,1)S(1)} %get-tuple-element.52), channel_id=1, source_target_pairs={{52,0},{56,4},{60,8},{0,12},{4,16},{8,20},{12,24},{16,28},{20,32},... | collective-permute-start | bytes 122888 | tf_op jit(solution)/shard_map/ppermute | solution.py:237
  172.3 13.8 %collective-permute-start.14 = (bf16[120,512]{1,0:T(8,128)(2,1)S(1)}, bf16[120,512]{1,0:T(8,128)(2,1)S(1)}, u32[]{:S(2)}, u32[]{:S(2)}) collective-permute-start(bf16[120,512]{1,0:T(8,128)(2,1)S(1)} %get-tuple-element.48), channel_id=1, source_target_pairs={{60,0},{0,4},{4,8},{8,12},{12,16},{16,20},{20,24},{24,28},{28,32},... | collective-permute-start | bytes 368648 | tf_op jit(solution)/shard_map/ppermute | solution.py:237
  174.2 12.3 %collective-permute-start.15 = (bf16[120,512]{1,0:T(8,128)(2,1)S(1)}, bf16[120,512]{1,0:T(8,128)(2,1)S(1)}, u32[]{:S(2)}, u32[]{:S(2)}) collective-permute-start(bf16[120,512]{1,0:T(8,128)(2,1)S(1)} %get-tuple-element.49), channel_id=1, source_target_pairs={{56,0},{60,4},{0,8},{4,12},{8,16},{12,20},{16,24},{20,28},{24,32},... | collective-permute-start | bytes 368648 | tf_op jit(solution)/shard_map/ppermute | solution.py:237
  177.3 9.2 %collective-permute-start.16 = (bf16[120,512]{1,0:T(8,128)(2,1)S(1)}, bf16[120,512]{1,0:T(8,128)(2,1)S(1)}, u32[]{:S(2)}, u32[]{:S(2)}) collective-permute-start(bf16[120,512]{1,0:T(8,128)(2,1)S(1)} %get-tuple-element.50), channel_id=1, source_target_pairs={{4,0},{8,4},{12,8},{16,12},{20,16},{24,20},{28,24},{32,28},{36,32}... | collective-permute-start | bytes 368648 | tf_op jit(solution)/shard_map/ppermute | solution.py:237
  182.4 7.9 %collective-permute-start.17 = (bf16[120,512]{1,0:T(8,128)(2,1)S(1)}, bf16[120,512]{1,0:T(8,128)(2,1)S(1)}, u32[]{:S(2)}, u32[]{:S(2)}) collective-permute-start(bf16[120,512]{1,0:T(8,128)(2,1)S(1)} %get-tuple-element.51), channel_id=1, source_target_pairs={{8,0},{12,4},{16,8},{20,12},{24,16},{28,20},{32,24},{36,28},{40,32... | collective-permute-start | bytes 368648 | tf_op jit(solution)/shard_map/ppermute | solution.py:237
  191.0 13.7 %collective-permute-start.19 = (bf16[40,512]{1,0:T(8,128)(2,1)S(1)}, bf16[40,512]{1,0:T(8,128)(2,1)S(1)}, u32[]{:S(2)}, u32[]{:S(2)}) collective-permute-start(bf16[40,512]{1,0:T(8,128)(2,1)S(1)} %get-tuple-element.55), channel_id=1, source_target_pairs={{44,0},{48,4},{52,8},{56,12},{60,16},{0,20},{4,24},{8,28},{12,32},... | collective-permute-start | bytes 122888 | tf_op jit(solution)/shard_map/ppermute | solution.py:237
  193.1 12.0 %collective-permute-start.20 = (bf16[40,512]{1,0:T(8,128)(2,1)S(1)}, bf16[40,512]{1,0:T(8,128)(2,1)S(1)}, u32[]{:S(2)}, u32[]{:S(2)}) collective-permute-start(bf16[40,512]{1,0:T(8,128)(2,1)S(1)} %get-tuple-element.56), channel_id=1, source_target_pairs={{20,0},{24,4},{28,8},{32,12},{36,16},{40,20},{44,24},{48,28},{52,3... | collective-permute-start | bytes 122888 | tf_op jit(solution)/shard_map/ppermute | solution.py:237
  202.9 2.2 %copy-start.4 = (s32[40,8]{0,1:T(8,128)S(1)}, s32[40,8]{0,1:T(8,128)}, u32[]{:S(2)}) copy-start(s32[40,8]{0,1:T(8,128)} %param.9) | copy-start | bytes 3844
  (2 other events, 2.0 us)
